TPU v7x, 32 devices: a whole 2x2x4 slice. The times are simulated.
32 devices in a mesh: blk: 16 (over z, y, x), pipe: 2 (over core).
Axes of the slice: x: 2, y: 2, z: 4, core: 2. Of those that a mesh axis runs over, the one named last changes fastest.
Arguments:
- x_saved: bfloat16 [2, 2, 2048, 4096], P('pipe', None, 'blk'), may hold values from -6 to 6
- cotangent: bfloat16 [2, 2048, 4096], P(None, 'blk'), may hold values from -6 to 6
- seq_right: bfloat16 [2, 16, 128, 128], P('pipe', 'blk'), may hold values from -0.5 to 0.5
- seq_left: bfloat16 [2, 128, 16, 16], P('pipe', 'blk'), may hold values from -1.5 to 1.5
- chan_first: bfloat16 [2, 64, 64, 64], P('pipe'), may hold values from -0.75 to 0.75
- chan_second: bfloat16 [2, 64, 64, 64], P('pipe'), may hold values from -0.75 to 0.75
Outputs:
- grad_input: bfloat16 [2, 2, 2048, 4096], P('pipe', None, 'blk')
- grad_right: float32 [2, 16, 128, 128], P('pipe', 'blk')
- grad_left: float32 [2, 128, 16, 16], P('pipe', 'blk')
- grad_first: float32 [2, 64, 64, 64], P('pipe')
- grad_second: float32 [2, 64, 64, 64], P('pipe')
All inputs are finite; a program needn't handle non-finite values.
Results may differ from a plain program's by a relative error of at most 0.01.
Values may be sent and summed in bfloat16 or wider, within the bound.
No kernel may reach another device: no remote copies, remote signals or barrier semaphores. Data moves between devices by JAX's collectives and lax.ppermute only.
A program may use at most 128 MiB of HBM per device.

v0:
```python
import functools

import jax
import jax.numpy as jnp
from jax import lax
from jax.experimental import pallas as pl
from jax.experimental.pallas import tpu as pltpu
from jax.sharding import PartitionSpec as P

BF = jnp.bfloat16
F32 = jnp.float32
NN = (((1,), (0,)), ((), ()))
NT = (((1,), (1,)), ((), ()))


def mm(a, b, dims=NN):
    return lax.dot_general(a, b, dims, preferred_element_type=F32)


def whole(shape):
    return pl.BlockSpec(shape, lambda *_: (0,) * len(shape))


def call(kernel, name, out_shape, grid=None, in_specs=None, out_specs=None, scratch=(), prefetch=0, cost=None):
    params = pltpu.CompilerParams(vmem_limit_bytes=56 * 1024 * 1024)
    flops, moved = cost or (1 << 28, 8 << 20)
    estimate = pl.CostEstimate(flops=flops, bytes_accessed=moved, transcendentals=0)
    if grid is None:
        return pl.pallas_call(
            kernel, out_shape=out_shape, scratch_shapes=scratch, compiler_params=params, cost_estimate=estimate, name=name
        )
    spec = pltpu.PrefetchScalarGridSpec(
        num_scalar_prefetch=prefetch, grid=grid, in_specs=in_specs, out_specs=out_specs, scratch_shapes=scratch
    )
    return pl.pallas_call(
        kernel, out_shape=out_shape, grid_spec=spec, compiler_params=params, cost_estimate=estimate, name=name
    )


def sds(shape, dtype):
    return jax.ShapeDtypeStruct(shape, dtype)


def columns(q):
    return slice(128 * q, 128 * (q + 1))


def regroup(wide, q, blocks):
    parts = [wide[pl.ds(2 * q + h, blocks, stride=blocks), :] for h in range(2)]
    return jnp.concatenate(parts, axis=0).astype(BF)


def diagonal(product, side):
    lane = lax.broadcasted_iota(jnp.int32, (side, 2 * side), 1)
    return jnp.where(lane < side, product[:side], product[side:])


def expand_kernel(first, second, first_bd, first_bt, second_bd, second_bt):
    side = first.shape[1]
    zero = jnp.zeros((side, side), F32)
    for source, straight, turned in ((first, first_bd, first_bt), (second, second_bd, second_bt)):
        for q in range(source.shape[0] // 2):
            lower, upper = source[2 * q].astype(F32), source[2 * q + 1].astype(F32)
            block = jnp.concatenate(
                [jnp.concatenate([lower, zero], axis=1), jnp.concatenate([zero, upper], axis=1)], axis=0
            )
            straight[q] = block.astype(BF)
            turned[q] = block.T.astype(BF)


def gate_kernel(p, keep, recv, upstream, left_t, back):
    act = jnp.where(p[0] == 0, recv[...].astype(F32), keep[0].astype(F32))
    gate = (upstream[0].astype(F32) * act).astype(BF)
    back[...] = mm(left_t[...], gate).astype(BF)


def forward_kernel(act, right, first_bd, second_bd, eye, rows, mixed, right_act, wide):
    blocks = 64
    pairs = first_bd.shape[0]
    right_act[...] = mm(right[...], act[...]).astype(BF)
    for q in range(pairs):
        wide[columns(q), :] = mm(first_bd[q], right_act[:, columns(q)], NT)
    for q in range(pairs):
        pair = regroup(wide, q, blocks)
        mixed[columns(q), :] = pair
        hidden = mm(second_bd[q], pair).astype(BF)
        rows[:, columns(q)] = mm(eye[...], hidden, NT).astype(BF)


def right_kernel(act, right, out):
    out[...] = mm(right[...], act[...]).astype(BF)


def middle_kernel(
    back, second_bt, first_bt, mixed, right_act, right_t, act, chan_back, right_grad, grads, wide, turned
):
    blocks = 64
    pairs = first_bt.shape[0]
    for q in range(pairs):
        wide[columns(q), :] = mm(second_bt[q], back[:, columns(q)], NT)
        grads[1, 64 * q : 64 * (q + 1), :] = diagonal(mm(mixed[columns(q), :], back[:, columns(q)]), 64)
    for q in range(pairs):
        pair = regroup(wide, q, blocks)
        grads[0, 64 * q : 64 * (q + 1), :] = diagonal(mm(pair, right_act[:, columns(q)]), 64)
        piece = mm(first_bt[q], pair).astype(BF)
        turned[columns(q), :] = piece
        chan_back[:, columns(q)] = mm(right_t[...], piece, NT)
    right_grad[...] = mm(act[...], turned[...]).T


def turn_kernel(
    p,
    rows,
    upstream,
    act,
    chan_back,
    act_low,
    left,
    left_t_low,
    second_bt,
    first_bt,
    eye,
    input_grad,
    left_grad,
    gate_low,
    back_low,
    mixed_grad,
    sent,
    wide,
):
    step = pl.program_id(0)
    steps = pl.num_programs(0)
    pairs = second_bt.shape[0]
    gy = upstream[0].astype(F32)
    carried = mm(left[...], rows[...])
    incoming = (gy * carried + chan_back[...]).astype(BF)
    input_grad[...] = incoming
    gate = (gy * act[...].astype(F32)).astype(BF)
    term = mm(gate, rows[...], NT)

    @pl.when(step == 0)
    def _():
        left_grad[...] = term

    @pl.when(step > 0)
    def _():
        left_grad[...] += term

    gate = (incoming.astype(F32) * act_low[...].astype(F32)).astype(BF)
    gate_low[...] = gate
    back = mm(left_t_low[...], gate).astype(BF)
    back_low[...] = back
    for q in range(pairs):
        at = pl.multiple_of((step * pairs + q) * 128, 128)
        wide[pl.ds(at, 128), :] = mm(second_bt[q], back[:, columns(q)], NT)

    @pl.when(step == steps - 1)
    def _():
        for q in range(first_bt.shape[0]):
            pair = regroup(wide, q, 64)
            mixed_grad[columns(q), :] = pair
            piece = mm(first_bt[q], pair).astype(BF)
            sent[:, columns(q)] = mm(eye[...], piece, NT).astype(BF)


def lower_kernel(
    rows, first_bd, second_bd, left, gate, back, mixed_grad, carried, left_grad, grads, wide, turned
):
    pairs = first_bd.shape[0]
    for q in range(pairs):
        wide[columns(q), :] = mm(first_bd[q], rows[:, columns(q)], NT)
        grads[0, 64 * q : 64 * (q + 1), :] = diagonal(mm(mixed_grad[columns(q), :], rows[:, columns(q)]), 64)
    for q in range(pairs):
        pair = regroup(wide, q, 64)
        grads[1, 64 * q : 64 * (q + 1), :] = diagonal(mm(pair, back[:, columns(q)]), 64)
        hidden = mm(second_bd[q], pair).astype(BF)
        turned[columns(q), :] = hidden
        carried[:, columns(q)] = mm(left[...], hidden, NT)
    left_grad[...] = mm(gate[...], turned[...])


def last_kernel(received, right_t, upstream, carried, act, input_grad, right_grad):
    step = pl.program_id(0)
    chan_back = mm(right_t[...], received[...])
    input_grad[...] = (upstream[...].astype(F32) * carried[...] + chan_back).astype(BF)
    term = mm(received[...], act[...], NT)

    @pl.when(step == 0)
    def _():
        right_grad[...] = term

    @pl.when(step > 0)
    def _():
        right_grad[...] += term


def swap(value):
    return lax.ppermute(value, "pipe", [(0, 1), (1, 0)])


def exchange(rows, devices):
    chunks = rows.reshape(devices, rows.shape[0] // devices, *rows.shape[1:])
    return lax.all_to_all(chunks, "blk", split_axis=0, concat_axis=0, tiled=True).reshape(rows.shape)


def reduced(grads, core, devices):
    kept = lax.dynamic_index_in_dim(grads, core, 0, keepdims=False)
    sent = lax.dynamic_index_in_dim(grads, 1 - core, 0, keepdims=False)
    part = (kept + swap(sent)).astype(BF)
    rows = part.shape[0]
    pieces = exchange(part, devices).reshape(devices, rows // devices, 128)
    total = jnp.sum(pieces.astype(F32), axis=0).astype(BF)
    spread = jnp.broadcast_to(total[None], (devices,) + total.shape).reshape(rows, 128)
    return exchange(spread, devices)


def body(x_saved, cotangent, seq_right, seq_left, chan_first, chan_second):
    devices = lax.axis_size("blk")
    core = lax.axis_index("pipe")
    p = core.astype(jnp.int32).reshape(1)
    saved = x_saved[0]
    micro, tokens, width = saved.shape
    span = seq_right.shape[2]
    per, count = seq_left.shape[1], seq_left.shape[2]
    blocks, side = chan_first.shape[1], chan_first.shape[2]
    pairs = blocks // 2

    def by_section(own, other):
        return jnp.where(core == 0, own, other), jnp.where(core == 0, other, own)

    received = swap(lax.dynamic_index_in_dim(saved, 1 - core, 0, keepdims=False))
    left_0, left_1 = by_section(seq_left[0], swap(seq_left[0]))
    right_0, right_1 = by_section(seq_right[0, 0], swap(seq_right[0, 0]))
    first_0, first_1 = by_section(chan_first[0], swap(chan_first[0]))
    second_0, second_1 = by_section(chan_second[0], swap(chan_second[0]))
    own_act = lax.dynamic_index_in_dim(saved, core, 0, keepdims=False)
    act_0, act_1 = by_section(own_act, received)
    eye = jnp.eye(tokens, dtype=BF)

    def spread_left(block):
        apart = jnp.eye(per, dtype=BF)[:, None, None, :]
        full = (block[:, :, :, None] * apart).reshape(per * count, count * per)
        return full, full.T

    full_0, turned_0 = spread_left(left_0)
    full_1, turned_1 = spread_left(left_1)

    step = width // 8
    square = whole((tokens, tokens))
    moving = pl.BlockSpec((tokens, step), lambda i, *_: (0, i))
    chosen = pl.BlockSpec((1, tokens, step), lambda i, p: (p[0], 0, i))
    act_shape = (tokens, width)
    col_shape = (width, tokens)

    back_1 = call(
        gate_kernel,
        "gate",
        sds(act_shape, BF),
        grid=(width // step,),
        prefetch=1,
        in_specs=[chosen, moving, chosen, square],
        out_specs=moving,
    )(p, saved, received, cotangent, turned_1)
    returned_1 = exchange(back_1, devices)

    expanded = [sds((pairs, 2 * side, 2 * side), BF)] * 4
    expand = call(expand_kernel, "expand", expanded)
    fbd_1, fbt_1, sbd_1, sbt_1 = expand(first_1, second_1)
    fbd_0, fbt_0, sbd_0, sbt_0 = expand(first_0, second_0)

    rows_1, mixed_1, right_act_1 = call(
        forward_kernel,
        "forward",
        [sds(act_shape, BF), sds(col_shape, BF), sds(act_shape, BF)],
        scratch=[pltpu.VMEM(col_shape, F32)],
    )(act_1, right_1, fbd_1, sbd_1, eye)
    gathered_1 = exchange(rows_1, devices)

    right_act_0 = call(right_kernel, "right", sds(act_shape, BF))(act_0, right_0)
    gathered_0 = exchange(right_act_0, devices)

    chan_back_1, right_grad_1, grads_1 = call(
        middle_kernel,
        "middle",
        [sds(act_shape, F32), sds((span, span), F32), sds((2, pairs * side, 2 * side), F32)],
        scratch=[pltpu.VMEM(col_shape, F32), pltpu.VMEM(col_shape, BF)],
    )(returned_1, sbt_1, fbt_1, mixed_1, right_act_1, right_1.T, act_1)

    input_1, left_full_1, gate_0, back_0, mixed_grad_0, sent_0 = call(
        turn_kernel,
        "turn",
        [
            sds(act_shape, BF),
            sds((tokens, tokens), F32),
            sds(act_shape, BF),
            sds(act_shape, BF),
            sds(col_shape, BF),
            sds(act_shape, BF),
        ],
        grid=(width // step,),
        prefetch=1,
        in_specs=[
            moving,
            chosen,
            moving,
            moving,
            moving,
            square,
            square,
            pl.BlockSpec((step // (2 * side), 2 * side, 2 * side), lambda i, *_: (i, 0, 0)),
            whole((pairs, 2 * side, 2 * side)),
            square,
        ],
        out_specs=[moving, square, moving, moving, whole(col_shape), whole(act_shape)],
        scratch=[pltpu.VMEM(col_shape, F32)],
    )(p, gathered_1, cotangent, act_1, chan_back_1, act_0, full_1, turned_0, sbt_0, fbt_0, eye)
    returned_0 = exchange(sent_0, devices)

    carried_0, left_full_0, grads_0 = call(
        lower_kernel,
        "lower",
        [sds(act_shape, F32), sds((tokens, tokens), F32), sds((2, pairs * side, 2 * side), F32)],
        scratch=[pltpu.VMEM(col_shape, F32), pltpu.VMEM(col_shape, BF)],
    )(gathered_0, fbd_0, sbd_0, full_0, gate_0, back_0, mixed_grad_0)

    input_0, right_grad_0 = call(
        last_kernel,
        "last",
        [sds(act_shape, BF), sds((span, span), F32)],
        grid=(width // step,),
        in_specs=[moving, square, moving, moving, moving],
        out_specs=[moving, square],
    )(returned_0, right_0.T, input_1, carried_0, act_0)

    sums_1 = reduced(grads_1, core, devices)
    sums_0 = reduced(grads_0, core, devices)

    def left_blocks(full):
        apart = jnp.eye(per, dtype=F32)[:, None, None, :]
        return jnp.sum(full.reshape(per, count, count, per) * apart, axis=3)

    def to_sections(low, high):
        kept = jnp.where(core == 0, low, high)
        came = swap(jnp.where(core == 0, high, low))
        return jnp.where(core == 0, kept, came), jnp.where(core == 0, came, kept)

    input_grad = jnp.stack(to_sections(input_0, input_1))
    left_grad = sum(to_sections(left_blocks(left_full_0), left_blocks(left_full_1)))
    right_grad = sum(to_sections(right_grad_0, right_grad_1))
    first_sum, second_sum = to_sections(sums_0, sums_1)
    first_grad = first_sum.astype(F32).reshape(pairs, side, 2, side).transpose(0, 2, 1, 3).reshape(blocks, side, side)
    second_grad = second_sum.astype(F32).reshape(pairs, side, 2, side).transpose(0, 2, 3, 1).reshape(blocks, side, side)
    return (
        input_grad[None],
        right_grad[None, None],
        left_grad[None],
        first_grad[None],
        second_grad[None],
    )


def solution(mesh):
    in_specs = (
        P("pipe", None, "blk", None),
        P(None, "blk", None),
        P("pipe", "blk", None, None),
        P("pipe", "blk", None, None),
        P("pipe", None, None, None),
        P("pipe", None, None, None),
    )
    out_specs = (
        P("pipe", None, "blk", None),
        P("pipe", "blk", None, None),
        P("pipe", "blk", None, None),
        P("pipe", None, None, None),
        P("pipe", None, None, None),
    )
    return jax.shard_map(body, mesh=mesh, in_specs=in_specs, out_specs=out_specs, check_vma=False)
```

profile of v0, /device:TPU:0, one launch (start us, length us, event | category | flops | bytes accessed | tf_op | source)
XLA Modules:
  0.0 228.8 jit_solution(17062840237723022160)
XLA Ops:
  0.7 1.4 dynamic-slice_bitcast_fusion.2
  2.0 0.5 collective-permute-start
  2.7 0.4 collective-permute-start.2
  3.5 0.5 collective-permute-start.4
  3.9 1.8 collective-permute-done.4
  5.8 0.8 broadcast_multiply_fusion
  6.6 1.8 mul.53
  8.4 1.0 copy-done.2
  9.3 6.5 %gate.1 = bf16[128,4096]{1,0:T(8,128)(2,1)} custom-call(s32[1]{0:T(128)} %bitcast.p, bf16[2,128,4096]{2,1,0:T(8,128)(2,1)} %bitcast.83, bf16[128,4096]{1,0:T(8,128)(2,1)} %copy-done.2, bf16[2,128,4096]{2,1,0:T(8,128)(2,1)} %upstream.3, bf16[128,128]{1,0:T(8,128)(2,1)} %bitcast.100), custom_call_target="tpu_custom_call" | custom-call | flops 268435456 | bytes 8388608 | tf_op jit(solution)/shard_map/gate/pallas_call | solution.py:255
  15.8 8.2 %all-to-all-start.1 = ((bf16[16,8,4096]{2,1,0:T(8,128)(2,1)}), bf16[16,8,4096]{2,1,0:T(8,128)(2,1)S(1)}, u32[]{:S(2)}, u32[]{:S(2)}) async-start(bf16[16,8,4096]{2,1,0:T(8,128)(2,1)} %bitcast.88), calls=%async_computation.1 | async-start | bytes 2097152 | tf_op jit(solution)/shard_map/all_to_all | solution.py:203
  24.1 0.6 fusion.4.eye
  24.7 0.7 copy.70.right
  25.5 2.7 %broadcast_select_fusion = (bf16[64,64,64]{2,1,0:T(8,128)(2,1)}, bf16[64,64,64]{2,1,0:T(8,128)(2,1)}) fusion(bf16[64,64,64]{2,1,0:T(8,128)(2,1)} %collective-permute-done.3, pred[]{:T(512)S(6)} %eq.21, bf16[1,64,64,64]{3,2,1,0:T(8,128)(2,1)S(1)} %copy-done.11), kind=kLoop, calls=%fused_computation.12 | loop fusion | flops 524288 | bytes 2097153 | tf_op jit(solution)/shard_map/jit(_where)/select_n | solution.py:229
  28.2 3.1 %broadcast_select_fusion.1 = (bf16[64,64,64]{2,1,0:T(8,128)(2,1)}, bf16[64,64,64]{2,1,0:T(8,128)(2,1)}) fusion(bf16[64,64,64]{2,1,0:T(8,128)(2,1)} %collective-permute-done.2, pred[]{:T(512)S(6)} %eq.21, bf16[1,64,64,64]{3,2,1,0:T(8,128)(2,1)} %param.10), kind=kLoop, calls=%fused_computation.13 | loop fusion | flops 524288 | bytes 2097153 | tf_op jit(solution)/shard_map/jit(_where)/select_n | solution.py:229
  31.2 4.5 %expand.2 = (bf16[32,128,128]{2,1,0:T(8,128)(2,1)}, bf16[32,128,128]{2,1,0:T(8,128)(2,1)}, bf16[32,128,128]{2,1,0:T(8,128)(2,1)}, bf16[32,128,128]{2,1,0:T(8,128)(2,1)}) custom-call(bf16[64,64,64]{2,1,0:T(8,128)(2,1)} %get-tuple-element.89.first, bf16[64,64,64]{2,1,0:T(8,128)(2,1)} %get-tuple-element.87.second), custom_call_target="tpu_custom_call" | custom-call | flops 268435456 | bytes 8388608 | tf_op jit(solution)/shard_map/expand/pallas_call | solution.py:268
  35.8 1.5 bitcast_select_fusion
  37.2 7.1 %forward.1 = (bf16[128,4096]{1,0:T(8,128)(2,1)}, bf16[4096,128]{1,0:T(8,128)(2,1)}, bf16[128,4096]{1,0:T(8,128)(2,1)}) custom-call(bf16[128,4096]{1,0:T(8,128)(2,1)} %get-tuple-element.85.act, bf16[128,128]{1,0:T(8,128)(2,1)} %copy.70.right, bf16[32,128,128]{2,1,0:T(8,128)(2,1)} %get-tuple-element.30.first_bd, ...), custom_call_target="tpu_custom_call" | custom-call | flops 268435456 | bytes 8388608 | tf_op jit(solution)/shard_map/forward/pallas_call | solution.py:271
  44.3 4.3 %all-to-all-done.1 = bf16[16,8,4096]{2,1,0:T(8,128)(2,1)S(1)} async-done(((bf16[16,8,4096]{2,1,0:T(8,128)(2,1)}), bf16[16,8,4096]{2,1,0:T(8,128)(2,1)S(1)}, u32[]{:S(2)}, u32[]{:S(2)}) %all-to-all-start.1) | async-done | bytes 1048608 | tf_op jit(solution)/shard_map/all_to_all | solution.py:203
  48.7 6.1 %all-to-all-start = ((bf16[16,8,4096]{2,1,0:T(8,128)(2,1)}), bf16[16,8,4096]{2,1,0:T(8,128)(2,1)S(1)}, u32[]{:S(2)}, u32[]{:S(2)}) async-start(bf16[16,8,4096]{2,1,0:T(8,128)(2,1)} %bitcast.98), calls=%async_computation | async-start | bytes 2097152 | tf_op jit(solution)/shard_map/all_to_all | solution.py:203
  54.8 0.7 copy.73.right
  55.5 2.6 %right.1 = bf16[128,4096]{1,0:T(8,128)(2,1)} custom-call(bf16[128,4096]{1,0:T(8,128)(2,1)} %get-tuple-element.84.act_low.act, bf16[128,128]{1,0:T(8,128)(2,1)} %copy.73.right), custom_call_target="tpu_custom_call" | custom-call | flops 268435456 | bytes 8388608 | tf_op jit(solution)/shard_map/right/pallas_call | solution.py:279
  58.1 20.0 %all-to-all-done = bf16[16,8,4096]{2,1,0:T(8,128)(2,1)S(1)} async-done(((bf16[16,8,4096]{2,1,0:T(8,128)(2,1)}), bf16[16,8,4096]{2,1,0:T(8,128)(2,1)S(1)}, u32[]{:S(2)}, u32[]{:S(2)}) %all-to-all-start) | async-done | bytes 1048608 | tf_op jit(solution)/shard_map/all_to_all | solution.py:203
  78.1 5.9 %all-to-all-start.3 = ((bf16[16,8,4096]{2,1,0:T(8,128)(2,1)}), bf16[16,8,4096]{2,1,0:T(8,128)(2,1)S(1)}, u32[]{:S(2)}, u32[]{:S(2)}) async-start(bf16[16,8,4096]{2,1,0:T(8,128)(2,1)} %bitcast.89), calls=%async_computation.3 | async-start | bytes 2097152 | tf_op jit(solution)/shard_map/all_to_all | solution.py:203
  84.0 0.7 copy.72.left
  84.7 0.8 mul.56
  85.5 4.4 %expand.3 = (bf16[32,128,128]{2,1,0:T(8,128)(2,1)}, bf16[32,128,128]{2,1,0:T(8,128)(2,1)}, bf16[32,128,128]{2,1,0:T(8,128)(2,1)}, bf16[32,128,128]{2,1,0:T(8,128)(2,1)}) custom-call(bf16[64,64,64]{2,1,0:T(8,128)(2,1)} %get-tuple-element.88.first, bf16[64,64,64]{2,1,0:T(8,128)(2,1)} %get-tuple-element.86.second), custom_call_target="tpu_custom_call" | custom-call | flops 268435456 | bytes 8388608 | tf_op jit(solution)/shard_map/expand/pallas_call | solution.py:269
  89.8 7.9 %middle.1 = (f32[128,4096]{1,0:T(8,128)}, f32[128,128]{1,0:T(8,128)}, f32[2,2048,128]{2,1,0:T(8,128)}) custom-call(bf16[128,4096]{1,0:T(8,128)(2,1)} %bitcast.90, bf16[32,128,128]{2,1,0:T(8,128)(2,1)} %get-tuple-element.33.second_bt, bf16[32,128,128]{2,1,0:T(8,128)(2,1)} %get-tuple-element.34.first_bt, bf16[4096,128]{1,0:T(8,128)(2,1)} %get-tuple-element.35.mixed, ...), custom_call_target="tpu_custom_call" | custom-call | flops 268435456 | bytes 8388608 | tf_op jit(solution)/shard_map/middle/pallas_call | solution.py:282
  97.8 13.5 %turn.1 = (bf16[128,4096]{1,0:T(8,128)(2,1)}, f32[128,128]{1,0:T(8,128)}, bf16[128,4096]{1,0:T(8,128)(2,1)}, bf16[128,4096]{1,0:T(8,128)(2,1)}, bf16[4096,128]{1,0:T(8,128)(2,1)}, /*index=5*/bf16[128,4096]{1,0:T(8,128)(2,1)}) custom-call(s32[1]{0:T(128)} %bitcast.p, bf16[128,4096]{1,0:T(8,128)(2,1)} %bitcast.87, bf16[2,128,4096]{2,1,0:T(8,128)(2,1)} %upstream.3, ...), custom_call_target="tpu_custom_call" | custom-call | flops 268435456 | bytes 8388608 | tf_op jit(solution)/shard_map/turn/pallas_call | solution.py:289
  111.3 6.9 %all-to-all-start.2 = ((bf16[16,8,4096]{2,1,0:T(8,128)(2,1)}), bf16[16,8,4096]{2,1,0:T(8,128)(2,1)S(1)}, u32[]{:S(2)}, u32[]{:S(2)}) async-start(bf16[16,8,4096]{2,1,0:T(8,128)(2,1)} %bitcast.97), calls=%async_computation.2 | async-start | bytes 2097152 | tf_op jit(solution)/shard_map/all_to_all | solution.py:203
  118.2 0.7 copy.74.left
  118.9 7.9 %lower.1 = (f32[128,4096]{1,0:T(8,128)}, f32[128,128]{1,0:T(8,128)}, f32[2,2048,128]{2,1,0:T(8,128)}) custom-call(bf16[128,4096]{1,0:T(8,128)(2,1)} %bitcast.91, bf16[32,128,128]{2,1,0:T(8,128)(2,1)} %get-tuple-element.42.first_bd, bf16[32,128,128]{2,1,0:T(8,128)(2,1)} %get-tuple-element.43.second_bd, bf16[128,128]{1,0:T(8,128)(2,1)} %copy.74.left, ...), custom_call_target="tpu_custom_call" | custom-call | flops 268435456 | bytes 8388608 | tf_op jit(solution)/shard_map/lower/pallas_call | solution.py:319
  126.9 1.4 dynamic-slice_bitcast_fusion.1
  128.4 0.4 copy-done.9
  128.8 1.0 dynamic-slice_bitcast_fusion
  129.9 1.1 collective-permute-done.8
  131.0 0.9 fusion.1
  131.9 8.8 %all-to-all-done.2 = bf16[16,8,4096]{2,1,0:T(8,128)(2,1)S(1)} async-done(((bf16[16,8,4096]{2,1,0:T(8,128)(2,1)}), bf16[16,8,4096]{2,1,0:T(8,128)(2,1)S(1)}, u32[]{:S(2)}, u32[]{:S(2)}) %all-to-all-start.2) | async-done | bytes 1048608 | tf_op jit(solution)/shard_map/all_to_all | solution.py:203
  140.8 5.8 %all-to-all-start.4 = ((bf16[16,128,128]{2,1,0:T(8,128)(2,1)}), bf16[16,128,128]{2,1,0:T(8,128)(2,1)}, u32[]{:S(2)}, u32[]{:S(2)}) async-start(bf16[16,128,128]{2,1,0:T(8,128)(2,1)} %bitcast.94), calls=%async_computation.4 | async-start | bytes 1048576 | tf_op jit(solution)/shard_map/all_to_all | solution.py:203
  146.6 2.1 fusion
  148.8 11.6 %all-to-all-done.4 = bf16[16,128,128]{2,1,0:T(8,128)(2,1)} async-done(((bf16[16,128,128]{2,1,0:T(8,128)(2,1)}), bf16[16,128,128]{2,1,0:T(8,128)(2,1)}, u32[]{:S(2)}, u32[]{:S(2)}) %all-to-all-start.4) | async-done | bytes 524320 | tf_op jit(solution)/shard_map/all_to_all | solution.py:203
  160.4 3.8 %all-to-all-start.6 = ((bf16[16,128,128]{2,1,0:T(8,128)(2,1)}), bf16[16,128,128]{2,1,0:T(8,128)(2,1)S(1)}, u32[]{:S(2)}, u32[]{:S(2)}) async-start(bf16[16,128,128]{2,1,0:T(8,128)(2,1)} %bitcast.95), calls=%async_computation.6 | async-start | bytes 1048576 | tf_op jit(solution)/shard_map/all_to_all | solution.py:203
  164.2 1.1 reduce_sum.44
  165.4 12.5 %all-to-all-done.6 = bf16[16,128,128]{2,1,0:T(8,128)(2,1)S(1)} async-done(((bf16[16,128,128]{2,1,0:T(8,128)(2,1)}), bf16[16,128,128]{2,1,0:T(8,128)(2,1)S(1)}, u32[]{:S(2)}, u32[]{:S(2)}) %all-to-all-start.6) | async-done | bytes 524320 | tf_op jit(solution)/shard_map/all_to_all | solution.py:203
  177.9 0.9 broadcast_in_dim.13
  178.8 3.9 %all-to-all-start.5 = ((bf16[16,128,128]{1,2,0:T(8,128)(2,1)}), bf16[16,128,128]{1,2,0:T(8,128)(2,1)S(1)}, u32[]{:S(2)}, u32[]{:S(2)}) async-start(bf16[16,128,128]{1,2,0:T(8,128)(2,1)} %broadcast_in_dim.13), calls=%async_computation.5 | async-start | bytes 1048576 | tf_op jit(solution)/shard_map/all_to_all | solution.py:203
  183.5 6.8 %last.1 = (bf16[128,4096]{1,0:T(8,128)(2,1)}, f32[128,128]{1,0:T(8,128)}) custom-call(bf16[128,4096]{1,0:T(8,128)(2,1)} %bitcast.86, bf16[128,128]{1,0:T(8,128)(2,1)} %bitcast.102, bf16[128,4096]{1,0:T(8,128)(2,1)} %get-tuple-element.41.upstream, f32[128,4096]{1,0:T(8,128)} %get-tuple-element.47.carried, bf16[128,4096]{1,0:T(8,128)(2,1)} %get-tuple-element.84.act_low.act), custom_call_target="tpu_custom_call" | custom-call | flops 268435456 | bytes 8388608 | tf_op jit(solution)/shard_map/last/pallas_call | solution.py:326
  190.6 5.8 %all-to-all-done.5 = bf16[16,128,128]{1,2,0:T(8,128)(2,1)S(1)} async-done(((bf16[16,128,128]{1,2,0:T(8,128)(2,1)}), bf16[16,128,128]{1,2,0:T(8,128)(2,1)S(1)}, u32[]{:S(2)}, u32[]{:S(2)}) %all-to-all-start.5) | async-done | bytes 524320 | tf_op jit(solution)/shard_map/all_to_all | solution.py:203
  196.4 0.9 broadcast_in_dim.14
  197.3 4.4 %all-to-all-start.7 = ((bf16[16,128,128]{1,2,0:T(8,128)(2,1)}), bf16[16,128,128]{1,2,0:T(8,128)(2,1)}, u32[]{:S(2)}, u32[]{:S(2)}) async-start(bf16[16,128,128]{1,2,0:T(8,128)(2,1)} %broadcast_in_dim.14), calls=%async_computation.7 | async-start | bytes 1048576 | tf_op jit(solution)/shard_map/all_to_all | solution.py:203
  201.7 1.1 broadcast_select_fusion.4
  202.8 0.6 collective-permute-start.7
  203.7 1.5 collective-permute-done.7
  205.2 0.7 copy.92
  205.9 0.7 copy.91
  206.9 8.2 %all-to-all-done.7 = bf16[16,128,128]{1,2,0:T(8,128)(2,1)} async-done(((bf16[16,128,128]{1,2,0:T(8,128)(2,1)}), bf16[16,128,128]{1,2,0:T(8,128)(2,1)}, u32[]{:S(2)}, u32[]{:S(2)}) %all-to-all-start.7) | async-done | bytes 524320 | tf_op jit(solution)/shard_map/all_to_all | solution.py:203
  215.1 1.3 copy.84
  216.6 1.4 select_bitcast_fusion.1
  218.0 1.5 maximum_bitcast_fusion
  219.5 1.1 fusion.3
  221.0 0.8 reshape.109
  221.8 2.1 copy.88
  223.9 1.6 copy.89
  225.4 0.8 reshape.110
  226.3 2.5 %copy.90 = f32[32,2,64,64]{3,2,1,0:T(8,128)} copy(f32[32,2,64,64]{3,0,2,1:T(8,128)S(1)} %bitcast.85) | data formatting | bytes 2097152 | tf_op jit(solution)/shard_map/broadcast_in_dim;reshape | solution.py:358
  (81 shorter events, 2.9 us)
Async XLA Ops:
  0.6 1.9 copy-start.11
  0.6 2.4 %copy-start.20 = (bf16[1,1,128,128]{3,2,1,0:T(8,128)(2,1)S(1)}, bf16[1,1,128,128]{3,2,1,0:T(8,128)(2,1)}, u32[]{:S(2)}) copy-start(bf16[1,1,128,128]{3,2,1,0:T(8,128)(2,1)} %param.8) | copy-start | bytes 98308
  0.7 2.7 %copy-start.21 = (bf16[1,8,16,16]{3,2,1,0:T(8,128)(2,1)S(1)}, bf16[1,8,16,16]{3,2,1,0:T(8,128)(2,1)}, u32[]{:S(2)}) copy-start(bf16[1,8,16,16]{3,2,1,0:T(8,128)(2,1)} %param.9) | copy-start | bytes 12292
  2.0 6.3 %collective-permute-start = (bf16[128,4096]{1,0:T(8,128)(2,1)S(1)}, bf16[128,4096]{1,0:T(8,128)(2,1)S(1)}, u32[]{:S(2)}, u32[]{:S(2)}) collective-permute-start(bf16[128,4096]{1,0:T(8,128)(2,1)S(1)} %dynamic-slice_bitcast_fusion.2), channel_id=1, source_target_pairs={{0,1},{1,0},{2,3},{3,2},{4,5},{5,4},{6,7},{7,6},{8,9},{9,8},{10,11... | collective-permute-start | bytes 3145736 | tf_op jit(solution)/shard_map/ppermute | solution.py:198
  2.6 22.9 %collective-permute-start.3 = (bf16[64,64,64]{2,1,0:T(8,128)(2,1)S(1)}, bf16[64,64,64]{2,1,0:T(8,128)(2,1)}, u32[]{:S(2)}, u32[]{:S(2)}) collective-permute-start(bf16[64,64,64]{2,1,0:T(8,128)(2,1)S(1)} %bitcast.96), channel_id=1, source_target_pairs={{0,1},{1,0},{2,3},{3,2},{4,5},{5,4},{6,7},{7,6},{8,9},{9,8},{10,11... | collective-permute-start | bytes 1572872 | tf_op jit(solution)/shard_map/ppermute | solution.py:198
  2.7 25.5 %collective-permute-start.2 = (bf16[64,64,64]{2,1,0:T(8,128)(2,1)}, bf16[64,64,64]{2,1,0:T(8,128)(2,1)}, u32[]{:S(2)}, u32[]{:S(2)}) collective-permute-start(bf16[64,64,64]{2,1,0:T(8,128)(2,1)} %bitcast.4), channel_id=1, source_target_pairs={{0,1},{1,0},{2,3},{3,2},{4,5},{5,4},{6,7},{7,6},{8,9},{9,8},{10,11... | collective-permute-start | bytes 1572872 | tf_op jit(solution)/shard_map/ppermute | solution.py:198
  3.2 21.5 %collective-permute-start.1 = (bf16[128,128]{0,1:T(8,128)(2,1)S(1)}, bf16[128,128]{0,1:T(8,128)(2,1)S(1)}, u32[]{:S(2)}, u32[]{:S(2)}) collective-permute-start(bf16[128,128]{0,1:T(8,128)(2,1)S(1)} %bitcast.104), channel_id=1, source_target_pairs={{0,1},{1,0},{2,3},{3,2},{4,5},{5,4},{6,7},{7,6},{8,9},{9,8},{10,11... | collective-permute-start | bytes 98312 | tf_op jit(solution)/shard_map/ppermute | solution.py:198
  3.5 2.3 %collective-permute-start.4 = (bf16[8,16,16]{1,0,2:T(8,128)(2,1)S(1)}, bf16[8,16,16]{1,0,2:T(8,128)(2,1)S(1)}, u32[]{:S(2)}, u32[]{:S(2)}) collective-permute-start(bf16[8,16,16]{1,0,2:T(8,128)(2,1)S(1)} %bitcast.105), channel_id=1, source_target_pairs={{0,1},{1,0},{2,3},{3,2},{4,5},{5,4},{6,7},{7,6},{8,9},{9,8},{10,11... | collective-permute-start | bytes 12296 | tf_op jit(solution)/shard_map/ppermute | solution.py:198
  8.4 1.0 copy-start.2
  15.8 32.9 %all-to-all-start.1 = ((bf16[16,8,4096]{2,1,0:T(8,128)(2,1)}), bf16[16,8,4096]{2,1,0:T(8,128)(2,1)S(1)}, u32[]{:S(2)}, u32[]{:S(2)}) async-start(bf16[16,8,4096]{2,1,0:T(8,128)(2,1)} %bitcast.88), calls=%async_computation.1 | async-start | bytes 2097152 | tf_op jit(solution)/shard_map/all_to_all | solution.py:203
  24.7 3.4 %copy-start.15 = (bf16[128,128]{0,1:T(8,128)(2,1)}, bf16[128,128]{0,1:T(8,128)(2,1)S(1)}, u32[]{:S(2)}) copy-start(bf16[128,128]{0,1:T(8,128)(2,1)S(1)} %get-tuple-element.95) | copy-start | bytes 98308
  24.7 30.1 %copy-start.14 = (bf16[128,128]{0,1:T(8,128)(2,1)}, bf16[128,128]{0,1:T(8,128)(2,1)S(1)}, u32[]{:S(2)}) copy-start(bf16[128,128]{0,1:T(8,128)(2,1)S(1)} %get-tuple-element.94) | copy-start | bytes 98308
  28.1 7.6 %copy-start.3 = (bf16[128,4096]{1,0:T(8,128)(2,1)S(1)}, bf16[128,4096]{1,0:T(8,128)(2,1)}, u32[]{:S(2)}) copy-start(bf16[128,4096]{1,0:T(8,128)(2,1)} %copy-done.2) | copy-start | bytes 3145732
  31.2 4.5 %copy-start.1 = (bf16[1,2,128,4096]{3,2,1,0:T(8,128)(2,1)S(1)}, bf16[1,2,128,4096]{3,2,1,0:T(8,128)(2,1)}, u32[]{:S(2)}) copy-start(bf16[1,2,128,4096]{3,2,1,0:T(8,128)(2,1)} %param.6) | copy-start | bytes 6291460
  48.7 9.4 %copy-start.6 = (bf16[16,8,4096]{2,1,0:T(8,128)(2,1)}, bf16[16,8,4096]{2,1,0:T(8,128)(2,1)S(1)}, u32[]{:S(2)}) copy-start(bf16[16,8,4096]{2,1,0:T(8,128)(2,1)S(1)} %all-to-all-done.1) | copy-start | bytes 3145732
  48.7 29.4 %all-to-all-start = ((bf16[16,8,4096]{2,1,0:T(8,128)(2,1)}), bf16[16,8,4096]{2,1,0:T(8,128)(2,1)S(1)}, u32[]{:S(2)}, u32[]{:S(2)}) async-start(bf16[16,8,4096]{2,1,0:T(8,128)(2,1)} %bitcast.98), calls=%async_computation | async-start | bytes 2097152 | tf_op jit(solution)/shard_map/all_to_all | solution.py:203
  55.5 28.5 %copy-start.12 = (bf16[128,128]{0,1:T(8,128)(2,1)S(1)}, bf16[128,128]{0,1:T(8,128)(2,1)}, u32[]{:S(2)}) copy-start(bf16[128,128]{0,1:T(8,128)(2,1)} %mul.53) | copy-start | bytes 98308
  78.1 11.7 %copy-start.5 = (bf16[16,8,4096]{2,1,0:T(8,128)(2,1)}, bf16[16,8,4096]{2,1,0:T(8,128)(2,1)S(1)}, u32[]{:S(2)}) copy-start(bf16[16,8,4096]{2,1,0:T(8,128)(2,1)S(1)} %all-to-all-done) | copy-start | bytes 3145732
  78.1 33.2 %all-to-all-start.3 = ((bf16[16,8,4096]{2,1,0:T(8,128)(2,1)}), bf16[16,8,4096]{2,1,0:T(8,128)(2,1)S(1)}, u32[]{:S(2)}, u32[]{:S(2)}) async-start(bf16[16,8,4096]{2,1,0:T(8,128)(2,1)} %bitcast.89), calls=%async_computation.3 | async-start | bytes 2097152 | tf_op jit(solution)/shard_map/all_to_all | solution.py:203
  111.3 6.9 %copy-start.13 = (bf16[128,128]{0,1:T(8,128)(2,1)S(1)}, bf16[128,128]{0,1:T(8,128)(2,1)}, u32[]{:S(2)}) copy-start(bf16[128,128]{0,1:T(8,128)(2,1)} %mul.56) | copy-start | bytes 98308
  111.3 7.6 %copy-start.8 = (bf16[16,8,4096]{2,1,0:T(8,128)(2,1)}, bf16[16,8,4096]{2,1,0:T(8,128)(2,1)S(1)}, u32[]{:S(2)}) copy-start(bf16[16,8,4096]{2,1,0:T(8,128)(2,1)S(1)} %all-to-all-done.3) | copy-start | bytes 3145732
  111.3 29.5 %all-to-all-start.2 = ((bf16[16,8,4096]{2,1,0:T(8,128)(2,1)}), bf16[16,8,4096]{2,1,0:T(8,128)(2,1)S(1)}, u32[]{:S(2)}, u32[]{:S(2)}) async-start(bf16[16,8,4096]{2,1,0:T(8,128)(2,1)} %bitcast.97), calls=%async_computation.2 | async-start | bytes 2097152 | tf_op jit(solution)/shard_map/all_to_all | solution.py:203
  126.9 1.9 copy-start.9
  126.9 4.2 %copy-start.10 = (f32[2,2048,128]{2,1,0:T(8,128)S(1)}, f32[2,2048,128]{2,1,0:T(8,128)}, u32[]{:S(2)}) copy-start(f32[2,2048,128]{2,1,0:T(8,128)} %get-tuple-element.53) | copy-start | bytes 6291460
  128.3 2.7 %collective-permute-start.8 = (f32[2048,128]{1,0:T(8,128)S(1)}, f32[2048,128]{1,0:T(8,128)S(1)}, u32[]{:S(2)}, u32[]{:S(2)}) collective-permute-start(f32[2048,128]{1,0:T(8,128)S(1)} %dynamic-slice_bitcast_fusion.1), channel_id=1, source_target_pairs={{0,1},{1,0},{2,3},{3,2},{4,5},{5,4},{6,7},{7,6},{8,9},{9,8},{10,11... | collective-permute-start | bytes 3145736 | tf_op jit(solution)/shard_map/ppermute | solution.py:198
  129.8 16.8 %collective-permute-start.9 = (f32[2048,128]{1,0:T(8,128)}, f32[2048,128]{1,0:T(8,128)}, u32[]{:S(2)}, u32[]{:S(2)}) collective-permute-start(f32[2048,128]{1,0:T(8,128)} %dynamic-slice_bitcast_fusion), channel_id=1, source_target_pairs={{0,1},{1,0},{2,3},{3,2},{4,5},{5,4},{6,7},{7,6},{8,9},{9,8},{10,11... | collective-permute-start | bytes 3145736 | tf_op jit(solution)/shard_map/ppermute | solution.py:198
  140.8 19.6 %copy-start.4 = (bf16[16,8,4096]{2,1,0:T(8,128)(2,1)}, bf16[16,8,4096]{2,1,0:T(8,128)(2,1)S(1)}, u32[]{:S(2)}) copy-start(bf16[16,8,4096]{2,1,0:T(8,128)(2,1)S(1)} %all-to-all-done.2) | copy-start | bytes 3145732
  140.8 19.6 %all-to-all-start.4 = ((bf16[16,128,128]{2,1,0:T(8,128)(2,1)}), bf16[16,128,128]{2,1,0:T(8,128)(2,1)}, u32[]{:S(2)}, u32[]{:S(2)}) async-start(bf16[16,128,128]{2,1,0:T(8,128)(2,1)} %bitcast.94), calls=%async_computation.4 | async-start | bytes 1048576 | tf_op jit(solution)/shard_map/all_to_all | solution.py:203
  148.8 33.9 %copy-start.18 = (f32[128,128]{1,0:T(8,128)S(1)}, f32[128,128]{1,0:T(8,128)}, u32[]{:S(2)}) copy-start(f32[128,128]{1,0:T(8,128)} %get-tuple-element.51) | copy-start | bytes 196612
  148.8 34.2 %copy-start.17 = (f32[128,128]{1,0:T(8,128)S(1)}, f32[128,128]{1,0:T(8,128)}, u32[]{:S(2)}) copy-start(f32[128,128]{1,0:T(8,128)} %get-tuple-element.52) | copy-start | bytes 196612
  160.4 17.6 %all-to-all-start.6 = ((bf16[16,128,128]{2,1,0:T(8,128)(2,1)}), bf16[16,128,128]{2,1,0:T(8,128)(2,1)S(1)}, u32[]{:S(2)}, u32[]{:S(2)}) async-start(bf16[16,128,128]{2,1,0:T(8,128)(2,1)} %bitcast.95), calls=%async_computation.6 | async-start | bytes 1048576 | tf_op jit(solution)/shard_map/all_to_all | solution.py:203
  178.8 17.6 %all-to-all-start.5 = ((bf16[16,128,128]{1,2,0:T(8,128)(2,1)}), bf16[16,128,128]{1,2,0:T(8,128)(2,1)S(1)}, u32[]{:S(2)}, u32[]{:S(2)}) async-start(bf16[16,128,128]{1,2,0:T(8,128)(2,1)} %broadcast_in_dim.13), calls=%async_computation.5 | async-start | bytes 1048576 | tf_op jit(solution)/shard_map/all_to_all | solution.py:203
  190.3 11.3 %copy-start = (bf16[128,4096]{1,0:T(8,128)(2,1)S(1)}, bf16[128,4096]{1,0:T(8,128)(2,1)}, u32[]{:S(2)}) copy-start(bf16[128,4096]{1,0:T(8,128)(2,1)} %get-tuple-element.41.upstream) | copy-start | bytes 3145732
  190.3 11.3 %copy-start.7 = (bf16[128,4096]{1,0:T(8,128)(2,1)S(1)}, bf16[128,4096]{1,0:T(8,128)(2,1)}, u32[]{:S(2)}) copy-start(bf16[128,4096]{1,0:T(8,128)(2,1)} %get-tuple-element.48) | copy-start | bytes 3145732
  197.3 6.1 %copy-start.16 = (f32[128,128]{1,0:T(8,128)S(1)}, f32[128,128]{1,0:T(8,128)}, u32[]{:S(2)}) copy-start(f32[128,128]{1,0:T(8,128)} %get-tuple-element.50) | copy-start | bytes 196612
  197.3 6.2 %copy-start.19 = (f32[128,128]{1,0:T(8,128)S(1)}, f32[128,128]{1,0:T(8,128)}, u32[]{:S(2)}) copy-start(f32[128,128]{1,0:T(8,128)} %get-tuple-element.49) | copy-start | bytes 196612
  197.3 17.8 %all-to-all-start.7 = ((bf16[16,128,128]{1,2,0:T(8,128)(2,1)}), bf16[16,128,128]{1,2,0:T(8,128)(2,1)}, u32[]{:S(2)}, u32[]{:S(2)}) async-start(bf16[16,128,128]{1,2,0:T(8,128)(2,1)} %broadcast_in_dim.14), calls=%async_computation.7 | async-start | bytes 1048576 | tf_op jit(solution)/shard_map/all_to_all | solution.py:203
  202.8 13.8 %collective-permute-start.5 = (bf16[128,4096]{1,0:T(8,128)(2,1)}, bf16[128,4096]{1,0:T(8,128)(2,1)}, u32[]{:S(2)}, u32[]{:S(2)}) collective-permute-start(bf16[128,4096]{1,0:T(8,128)(2,1)} %broadcast_select_fusion.4), channel_id=1, source_target_pairs={{0,1},{1,0},{2,3},{3,2},{4,5},{5,4},{6,7},{7,6},{8,9},{9,8},{10,11... | collective-permute-start | bytes 3145736 | tf_op jit(solution)/shard_map/ppermute | solution.py:198
  202.8 2.4 %collective-permute-start.7 = (f32[8,16,16]{1,0,2:T(8,128)S(1)}, f32[8,16,16]{1,0,2:T(8,128)S(1)}, u32[]{:S(2)}, u32[]{:S(2)}) collective-permute-start(f32[8,16,16]{1,0,2:T(8,128)S(1)} %broadcast_select_fusion.8), channel_id=1, source_target_pairs={{0,1},{1,0},{2,3},{3,2},{4,5},{5,4},{6,7},{7,6},{8,9},{9,8},{10,11... | collective-permute-start | bytes 24584 | tf_op jit(solution)/shard_map/ppermute | solution.py:198
  203.6 2.3 %collective-permute-start.6 = (f32[128,128]{0,1:T(8,128)S(1)}, f32[128,128]{0,1:T(8,128)S(1)}, u32[]{:S(2)}, u32[]{:S(2)}) collective-permute-start(f32[128,128]{0,1:T(8,128)S(1)} %broadcast_select_fusion.11), channel_id=1, source_target_pairs={{0,1},{1,0},{2,3},{3,2},{4,5},{5,4},{6,7},{7,6},{8,9},{9,8},{10,11... | collective-permute-start | bytes 196616 | tf_op jit(solution)/shard_map/ppermute | solution.py:198
  216.5 3.0 %collective-permute-start.10 = (bf16[2048,128]{1,0:T(8,128)(2,1)S(1)}, bf16[2048,128]{1,0:T(8,128)(2,1)S(1)}, u32[]{:S(2)}, u32[]{:S(2)}) collective-permute-start(bf16[2048,128]{1,0:T(8,128)(2,1)S(1)} %bitcast.99), channel_id=1, source_target_pairs={{0,1},{1,0},{2,3},{3,2},{4,5},{5,4},{6,7},{7,6},{8,9},{9,8},{10,11... | collective-permute-start | bytes 1572872 | tf_op jit(solution)/shard_map/ppermute | solution.py:198
where the time goes:
time: 231 us; the launch traced here: 229 us
  waiting for transfers between devices  75.6 us (33%)
  Pallas kernels  61.3 us (27%)
  starting transfers between devices  47.6 us (21%)
  local copies, waits for them, and re-layouts  24.9 us (11%)
  other arithmetic  18.4 us (8%)
    all_to_all x8, waiting for transfers between devices, exchange(): lax.all_to_all(chunks, 'blk', split_axis=0, concat_axis=0, tiled=True)  71.2 us
    all_to_all x8, starting transfers between devices, exchange(): lax.all_to_all(chunks, 'blk', split_axis=0, concat_axis=0, tiled=True)  45 us
    pallas_call x1, Pallas kernels, body(): call(turn_kernel, 'turn', [sds(act_shape, BF), sds((tokens, tokens), F32)...  13.5 us
    pallas_call x1, Pallas kernels, body(): call(lower_kernel, 'lower', [sds(act_shape, F32), sds((tokens, tokens), F...  7.92 us
    pallas_call x1, Pallas kernels, body(): call(middle_kernel, 'middle', [sds(act_shape, F32), sds((span, span), F32...  7.92 us
    select_n x5, other arithmetic, by_section(): return (jnp.where(core == 0, own, other), jnp.where(core == 0, other, own))  7.25 us
    pallas_call x1, Pallas kernels, body(): call(forward_kernel, 'forward', [sds(act_shape, BF), sds(col_shape, BF),...  7.12 us
    pallas_call x1, Pallas kernels, body(): call(last_kernel, 'last', [sds(act_shape, BF), sds((span, span), F32)], g...  6.85 us
  transfers between devices with their start and end apart: 19, of which 10 were waited for; matrix products, arithmetic and copies ran while one was open for 13% of the time, Pallas kernels for 27%

commit v1 on v0

v1 whole, which is shorter than its diff:
```python
import functools

import jax
import jax.numpy as jnp
import numpy as np
from jax import lax
from jax.experimental import pallas as pl
from jax.experimental.pallas import tpu as pltpu
from jax.sharding import PartitionSpec as P

BF = jnp.bfloat16
F32 = jnp.float32
NN = (((1,), (0,)), ((), ()))
NT = (((1,), (1,)), ((), ()))


def mm(a, b, dims=NN, precision=None):
    return lax.dot_general(a, b, dims, preferred_element_type=F32, precision=precision)


def whole(shape):
    return pl.BlockSpec(shape, lambda *_: (0,) * len(shape))


def call(kernel, name, out_shape, grid, in_specs, out_specs, scratch=()):
    params = pltpu.CompilerParams(vmem_limit_bytes=56 * 1024 * 1024)
    estimate = pl.CostEstimate(flops=1 << 28, bytes_accessed=8 << 20, transcendentals=0)
    spec = pltpu.PrefetchScalarGridSpec(
        num_scalar_prefetch=1, grid=grid, in_specs=in_specs, out_specs=out_specs, scratch_shapes=scratch
    )
    return pl.pallas_call(
        kernel, out_shape=out_shape, grid_spec=spec, compiler_params=params, cost_estimate=estimate, name=name
    )


def sds(shape, dtype):
    return jax.ShapeDtypeStruct(shape, dtype)


def columns(q):
    return slice(128 * q, 128 * (q + 1))


def half(q):
    return slice(64 * q, 64 * (q + 1))


def pick(p, low, high):
    return jnp.where(p[0] == 0, low.astype(F32), high.astype(F32))


def regroup(wide, q, blocks):
    parts = [wide[pl.ds(2 * q + h, blocks, stride=blocks), :] for h in range(2)]
    return jnp.concatenate(parts, axis=0).astype(BF)


def diagonal(product):
    lane = lax.broadcasted_iota(jnp.int32, (64, 128), 1)
    return jnp.where(lane < 64, product[:64], product[64:])


def spread(left, onehot, mask):
    return (mm(left, onehot, NT) * mask.astype(F32)).astype(BF)


def spread_turned(left, onehot, mask):
    return (mm(onehot, left, NT) * mask.astype(F32).T).astype(BF)


def gate_kernel(p, keep, recv, upstream, left_own, left_other, onehot, mask, back, left_t):
    @pl.when(pl.program_id(0) == 0)
    def _():
        left = pick(p, left_other[...], left_own[...]).astype(BF)
        left_t[...] = spread_turned(left, onehot[...], mask[...])

    act = pick(p, recv[...], keep[0])
    gate = (upstream[0].astype(F32) * act).astype(BF)
    back[...] = mm(left_t[...], gate).astype(BF)


def expand_kernel(section, p, first, first_other, second, second_other, first_bd, first_bt, second_bd, second_bt):
    side = first.shape[1]
    zero = jnp.zeros((side, side), F32)
    for own, other, straight, turned in (
        (first, first_other, first_bd, first_bt),
        (second, second_other, second_bd, second_bt),
    ):
        for q in range(own.shape[0] // 2):
            pair = [(own[2 * q + h], other[2 * q + h]) for h in range(2)]
            parts = [pick(p, b, a) if section else pick(p, a, b) for a, b in pair]
            block = jnp.concatenate(
                [jnp.concatenate([parts[0], zero], axis=1), jnp.concatenate([zero, parts[1]], axis=1)], axis=0
            )
            straight[q] = block.astype(BF)
            turned[q] = block.T.astype(BF)


def forward_kernel(
    p,
    keep,
    recv,
    right_own,
    right_other,
    first_bd,
    second_bd,
    eye,
    rows,
    mixed,
    right_act,
    act_0,
    act_1,
    right_t_1,
    right_t_0,
    right_0,
    wide,
):
    act_0[...] = pick(p, keep[0], recv[...]).astype(BF)
    act_1[...] = pick(p, recv[...], keep[0]).astype(BF)
    low = pick(p, right_own[...], right_other[...]).astype(BF)
    high = pick(p, right_other[...], right_own[...]).astype(BF)
    right_0[...] = low
    right_t_0[...] = low.astype(F32).T.astype(BF)
    right_t_1[...] = high.astype(F32).T.astype(BF)
    right_act[...] = mm(high, act_1[...]).astype(BF)
    pairs = first_bd.shape[0]
    for q in range(pairs):
        wide[columns(q), :] = mm(first_bd[q], right_act[:, columns(q)], NT)
    for q in range(pairs):
        pair = regroup(wide, q, 2 * pairs)
        mixed[columns(q), :] = pair
        hidden = mm(second_bd[q], pair).astype(BF)
        rows[:, columns(q)] = mm(eye[...], hidden, NT).astype(BF)


def middle_kernel(
    p,
    back,
    second_bt,
    first_bt,
    mixed,
    right_act,
    right_t,
    act,
    right_low,
    act_low,
    right_act_low,
    chan_back,
    right_grad,
    first_grad,
    second_grad,
    wide,
    turned,
):
    right_act_low[...] = mm(right_low[...], act_low[...]).astype(BF)
    pairs = first_bt.shape[0]
    for q in range(pairs):
        wide[columns(q), :] = mm(second_bt[q], back[:, columns(q)], NT)
        second_grad[half(q), :] = diagonal(mm(mixed[columns(q), :], back[:, columns(q)]).T).astype(BF)
    for q in range(pairs):
        pair = regroup(wide, q, 2 * pairs)
        first_grad[half(q), :] = diagonal(mm(pair, right_act[:, columns(q)])).astype(BF)
        piece = mm(first_bt[q], pair).astype(BF)
        turned[columns(q), :] = piece
        chan_back[:, columns(q)] = mm(right_t[...], piece, NT)
    right_grad[...] = mm(act[...], turned[...]).T


def turn_kernel(
    p,
    rows,
    upstream,
    act,
    chan_back,
    act_low,
    left_own,
    left_other,
    second_bt,
    first_bt,
    eye,
    onehot,
    mask,
    input_grad,
    left_grad,
    gate_low,
    back_low,
    mixed_grad,
    sent,
    wide,
    left_acc,
    left,
    left_t_low,
):
    step = pl.program_id(0)
    steps = pl.num_programs(0)
    pairs = second_bt.shape[0]

    @pl.when(step == 0)
    def _():
        left[...] = spread(pick(p, left_other[...], left_own[...]).astype(BF), onehot[...], mask[...])
        left_t_low[...] = spread_turned(pick(p, left_own[...], left_other[...]).astype(BF), onehot[...], mask[...])

    gy = upstream[0].astype(F32)
    carried = mm(left[...], rows[...])
    incoming = (gy * carried + chan_back[...]).astype(BF)
    input_grad[...] = incoming
    gate = (gy * act[...].astype(F32)).astype(BF)
    term = mm(gate, rows[...], NT)

    @pl.when(step == 0)
    def _():
        left_acc[...] = term

    @pl.when(step > 0)
    def _():
        left_acc[...] += term

    gate = (incoming.astype(F32) * act_low[...].astype(F32)).astype(BF)
    gate_low[...] = gate
    back = mm(left_t_low[...], gate).astype(BF)
    back_low[...] = back
    for q in range(pairs):
        at = pl.multiple_of((step * pairs + q) * 128, 128)
        wide[pl.ds(at, 128), :] = mm(second_bt[q], back[:, columns(q)], NT)

    @pl.when(step == steps - 1)
    def _():
        for q in range(first_bt.shape[0]):
            pair = regroup(wide, q, 2 * first_bt.shape[0])
            mixed_grad[columns(q), :] = pair
            piece = mm(first_bt[q], pair).astype(BF)
            sent[:, columns(q)] = mm(eye[...], piece, NT).astype(BF)
        left_grad[...] = mm(
            left_acc[...] * mask[...].astype(F32), onehot[...].astype(F32), precision=lax.Precision.HIGHEST
        )


def lower_kernel(
    p,
    rows,
    first_bd,
    second_bd,
    left_own,
    left_other,
    gate,
    back,
    mixed_grad,
    onehot,
    mask,
    carried,
    left_grad,
    first_grad,
    second_grad,
    wide,
    turned,
):
    pairs = first_bd.shape[0]
    left = spread(pick(p, left_own[...], left_other[...]).astype(BF), onehot[...], mask[...])
    for q in range(pairs):
        wide[columns(q), :] = mm(first_bd[q], rows[:, columns(q)], NT)
        first_grad[half(q), :] = diagonal(mm(mixed_grad[columns(q), :], rows[:, columns(q)])).astype(BF)
    for q in range(pairs):
        pair = regroup(wide, q, 2 * pairs)
        second_grad[half(q), :] = diagonal(mm(pair, back[:, columns(q)]).T).astype(BF)
        hidden = mm(second_bd[q], pair).astype(BF)
        turned[columns(q), :] = hidden
        carried[:, columns(q)] = mm(left, hidden, NT)
    term = mm(gate[...], turned[...])
    left_grad[...] = mm(term * mask[...].astype(F32), onehot[...].astype(F32), precision=lax.Precision.HIGHEST)


def last_kernel(p, received, right_t, upstream, carried, act, input_grad, right_grad):
    step = pl.program_id(0)
    chan_back = mm(right_t[...], received[...])
    input_grad[...] = (upstream[...].astype(F32) * carried[...] + chan_back).astype(BF)
    term = mm(received[...], act[...], NT)

    @pl.when(step == 0)
    def _():
        right_grad[...] = term

    @pl.when(step > 0)
    def _():
        right_grad[...] += term


def total_kernel(p, pieces, out):
    total = pieces[0].astype(F32)
    for i in range(1, pieces.shape[0]):
        total += pieces[i].astype(F32)
    out[...] = total.astype(BF)


def unpack_kernel(p, kept, came, first, second):
    side = first.shape[1]

    def unpack(array, out):
        for q in range(first.shape[0] // 2):
            parts = []
            for row in range(64 * q, 64 * (q + 1), min(64, array.shape[2])):
                owner, at = divmod(row, array.shape[2])
                parts.append(array[owner, 0, at : at + min(64, array.shape[2]), :].astype(F32))
            value = jnp.concatenate(parts, axis=0) if len(parts) > 1 else parts[0]
            out[2 * q] = value[:, :side]
            out[2 * q + 1] = value[:, side:]

    @pl.when(p[0] == 0)
    def _():
        unpack(kept, first)
        unpack(came, second)

    @pl.when(p[0] != 0)
    def _():
        unpack(kept, second)
        unpack(came, first)


def swap(value):
    return lax.ppermute(value, "pipe", [(0, 1), (1, 0)])


def after(value, *others):
    return lax.optimization_barrier((value, *others))[0]


def exchange(rows, devices):
    chunks = rows.reshape(devices, rows.shape[0] // devices, *rows.shape[1:])
    return lax.all_to_all(chunks, "blk", split_axis=0, concat_axis=0, tiled=True).reshape(rows.shape)


def body(x_saved, cotangent, seq_right, seq_left, chan_first, chan_second):
    devices = lax.axis_size("blk")
    core = lax.axis_index("pipe")
    p = core.astype(jnp.int32).reshape(1)
    saved = x_saved[0]
    micro, tokens, width = saved.shape
    span = seq_right.shape[2]
    per, count = seq_left.shape[1], seq_left.shape[2]
    blocks, side = chan_first.shape[1], chan_first.shape[2]
    pairs = blocks // 2

    received = swap(lax.dynamic_index_in_dim(saved, 1 - core, 0, keepdims=False))
    left_own = seq_left[0].reshape(per * count, count)
    left_other = swap(left_own)
    right_own = seq_right[0, 0]
    right_other = swap(right_own)
    first_own, first_other = chan_first[0], swap(chan_first[0])
    second_own, second_other = chan_second[0], swap(chan_second[0])

    place = np.arange(tokens)
    mask = jnp.asarray(place[:, None] // count == place[None, :] % per, BF)
    onehot = jnp.asarray(place[:, None] // per == np.arange(count)[None, :], BF)
    eye = jnp.asarray(np.eye(tokens), BF)

    step = width // 4
    square = whole((tokens, tokens))
    narrow = whole((tokens, count))
    moving = pl.BlockSpec((tokens, step), lambda i, *_: (0, i))
    chosen = pl.BlockSpec((1, tokens, step), lambda i, p: (p[0], 0, i))
    act_shape = (tokens, width)
    col_shape = (width, tokens)
    pair_shape = (pairs, 2 * side, 2 * side)
    grad_shape = (pairs * side, 2 * side)
    act_full, col_full, pair_full, grad_full = map(whole, (act_shape, col_shape, pair_shape, grad_shape))
    chosen_full = pl.BlockSpec((1,) + act_shape, lambda i, p: (p[0], 0, 0))
    box = whole((blocks, side, side))
    squared = sds((tokens, tokens), BF)

    back_1 = call(
        gate_kernel,
        "gate",
        sds(act_shape, BF),
        (width // step,),
        [chosen, moving, chosen, narrow, narrow, narrow, square],
        moving,
        [pltpu.VMEM((tokens, tokens), BF)],
    )(p, saved, received, cotangent, left_own, left_other, onehot, mask)
    returned_1 = exchange(back_1, devices)
    p = after(p, back_1)

    def expand(p, section):
        return call(
            functools.partial(expand_kernel, section),
            "expand",
            [sds(pair_shape, BF)] * 4,
            (1,),
            [box] * 4,
            [pair_full] * 4,
        )(p, first_own, first_other, second_own, second_other)

    fbd_1, fbt_1, sbd_1, sbt_1 = expand(p, 1)
    rows_1, mixed_1, right_act_1, act_0, act_1, right_t_1, right_t_0, right_0 = call(
        forward_kernel,
        "forward",
        [sds(act_shape, BF), sds(col_shape, BF)] + [sds(act_shape, BF)] * 3 + [squared] * 3,
        (1,),
        [chosen_full, act_full, square, square, pair_full, pair_full, square],
        [act_full, col_full] + [act_full] * 3 + [square] * 3,
        [pltpu.VMEM(col_shape, F32)],
    )(p, saved, received, right_own, right_other, fbd_1, sbd_1, eye)
    gathered_1 = exchange(rows_1, devices)
    p = after(p, rows_1)
    fbd_0, fbt_0, sbd_0, sbt_0 = expand(p, 0)

    right_act_0, chan_back_1, right_grad_1, first_1, second_1 = call(
        middle_kernel,
        "middle",
        [sds(act_shape, BF), sds(act_shape, F32), sds((span, span), F32)] + [sds(grad_shape, BF)] * 2,
        (1,),
        [act_full, pair_full, pair_full, col_full, act_full, square, act_full, square, act_full],
        [act_full, act_full, square, grad_full, grad_full],
        [pltpu.VMEM(col_shape, F32), pltpu.VMEM(col_shape, BF)],
    )(p, returned_1, sbt_1, fbt_1, mixed_1, right_act_1, right_t_1, act_1, right_0, act_0)
    gathered_0 = exchange(right_act_0, devices)

    def over_cores(first, second):
        came = swap(jnp.where(core == 0, second, first)).astype(F32)
        return (jnp.where(core == 0, first, second).astype(F32) + came).astype(BF)

    part_1 = over_cores(first_1, second_1)

    input_1, left_grad_1, gate_0, back_0, mixed_grad_0, sent_0 = call(
        turn_kernel,
        "turn",
        [
            sds(act_shape, BF),
            sds((tokens, count), F32),
            sds(act_shape, BF),
            sds(act_shape, BF),
            sds(col_shape, BF),
            sds(act_shape, BF),
        ],
        (width // step,),
        [
            moving,
            chosen,
            moving,
            moving,
            moving,
            narrow,
            narrow,
            pl.BlockSpec((step // (2 * side), 2 * side, 2 * side), lambda i, *_: (i, 0, 0)),
            pair_full,
            square,
            narrow,
            square,
        ],
        [moving, narrow, moving, moving, col_full, act_full],
        [pltpu.VMEM(col_shape, F32), pltpu.VMEM((tokens, tokens), F32)] + [pltpu.VMEM((tokens, tokens), BF)] * 2,
    )(
        p,
        gathered_1,
        cotangent,
        act_1,
        chan_back_1,
        act_0,
        left_own,
        left_other,
        sbt_0,
        fbt_0,
        eye,
        onehot,
        mask,
    )
    returned_0 = exchange(sent_0, devices)

    carried_0, left_grad_0, first_0, second_0 = call(
        lower_kernel,
        "lower",
        [sds(act_shape, F32), sds((tokens, count), F32)] + [sds(grad_shape, BF)] * 2,
        (1,),
        [act_full, pair_full, pair_full, narrow, narrow, act_full, act_full, col_full, narrow, square],
        [act_full, narrow, grad_full, grad_full],
        [pltpu.VMEM(col_shape, F32), pltpu.VMEM(col_shape, BF)],
    )(p, gathered_0, fbd_0, sbd_0, left_own, left_other, gate_0, back_0, mixed_grad_0, onehot, mask)

    parts = jnp.stack([over_cores(first_0, second_0), part_1]).reshape(2, devices, -1, 2 * side).swapaxes(0, 1)
    pieces = lax.all_to_all(after(parts, returned_0), "blk", split_axis=0, concat_axis=0, tiled=True)
    own = call(
        total_kernel, "total", sds(pieces.shape[1:], BF), (1,), [whole(pieces.shape)], whole(pieces.shape[1:])
    )(p, pieces)
    everyone = jnp.broadcast_to(own[None], (devices,) + own.shape)
    sums = lax.all_to_all(everyone, "blk", split_axis=0, concat_axis=0, tiled=True)
    sums_came = swap(lax.dynamic_slice_in_dim(sums, 1 - core, 1, axis=1))

    input_0, right_grad_0 = call(
        last_kernel,
        "last",
        [sds(act_shape, BF), sds((span, span), F32)],
        (width // step,),
        [moving, square, moving, moving, moving],
        [moving, square],
    )(p, returned_0, right_t_0, input_1, carried_0, act_0)

    def to_section(low, high):
        return jnp.where(core == 0, low, high) + swap(jnp.where(core == 0, high, low))

    came = swap(jnp.where(core == 0, input_1, input_0))
    input_grad = jnp.where(core == 0, jnp.stack([input_0, came]), jnp.stack([came, input_1]))
    left_grad = to_section(left_grad_0, left_grad_1).reshape(per, count, count)
    right_grad = to_section(right_grad_0, right_grad_1)
    p = after(p, input_grad, left_grad, right_grad)
    part = (sums.shape[0], 1) + sums.shape[2:]
    first_grad, second_grad = call(
        unpack_kernel,
        "unpack",
        [sds((blocks, side, side), F32)] * 2,
        (1,),
        [pl.BlockSpec(part, lambda i, p: (0, p[0], 0, 0)), whole(part)],
        [box] * 2,
    )(p, sums, sums_came)
    return (
        input_grad[None],
        right_grad[None, None],
        left_grad[None],
        first_grad[None],
        second_grad[None],
    )


def solution(mesh):
    in_specs = (
        P("pipe", None, "blk", None),
        P(None, "blk", None),
        P("pipe", "blk", None, None),
        P("pipe", "blk", None, None),
        P("pipe", None, None, None),
        P("pipe", None, None, None),
    )
    out_specs = (
        P("pipe", None, "blk", None),
        P("pipe", "blk", None, None),
        P("pipe", "blk", None, None),
        P("pipe", None, None, None),
        P("pipe", None, None, None),
    )
    return jax.shard_map(body, mesh=mesh, in_specs=in_specs, out_specs=out_specs, check_vma=False)
```

time: 231 us -> 202 us (0.87)
  blocking collectives: 0 us -> 30.8 us
  local copies, waits for them, and re-layouts: 24.9 us -> 6.81 us
  starting transfers between devices: 47.6 us -> 32.8 us
  waiting for transfers between devices: 75.6 us -> 61.5 us
  other arithmetic: 18.4 us -> 7.55 us
    all_to_all x8 -> x4, waiting for transfers between devices: 71.2 us -> 38.9 us  [exchange(): lax.all_to_all(chunks, 'blk', split_axis=0, concat_axis=0, tiled=True)]
    all_to_all x0 -> x1, blocking collectives: none -> 30.8 us  [body(): lax.all_to_all(after(parts, returned_0), 'blk', split_axis=0, concat_axis...]
    all_to_all x8 -> x4, starting transfers between devices: 45 us -> 26.3 us  [exchange(): lax.all_to_all(chunks, 'blk', split_axis=0, concat_axis=0, tiled=True)]
    all_to_all x0 -> x1, waiting for transfers between devices: none -> 13.8 us  [body(): lax.all_to_all(everyone, 'blk', split_axis=0, concat_axis=0, tiled=True)]
    another operation x6 -> x0, local copies, waits for them, and re-layouts: 8.15 us -> none  [the longest x3 4.92 us: body(): second_grad[None]]
    ppermute x11, waiting for transfers between devices: 4.41 us -> 8.81 us  [swap(): return lax.ppermute(value, 'pipe', [(0, 1), (1, 0)])]
    mul x4 -> x0, local copies, waits for them, and re-layouts: 4.02 us -> none  [spread_left(): full = (block[:, :, :, None] * apart).reshape(per * count, count * per)]
    all_to_all x0 -> x1, starting transfers between devices: none -> 3.89 us  [body(): lax.all_to_all(everyone, 'blk', split_axis=0, concat_axis=0, tiled=True)]
  transfers between devices with their start and end apart: 19 -> 16, of which waited for: 10 -> 10; matrix products, arithmetic and copies ran while one was open for 13% -> 4% of each run, Pallas kernels for 27% -> 25%
where the time goes in v1:
time: 202 us; the launch traced here: 200 us
  waiting for transfers between devices  61.5 us (30%)
  Pallas kernels  60 us (30%)
  starting transfers between devices  32.8 us (16%)
  blocking collectives  30.8 us (15%)
  other arithmetic  7.55 us (4%)
  local copies, waits for them, and re-layouts  6.81 us (3%)
    all_to_all x4, waiting for transfers between devices, exchange(): lax.all_to_all(chunks, 'blk', split_axis=0, concat_axis=0, tiled=True)  38.9 us
    all_to_all x1, blocking collectives, body(): lax.all_to_all(after(parts, returned_0), 'blk', split_axis=0, concat_axis...  30.8 us
    all_to_all x4, starting transfers between devices, exchange(): lax.all_to_all(chunks, 'blk', split_axis=0, concat_axis=0, tiled=True)  26.3 us
    all_to_all x1, waiting for transfers between devices, body(): lax.all_to_all(everyone, 'blk', split_axis=0, concat_axis=0, tiled=True)  13.8 us
    pallas_call x1, Pallas kernels, body(): call(turn_kernel, 'turn', [sds(act_shape, BF), sds((tokens, count), F32),...  11.3 us
    pallas_call x2, Pallas kernels, expand(): call(functools.partial(expand_kernel, section), 'expand', [sds(pair_shape...  10.1 us
    ppermute x11, waiting for transfers between devices, swap(): return lax.ppermute(value, 'pipe', [(0, 1), (1, 0)])  8.81 us
    pallas_call x1, Pallas kernels, body(): call(forward_kernel, 'forward', [sds(act_shape, BF), sds(col_shape, BF)]...  8.15 us
  transfers between devices with their start and end apart: 16, of which 10 were waited for; matrix products, arithmetic and copies ran while one was open for 4% of the time, Pallas kernels for 25%

profile of v1, /device:TPU:0, one launch (start us, length us, event | category | flops | bytes accessed | tf_op | source)
XLA Modules:
  0.0 200.5 jit_solution(5352982154841300739)
XLA Ops:
  0.6 0.0 copy-start.17
  0.6 1.3 dynamic-slice_bitcast_fusion
  1.9 0.5 collective-permute-start
  2.5 0.1 collective-permute-start.1
  2.6 2.2 %collective-permute-done.1.left_other = bf16[128,16]{1,0:T(8,128)(2,1)S(1)} collective-permute-done((bf16[128,16]{1,0:T(8,128)(2,1)S(1)}, bf16[128,16]{1,0:T(8,128)(2,1)S(1)}, u32[]{:S(2)}, u32[]{:S(2)}) %collective-permute-start.1) | collective-permute-done | bytes 4128 | tf_op jit(solution)/shard_map/ppermute | solution.py:318
  4.8 0.0 collective-permute-done.recv
  4.8 0.6 copy-done.18
  5.4 0.4 copy-done.8
  5.8 4.5 %gate.1 = bf16[128,4096]{1,0:T(8,128)(2,1)} custom-call(s32[1]{0:T(128)} %bitcast.p, bf16[2,128,4096]{2,1,0:T(8,128)(2,1)} %bitcast.27, bf16[128,4096]{1,0:T(8,128)(2,1)} %copy-done.8, bf16[2,128,4096]{2,1,0:T(8,128)(2,1)} %upstream.3, bf16[128,16]{1,0:T(8,128)(2,1)} %bitcast.47, bf16[128,16]{1,0:T(8,128)(2,1)} %copy-done.18, ...), custom_call_target="tpu_custom_call" | custom-call | flops 268435456 | bytes 8388608 | tf_op jit(solution)/shard_map/gate/pallas_call | solution.py:368
  10.3 8.4 %all-to-all-start.1 = ((bf16[16,8,4096]{2,1,0:T(8,128)(2,1)}), bf16[16,8,4096]{2,1,0:T(8,128)(2,1)S(1)}, u32[]{:S(2)}, u32[]{:S(2)}) async-start(bf16[16,8,4096]{2,1,0:T(8,128)(2,1)} %bitcast.38), calls=%async_computation.1 | async-start | bytes 2097152 | tf_op jit(solution)/shard_map/all_to_all | solution.py:327
  18.7 0.0 copy-done.2
  18.7 0.1 collective-permute-start.3
  18.8 0.5 collective-permute-start.4
  19.3 0.1 collective-permute-start.2
  19.3 2.1 %collective-permute-done.3.first_other = bf16[64,64,64]{2,1,0:T(8,128)(2,1)S(1)} collective-permute-done((bf16[64,64,64]{2,1,0:T(8,128)(2,1)S(1)}, bf16[64,64,64]{2,1,0:T(8,128)(2,1)S(1)}, u32[]{:S(2)}, u32[]{:S(2)}) %collective-permute-start.3) | collective-permute-done | bytes 524320 | tf_op jit(solution)/shard_map/ppermute | solution.py:318
  21.4 1.5 collective-permute-done.4.second_other
  22.9 1.0 copy-done.5
  23.9 5.0 %expand.2 = (bf16[32,128,128]{2,1,0:T(8,128)(2,1)}, bf16[32,128,128]{2,1,0:T(8,128)(2,1)}, bf16[32,128,128]{2,1,0:T(8,128)(2,1)}, bf16[32,128,128]{2,1,0:T(8,128)(2,1)}) custom-call(s32[1]{0:T(128)} %bitcast.p, bf16[64,64,64]{2,1,0:T(8,128)(2,1)} %bitcast.30, bf16[64,64,64]{2,1,0:T(8,128)(2,1)} %copy-done.4, bf16[64,64,64]{2,1,0:T(8,128)(2,1)} %bitcast.33, ...), custom_call_target="tpu_custom_call" | custom-call | flops 268435456 | bytes 8388608 | tf_op jit(solution)/shard_map/expand/pallas_call | solution.py:381
  28.9 0.0 collective-permute-done.2.right_other
  28.9 0.6 copy-done.24
  29.5 8.1 %forward.1 = (bf16[128,4096]{1,0:T(8,128)(2,1)}, bf16[4096,128]{1,0:T(8,128)(2,1)}, bf16[128,4096]{1,0:T(8,128)(2,1)}, bf16[128,4096]{1,0:T(8,128)(2,1)}, bf16[1...) custom-call(s32[1]{0:T(128)} %bitcast.p, ...), custom_call_target="tpu_custom_call" | custom-call | flops 268435456 | bytes 8388608 | tf_op jit(solution)/shard_map/forward/pallas_call | solution.py:391
  37.7 5.6 %all-to-all-done.1 = bf16[16,8,4096]{2,1,0:T(8,128)(2,1)S(1)} async-done(((bf16[16,8,4096]{2,1,0:T(8,128)(2,1)}), bf16[16,8,4096]{2,1,0:T(8,128)(2,1)S(1)}, u32[]{:S(2)}, u32[]{:S(2)}) %all-to-all-start.1) | async-done | bytes 1048608 | tf_op jit(solution)/shard_map/all_to_all | solution.py:327
  43.3 6.1 %all-to-all-start = ((bf16[16,8,4096]{2,1,0:T(8,128)(2,1)}), bf16[16,8,4096]{2,1,0:T(8,128)(2,1)S(1)}, u32[]{:S(2)}, u32[]{:S(2)}) async-start(bf16[16,8,4096]{2,1,0:T(8,128)(2,1)} %bitcast.46), calls=%async_computation | async-start | bytes 2097152 | tf_op jit(solution)/shard_map/all_to_all | solution.py:327
  49.4 7.9 %middle.1 = (bf16[128,4096]{1,0:T(8,128)(2,1)}, f32[128,4096]{1,0:T(8,128)}, f32[128,128]{1,0:T(8,128)}, bf16[2048,128]{1,0:T(8,128)(2,1)}, bf16[2048,128]{1,0:T(8,128)(2,1)}) custom-call(s32[1]{0:T(128)} %bitcast.p, bf16[128,4096]{1,0:T(8,128)(2,1)} %bitcast.41, bf16[32,128,128]{2,1,0:T(8,128)(2,1)} %get-tuple-element.50.second_bt, ...), custom_call_target="tpu_custom_call" | custom-call | flops 268435456 | bytes 8388608 | tf_op jit(solution)/shard_map/middle/pallas_call | solution.py:404
  57.2 15.4 %all-to-all-done = bf16[16,8,4096]{2,1,0:T(8,128)(2,1)S(1)} async-done(((bf16[16,8,4096]{2,1,0:T(8,128)(2,1)}), bf16[16,8,4096]{2,1,0:T(8,128)(2,1)S(1)}, u32[]{:S(2)}, u32[]{:S(2)}) %all-to-all-start) | async-done | bytes 1048608 | tf_op jit(solution)/shard_map/all_to_all | solution.py:327
  72.7 5.9 %all-to-all-start.3 = ((bf16[16,8,4096]{2,1,0:T(8,128)(2,1)}), bf16[16,8,4096]{2,1,0:T(8,128)(2,1)S(1)}, u32[]{:S(2)}, u32[]{:S(2)}) async-start(bf16[16,8,4096]{2,1,0:T(8,128)(2,1)} %bitcast.45), calls=%async_computation.3 | async-start | bytes 2097152 | tf_op jit(solution)/shard_map/all_to_all | solution.py:327
  78.6 5.0 %expand.3 = (bf16[32,128,128]{2,1,0:T(8,128)(2,1)}, bf16[32,128,128]{2,1,0:T(8,128)(2,1)}, bf16[32,128,128]{2,1,0:T(8,128)(2,1)}, bf16[32,128,128]{2,1,0:T(8,128)(2,1)}) custom-call(s32[1]{0:T(128)} %bitcast.p, bf16[64,64,64]{2,1,0:T(8,128)(2,1)} %bitcast.31, bf16[64,64,64]{2,1,0:T(8,128)(2,1)} %copy-done.4, bf16[64,64,64]{2,1,0:T(8,128)(2,1)} %bitcast.34, ...), custom_call_target="tpu_custom_call" | custom-call | flops 268435456 | bytes 8388608 | tf_op jit(solution)/shard_map/expand/pallas_call | solution.py:381
  83.6 11.3 %turn.1 = (bf16[128,4096]{1,0:T(8,128)(2,1)}, f32[128,16]{1,0:T(8,128)}, bf16[128,4096]{1,0:T(8,128)(2,1)}, bf16[128,4096]{1,0:T(8,128)(2,1)}, bf16[4096,128]{1,0:T(8,128)(2,1)}, /*index=5*/bf16[128,4096]{1,0:T(8,128)(2,1)}) custom-call(s32[1]{0:T(128)} %bitcast.p, bf16[128,4096]{1,0:T(8,128)(2,1)} %bitcast.37, bf16[2,128,4096]{2,1,0:T(8,128)(2,1)} %upstream.3, ...), custom_call_target="tpu_custom_call" | custom-call | flops 268435456 | bytes 8388608 | tf_op jit(solution)/shard_map/turn/pallas_call | solution.py:421
  95.0 6.5 %all-to-all-done.3 = bf16[16,8,4096]{2,1,0:T(8,128)(2,1)S(1)} async-done(((bf16[16,8,4096]{2,1,0:T(8,128)(2,1)}), bf16[16,8,4096]{2,1,0:T(8,128)(2,1)S(1)}, u32[]{:S(2)}, u32[]{:S(2)}) %all-to-all-start.3) | async-done | bytes 1048608 | tf_op jit(solution)/shard_map/all_to_all | solution.py:327
  101.4 6.0 %all-to-all-start.2 = ((bf16[16,8,4096]{2,1,0:T(8,128)(2,1)}), bf16[16,8,4096]{2,1,0:T(8,128)(2,1)S(1)}, u32[]{:S(2)}, u32[]{:S(2)}) async-start(bf16[16,8,4096]{2,1,0:T(8,128)(2,1)} %bitcast.44), calls=%async_computation.2 | async-start | bytes 2097152 | tf_op jit(solution)/shard_map/all_to_all | solution.py:327
  107.5 0.1 broadcast_select_fusion.1
  107.6 0.1 collective-permute-start.9
  107.6 0.0 copy-done.6
  107.6 7.7 %lower.1 = (f32[128,4096]{1,0:T(8,128)}, f32[128,16]{1,0:T(8,128)}, bf16[2048,128]{1,0:T(8,128)(2,1)}, bf16[2048,128]{1,0:T(8,128)(2,1)}) custom-call(s32[1]{0:T(128)} %bitcast.p, bf16[128,4096]{1,0:T(8,128)(2,1)} %bitcast.36, bf16[32,128,128]{2,1,0:T(8,128)(2,1)} %get-tuple-element.64.first_bd, bf16[32,128,128]{2,1,0:T(8,128)(2,1)} %get-tuple-element.65.second_bd, ...), custom_call_target="tpu_custom_call" | custom-call | flops 268435456 | bytes 8388608 | tf_op jit(solution)/shard_map/lower/pallas_call | solution.py:466
  115.3 1.2 broadcast_select_fusion.2
  116.5 0.6 collective-permute-start.8
  117.1 0.0 collective-permute-done.9
  117.1 0.2 add_convert_fusion
  117.3 1.3 collective-permute-done.8
  118.6 0.2 add_convert_fusion.1
  118.9 0.1 maximum_bitcast_fusion
  119.0 11.4 %all-to-all-done.2 = bf16[16,8,4096]{2,1,0:T(8,128)(2,1)S(1)} async-done(((bf16[16,8,4096]{2,1,0:T(8,128)(2,1)}), bf16[16,8,4096]{2,1,0:T(8,128)(2,1)S(1)}, u32[]{:S(2)}, u32[]{:S(2)}) %all-to-all-start.2) | async-done | bytes 1048608 | tf_op jit(solution)/shard_map/all_to_all | solution.py:327
  130.3 30.8 %all_to_all.30.pieces = bf16[16,2,128,128]{3,2,1,0:T(8,128)(2,1)} all-to-all(bf16[16,2,128,128]{3,2,1,0:T(8,128)(2,1)S(1)} %maximum_bitcast_fusion), channel_id=1, replica_groups=mesh['blk'=16,'pipe'=2] {'blk'}, dimensions={0} | all-to-all | bytes 2097152 | tf_op jit(solution)/shard_map/all_to_all | solution.py:477
  161.1 2.0 total.1
  163.1 2.1 %broadcast_in_dim.17 = bf16[16,2,128,128]{3,2,1,0:T(8,128)(2,1)} broadcast(bf16[2,128,128]{2,1,0:T(8,128)(2,1)} %total.1), dimensions={1,2,3} | broadcast | bytes 1114112 | tf_op jit(solution)/shard_map/broadcast_in_dim | solution.py:481
  165.1 3.9 %all-to-all-start.5 = ((bf16[16,2,128,128]{3,2,1,0:T(8,128)(2,1)}), bf16[16,2,128,128]{3,2,1,0:T(8,128)(2,1)S(1)}, u32[]{:S(2)}, u32[]{:S(2)}) async-start(bf16[16,2,128,128]{3,2,1,0:T(8,128)(2,1)} %broadcast_in_dim.17), calls=%async_computation.5 | async-start | bytes 2097152 | tf_op jit(solution)/shard_map/all_to_all | solution.py:482
  169.0 0.0 copy-start
  169.1 4.9 %last.1 = (bf16[128,4096]{1,0:T(8,128)(2,1)}, f32[128,128]{1,0:T(8,128)}) custom-call(s32[1]{0:T(128)} %bitcast.p, bf16[128,4096]{1,0:T(8,128)(2,1)} %bitcast.39, bf16[128,128]{1,0:T(8,128)(2,1)} %get-tuple-element.61.right_t, bf16[128,4096]{1,0:T(8,128)(2,1)} %get-tuple-element.62.upstream, f32[128,4096]{1,0:T(8,128)} %get-tuple-element.69.carried, ...), custom_call_target="tpu_custom_call" | custom-call | flops 268435456 | bytes 8388608 | tf_op jit(solution)/shard_map/last/pallas_call | solution.py:485
  174.0 0.0 copy-start.19
  174.0 1.1 broadcast_select_fusion
  175.1 0.0 collective-permute-start.5
  175.1 0.6 collective-permute-start.7
  175.7 0.1 collective-permute-start.6
  175.8 1.7 collective-permute-done.7
  177.5 0.6 select_add_fusion
  178.1 13.8 %all-to-all-done.5.kept = bf16[16,2,128,128]{3,2,1,0:T(8,128)(2,1)S(1)} async-done(((bf16[16,2,128,128]{3,2,1,0:T(8,128)(2,1)}), bf16[16,2,128,128]{3,2,1,0:T(8,128)(2,1)S(1)}, u32[]{:S(2)}, u32[]{:S(2)}) %all-to-all-start.5) | async-done | bytes 1048608 | tf_op jit(solution)/shard_map/all_to_all | solution.py:482
  192.0 0.1 collective-permute-start.10
  192.0 0.0 collective-permute-done.6
  192.1 0.8 select_add_fusion.1
  192.9 0.0 collective-permute-done.5
  192.9 3.2 %maximum_select_fusion = bf16[1,2,128,4096]{3,2,1,0:T(8,128)(2,1)} fusion(bf16[1,1,128,4096]{3,2,1,0:T(8,128)(2,1)} %bitcast.16, bf16[1,1,128,4096]{3,2,1,0:T(8,128)(2,1)S(1)} %bitcast.40, bf16[1,1,128,4096]{3,2,1,0:T(8,128)(2,1)S(1)} %bitcast.29, pred[]{:T(512)S(6)} %eq.2), kind=kLoop, calls=%fused_computation | loop fusion | flops 3145728 | bytes 5242881 | tf_op jit(solution)/shard_map/jit(_where)/select_n | solution.py:498
  196.1 0.0 collective-permute-done.10.came
  196.1 0.8 copy-done.16
  196.9 3.6 %unpack.1 = (f32[64,64,64]{2,1,0:T(8,128)}, f32[64,64,64]{2,1,0:T(8,128)}) custom-call(s32[1]{0:T(128)} %bitcast.p, bf16[16,2,128,128]{3,2,1,0:T(8,128)(2,1)} %copy-done.1, bf16[16,1,128,128]{3,2,1,0:T(8,128)(2,1)} %copy-done.16), custom_call_target="tpu_custom_call" | custom-call | flops 268435456 | bytes 8388608 | tf_op jit(solution)/shard_map/unpack/pallas_call | solution.py:503
  (43 shorter events, 0.1 us)
Async XLA Ops:
  0.6 1.8 copy-start.17
  1.9 2.9 %collective-permute-start = (bf16[128,4096]{1,0:T(8,128)(2,1)S(1)}, bf16[128,4096]{1,0:T(8,128)(2,1)S(1)}, u32[]{:S(2)}, u32[]{:S(2)}) collective-permute-start(bf16[128,4096]{1,0:T(8,128)(2,1)S(1)} %dynamic-slice_bitcast_fusion), channel_id=1, source_target_pairs={{0,1},{1,0},{2,3},{3,2},{4,5},{5,4},{6,7},{7,6},{8,9},{9,8},{10,11... | collective-permute-start | bytes 3145736 | tf_op jit(solution)/shard_map/ppermute | solution.py:318
  2.5 2.3 %collective-permute-start.1 = (bf16[128,16]{1,0:T(8,128)(2,1)S(1)}, bf16[128,16]{1,0:T(8,128)(2,1)S(1)}, u32[]{:S(2)}, u32[]{:S(2)}) collective-permute-start(bf16[128,16]{1,0:T(8,128)(2,1)S(1)} %bitcast.50), channel_id=1, source_target_pairs={{0,1},{1,0},{2,3},{3,2},{4,5},{5,4},{6,7},{7,6},{8,9},{9,8},{10,11... | collective-permute-start | bytes 12296 | tf_op jit(solution)/shard_map/ppermute | solution.py:318
  4.8 0.6 copy-start.18
  4.8 1.0 copy-start.8
  5.8 13.5 %copy-start.23 = (bf16[1,1,128,128]{3,2,1,0:T(8,128)(2,1)S(1)}, bf16[1,1,128,128]{3,2,1,0:T(8,128)(2,1)}, u32[]{:S(2)}) copy-start(bf16[1,1,128,128]{3,2,1,0:T(8,128)(2,1)} %param.11) | copy-start | bytes 98308
  10.3 8.4 %copy-start.2 = (bf16[1,64,64,64]{3,2,1,0:T(8,128)(2,1)S(1)}, bf16[1,64,64,64]{3,2,1,0:T(8,128)(2,1)}, u32[]{:S(2)}) copy-start(bf16[1,64,64,64]{3,2,1,0:T(8,128)(2,1)} %param.13) | copy-start | bytes 1572868
  10.3 8.5 %copy-start.3 = (bf16[1,64,64,64]{3,2,1,0:T(8,128)(2,1)S(1)}, bf16[1,64,64,64]{3,2,1,0:T(8,128)(2,1)}, u32[]{:S(2)}) copy-start(bf16[1,64,64,64]{3,2,1,0:T(8,128)(2,1)} %param.14) | copy-start | bytes 1572868
  10.3 33.0 %all-to-all-start.1 = ((bf16[16,8,4096]{2,1,0:T(8,128)(2,1)}), bf16[16,8,4096]{2,1,0:T(8,128)(2,1)S(1)}, u32[]{:S(2)}, u32[]{:S(2)}) async-start(bf16[16,8,4096]{2,1,0:T(8,128)(2,1)} %bitcast.38), calls=%async_computation.1 | async-start | bytes 2097152 | tf_op jit(solution)/shard_map/all_to_all | solution.py:327
  18.7 2.7 %collective-permute-start.3 = (bf16[64,64,64]{2,1,0:T(8,128)(2,1)S(1)}, bf16[64,64,64]{2,1,0:T(8,128)(2,1)S(1)}, u32[]{:S(2)}, u32[]{:S(2)}) collective-permute-start(bf16[64,64,64]{2,1,0:T(8,128)(2,1)S(1)} %bitcast.32), channel_id=1, source_target_pairs={{0,1},{1,0},{2,3},{3,2},{4,5},{5,4},{6,7},{7,6},{8,9},{9,8},{10,11... | collective-permute-start | bytes 1572872 | tf_op jit(solution)/shard_map/ppermute | solution.py:318
  18.8 4.1 %collective-permute-start.4 = (bf16[64,64,64]{2,1,0:T(8,128)(2,1)S(1)}, bf16[64,64,64]{2,1,0:T(8,128)(2,1)S(1)}, u32[]{:S(2)}, u32[]{:S(2)}) collective-permute-start(bf16[64,64,64]{2,1,0:T(8,128)(2,1)S(1)} %bitcast.35), channel_id=1, source_target_pairs={{0,1},{1,0},{2,3},{3,2},{4,5},{5,4},{6,7},{7,6},{8,9},{9,8},{10,11... | collective-permute-start | bytes 1572872 | tf_op jit(solution)/shard_map/ppermute | solution.py:318
  19.3 9.7 %collective-permute-start.2 = (bf16[128,128]{1,0:T(8,128)(2,1)S(1)}, bf16[128,128]{1,0:T(8,128)(2,1)S(1)}, u32[]{:S(2)}, u32[]{:S(2)}) collective-permute-start(bf16[128,128]{1,0:T(8,128)(2,1)S(1)} %bitcast.54), channel_id=1, source_target_pairs={{0,1},{1,0},{2,3},{3,2},{4,5},{5,4},{6,7},{7,6},{8,9},{9,8},{10,11... | collective-permute-start | bytes 98312 | tf_op jit(solution)/shard_map/ppermute | solution.py:318
  21.4 1.5 copy-start.4
  22.9 1.0 copy-start.5
  28.9 0.6 copy-start.24
  43.3 6.1 %copy-start.11 = (bf16[16,8,4096]{2,1,0:T(8,128)(2,1)}, bf16[16,8,4096]{2,1,0:T(8,128)(2,1)S(1)}, u32[]{:S(2)}) copy-start(bf16[16,8,4096]{2,1,0:T(8,128)(2,1)S(1)} %all-to-all-done.1) | copy-start | bytes 3145732
  43.3 29.4 %all-to-all-start = ((bf16[16,8,4096]{2,1,0:T(8,128)(2,1)}), bf16[16,8,4096]{2,1,0:T(8,128)(2,1)S(1)}, u32[]{:S(2)}, u32[]{:S(2)}) async-start(bf16[16,8,4096]{2,1,0:T(8,128)(2,1)} %bitcast.46), calls=%async_computation | async-start | bytes 2097152 | tf_op jit(solution)/shard_map/all_to_all | solution.py:327
  72.7 10.9 %copy-start.7 = (bf16[16,8,4096]{2,1,0:T(8,128)(2,1)}, bf16[16,8,4096]{2,1,0:T(8,128)(2,1)S(1)}, u32[]{:S(2)}) copy-start(bf16[16,8,4096]{2,1,0:T(8,128)(2,1)S(1)} %all-to-all-done) | copy-start | bytes 3145732
  72.7 28.8 %all-to-all-start.3 = ((bf16[16,8,4096]{2,1,0:T(8,128)(2,1)}), bf16[16,8,4096]{2,1,0:T(8,128)(2,1)S(1)}, u32[]{:S(2)}, u32[]{:S(2)}) async-start(bf16[16,8,4096]{2,1,0:T(8,128)(2,1)} %bitcast.45), calls=%async_computation.3 | async-start | bytes 2097152 | tf_op jit(solution)/shard_map/all_to_all | solution.py:327
  94.9 12.5 %copy-start.12 = (bf16[2048,128]{1,0:T(8,128)(2,1)S(1)}, bf16[2048,128]{1,0:T(8,128)(2,1)}, u32[]{:S(2)}) copy-start(bf16[2048,128]{1,0:T(8,128)(2,1)} %get-tuple-element.78) | copy-start | bytes 1572868
  94.9 12.5 %copy-start.13 = (bf16[2048,128]{1,0:T(8,128)(2,1)S(1)}, bf16[2048,128]{1,0:T(8,128)(2,1)}, u32[]{:S(2)}) copy-start(bf16[2048,128]{1,0:T(8,128)(2,1)} %get-tuple-element.79) | copy-start | bytes 1572868
  101.4 6.2 %copy-start.6 = (bf16[16,8,4096]{2,1,0:T(8,128)(2,1)}, bf16[16,8,4096]{2,1,0:T(8,128)(2,1)S(1)}, u32[]{:S(2)}) copy-start(bf16[16,8,4096]{2,1,0:T(8,128)(2,1)S(1)} %all-to-all-done.3) | copy-start | bytes 3145732
  101.4 28.9 %all-to-all-start.2 = ((bf16[16,8,4096]{2,1,0:T(8,128)(2,1)}), bf16[16,8,4096]{2,1,0:T(8,128)(2,1)S(1)}, u32[]{:S(2)}, u32[]{:S(2)}) async-start(bf16[16,8,4096]{2,1,0:T(8,128)(2,1)} %bitcast.44), calls=%async_computation.2 | async-start | bytes 2097152 | tf_op jit(solution)/shard_map/all_to_all | solution.py:327
  107.6 9.6 %collective-permute-start.9 = (bf16[2048,128]{1,0:T(8,128)(2,1)S(1)}, bf16[2048,128]{1,0:T(8,128)(2,1)S(1)}, u32[]{:S(2)}, u32[]{:S(2)}) collective-permute-start(bf16[2048,128]{1,0:T(8,128)(2,1)S(1)} %broadcast_select_fusion.1), channel_id=1, source_target_pairs={{0,1},{1,0},{2,3},{3,2},{4,5},{5,4},{6,7},{7,6},{8,9},{9,8},{10,11... | collective-permute-start | bytes 1572872 | tf_op jit(solution)/shard_map/ppermute | solution.py:318
  115.3 3.3 %copy-start.14 = (bf16[2048,128]{1,0:T(8,128)(2,1)S(1)}, bf16[2048,128]{1,0:T(8,128)(2,1)}, u32[]{:S(2)}) copy-start(bf16[2048,128]{1,0:T(8,128)(2,1)} %get-tuple-element.76) | copy-start | bytes 1572868
  115.3 3.3 %copy-start.15 = (bf16[2048,128]{1,0:T(8,128)(2,1)S(1)}, bf16[2048,128]{1,0:T(8,128)(2,1)}, u32[]{:S(2)}) copy-start(bf16[2048,128]{1,0:T(8,128)(2,1)} %get-tuple-element.77) | copy-start | bytes 1572868
  116.5 2.1 %collective-permute-start.8 = (bf16[2048,128]{1,0:T(8,128)(2,1)S(1)}, bf16[2048,128]{1,0:T(8,128)(2,1)S(1)}, u32[]{:S(2)}, u32[]{:S(2)}) collective-permute-start(bf16[2048,128]{1,0:T(8,128)(2,1)S(1)} %broadcast_select_fusion.2), channel_id=1, source_target_pairs={{0,1},{1,0},{2,3},{3,2},{4,5},{5,4},{6,7},{7,6},{8,9},{9,8},{10,11... | collective-permute-start | bytes 1572872 | tf_op jit(solution)/shard_map/ppermute | solution.py:318
  130.3 34.8 %copy-start.9 = (bf16[16,8,4096]{2,1,0:T(8,128)(2,1)}, bf16[16,8,4096]{2,1,0:T(8,128)(2,1)S(1)}, u32[]{:S(2)}) copy-start(bf16[16,8,4096]{2,1,0:T(8,128)(2,1)S(1)} %all-to-all-done.2) | copy-start | bytes 3145732
  165.1 26.8 %all-to-all-start.5 = ((bf16[16,2,128,128]{3,2,1,0:T(8,128)(2,1)}), bf16[16,2,128,128]{3,2,1,0:T(8,128)(2,1)S(1)}, u32[]{:S(2)}, u32[]{:S(2)}) async-start(bf16[16,2,128,128]{3,2,1,0:T(8,128)(2,1)} %broadcast_in_dim.17), calls=%async_computation.5 | async-start | bytes 2097152 | tf_op jit(solution)/shard_map/all_to_all | solution.py:482
  169.0 4.9 %copy-start = (bf16[128,4096]{1,0:T(8,128)(2,1)S(1)}, bf16[128,4096]{1,0:T(8,128)(2,1)}, u32[]{:S(2)}) copy-start(bf16[128,4096]{1,0:T(8,128)(2,1)} %get-tuple-element.62.upstream) | copy-start | bytes 3145732
  174.0 1.2 copy-start.20
  174.0 1.2 copy-start.21
  174.0 1.7 copy-start.19
  174.0 1.7 copy-start.22
  174.0 18.9 %copy-start.10 = (bf16[128,4096]{1,0:T(8,128)(2,1)S(1)}, bf16[128,4096]{1,0:T(8,128)(2,1)}, u32[]{:S(2)}) copy-start(bf16[128,4096]{1,0:T(8,128)(2,1)} %get-tuple-element.70) | copy-start | bytes 3145732
  175.1 17.8 %collective-permute-start.5 = (bf16[128,4096]{1,0:T(8,128)(2,1)}, bf16[128,4096]{1,0:T(8,128)(2,1)}, u32[]{:S(2)}, u32[]{:S(2)}) collective-permute-start(bf16[128,4096]{1,0:T(8,128)(2,1)} %broadcast_select_fusion), channel_id=1, source_target_pairs={{0,1},{1,0},{2,3},{3,2},{4,5},{5,4},{6,7},{7,6},{8,9},{9,8},{10,11... | collective-permute-start | bytes 3145736 | tf_op jit(solution)/shard_map/ppermute | solution.py:318
  175.1 2.4 %collective-permute-start.7 = (f32[128,16]{1,0:T(8,128)S(1)}, f32[128,16]{1,0:T(8,128)S(1)}, u32[]{:S(2)}, u32[]{:S(2)}) collective-permute-start(f32[128,16]{1,0:T(8,128)S(1)} %broadcast_select_fusion.3), channel_id=1, source_target_pairs={{0,1},{1,0},{2,3},{3,2},{4,5},{5,4},{6,7},{7,6},{8,9},{9,8},{10,11... | collective-permute-start | bytes 24584 | tf_op jit(solution)/shard_map/ppermute | solution.py:318
  175.7 16.3 %collective-permute-start.6 = (f32[128,128]{1,0:T(8,128)S(1)}, f32[128,128]{1,0:T(8,128)S(1)}, u32[]{:S(2)}, u32[]{:S(2)}) collective-permute-start(f32[128,128]{1,0:T(8,128)S(1)} %broadcast_select_fusion.4), channel_id=1, source_target_pairs={{0,1},{1,0},{2,3},{3,2},{4,5},{5,4},{6,7},{7,6},{8,9},{9,8},{10,11... | collective-permute-start | bytes 196616 | tf_op jit(solution)/shard_map/ppermute | solution.py:318
  191.9 4.2 %copy-start.1 = (bf16[16,2,128,128]{3,2,1,0:T(8,128)(2,1)}, bf16[16,2,128,128]{3,2,1,0:T(8,128)(2,1)S(1)}, u32[]{:S(2)}) copy-start(bf16[16,2,128,128]{3,2,1,0:T(8,128)(2,1)S(1)} %all-to-all-done.5.kept) | copy-start | bytes 3145732
  192.0 4.1 %collective-permute-start.10 = (bf16[16,1,128,128]{3,2,1,0:T(8,128)(2,1)S(1)}, bf16[16,1,128,128]{3,2,1,0:T(8,128)(2,1)S(1)}, u32[]{:S(2)}, u32[]{:S(2)}) collective-permute-start(bf16[16,1,128,128]{3,2,1,0:T(8,128)(2,1)S(1)} %constant_dynamic-slice_fusion), channel_id=1, source_target_pairs={{0,1},{1,0},{2,3},{3,2},{4,5},{5,4},{6,7},{7,6},{8,9},{9,8},{10,11... | collective-permute-start | bytes 1572872 | tf_op jit(solution)/shard_map/ppermute | solution.py:318
  196.1 0.8 copy-start.16

commit v2 on v1

--- a/solution.py
+++ b/solution.py
@@ -22,11 +22,11 @@
     return pl.BlockSpec(shape, lambda *_: (0,) * len(shape))
 
 
-def call(kernel, name, out_shape, grid, in_specs, out_specs, scratch=()):
-    params = pltpu.CompilerParams(vmem_limit_bytes=56 * 1024 * 1024)
+def call(kernel, name, out_shape, grid, in_specs, out_specs, scratch=(), scalars=0):
+    params = pltpu.CompilerParams(vmem_limit_bytes=62 * 1024 * 1024)
     estimate = pl.CostEstimate(flops=1 << 28, bytes_accessed=8 << 20, transcendentals=0)
     spec = pltpu.PrefetchScalarGridSpec(
-        num_scalar_prefetch=1, grid=grid, in_specs=in_specs, out_specs=out_specs, scratch_shapes=scratch
+        num_scalar_prefetch=scalars, grid=grid, in_specs=in_specs, out_specs=out_specs, scratch_shapes=scratch
     )
     return pl.pallas_call(
         kernel, out_shape=out_shape, grid_spec=spec, compiler_params=params, cost_estimate=estimate, name=name
@@ -57,6 +57,14 @@
 def diagonal(product):
     lane = lax.broadcasted_iota(jnp.int32, (64, 128), 1)
     return jnp.where(lane < 64, product[:64], product[64:])
+
+
+def store(grads, part, q, value):
+    rows = grads.shape[2]
+    piece = min(rows, 64)
+    for first in range(0, 64, piece):
+        owner, at = divmod(64 * q + first, rows)
+        grads[owner, part, at : at + piece, :] = value[first : first + piece].astype(grads.dtype)
 
 
 def spread(left, onehot, mask):
@@ -101,6 +109,11 @@
     recv,
     right_own,
     right_other,
+    upstream,
+    left_own,
+    left_other,
+    onehot,
+    mask,
     first_bd,
     second_bd,
     eye,
@@ -109,13 +122,24 @@
     right_act,
     act_0,
     act_1,
+    gate,
     right_t_1,
     right_t_0,
     right_0,
+    full_1,
+    full_0,
+    turned_0,
     wide,
 ):
     act_0[...] = pick(p, keep[0], recv[...]).astype(BF)
-    act_1[...] = pick(p, recv[...], keep[0]).astype(BF)
+    act = pick(p, recv[...], keep[0])
+    act_1[...] = act.astype(BF)
+    gate[...] = (upstream[0].astype(F32) * act).astype(BF)
+    left_0 = pick(p, left_own[...], left_other[...]).astype(BF)
+    left_1 = pick(p, left_other[...], left_own[...]).astype(BF)
+    full_1[...] = spread(left_1, onehot[...], mask[...])
+    full_0[...] = spread(left_0, onehot[...], mask[...])
+    turned_0[...] = spread_turned(left_0, onehot[...], mask[...])
     low = pick(p, right_own[...], right_other[...]).astype(BF)
     high = pick(p, right_other[...], right_own[...]).astype(BF)
     right_0[...] = low
@@ -133,7 +157,6 @@
 
 
 def middle_kernel(
-    p,
     back,
     second_bt,
     first_bt,
@@ -146,8 +169,7 @@
     right_act_low,
     chan_back,
     right_grad,
-    first_grad,
-    second_grad,
+    grads,
     wide,
     turned,
 ):
@@ -155,10 +177,10 @@
     pairs = first_bt.shape[0]
     for q in range(pairs):
         wide[columns(q), :] = mm(second_bt[q], back[:, columns(q)], NT)
-        second_grad[half(q), :] = diagonal(mm(mixed[columns(q), :], back[:, columns(q)]).T).astype(BF)
+        store(grads, 1, q, diagonal(mm(mixed[columns(q), :], back[:, columns(q)]).T))
     for q in range(pairs):
         pair = regroup(wide, q, 2 * pairs)
-        first_grad[half(q), :] = diagonal(mm(pair, right_act[:, columns(q)])).astype(BF)
+        store(grads, 0, q, diagonal(mm(pair, right_act[:, columns(q)])))
         piece = mm(first_bt[q], pair).astype(BF)
         turned[columns(q), :] = piece
         chan_back[:, columns(q)] = mm(right_t[...], piece, NT)
@@ -166,14 +188,13 @@
 
 
 def turn_kernel(
-    p,
     rows,
     upstream,
-    act,
+    gate_high,
     chan_back,
     act_low,
-    left_own,
-    left_other,
+    left,
+    left_t_low,
     second_bt,
     first_bt,
     eye,
@@ -187,24 +208,15 @@
     sent,
     wide,
     left_acc,
-    left,
-    left_t_low,
 ):
     step = pl.program_id(0)
     steps = pl.num_programs(0)
     pairs = second_bt.shape[0]
 
-    @pl.when(step == 0)
-    def _():
-        left[...] = spread(pick(p, left_other[...], left_own[...]).astype(BF), onehot[...], mask[...])
-        left_t_low[...] = spread_turned(pick(p, left_own[...], left_other[...]).astype(BF), onehot[...], mask[...])
-
-    gy = upstream[0].astype(F32)
     carried = mm(left[...], rows[...])
-    incoming = (gy * carried + chan_back[...]).astype(BF)
+    incoming = (upstream[...].astype(F32) * carried + chan_back[...]).astype(BF)
     input_grad[...] = incoming
-    gate = (gy * act[...].astype(F32)).astype(BF)
-    term = mm(gate, rows[...], NT)
+    term = mm(gate_high[...], rows[...], NT)
 
     @pl.when(step == 0)
     def _():
@@ -235,12 +247,10 @@
 
 
 def lower_kernel(
-    p,
     rows,
     first_bd,
     second_bd,
-    left_own,
-    left_other,
+    left,
     gate,
     back,
     mixed_grad,
@@ -248,27 +258,25 @@
     mask,
     carried,
     left_grad,
-    first_grad,
-    second_grad,
+    grads,
     wide,
     turned,
 ):
     pairs = first_bd.shape[0]
-    left = spread(pick(p, left_own[...], left_other[...]).astype(BF), onehot[...], mask[...])
     for q in range(pairs):
         wide[columns(q), :] = mm(first_bd[q], rows[:, columns(q)], NT)
-        first_grad[half(q), :] = diagonal(mm(mixed_grad[columns(q), :], rows[:, columns(q)])).astype(BF)
+        store(grads, 0, q, diagonal(mm(mixed_grad[columns(q), :], rows[:, columns(q)])))
     for q in range(pairs):
         pair = regroup(wide, q, 2 * pairs)
-        second_grad[half(q), :] = diagonal(mm(pair, back[:, columns(q)]).T).astype(BF)
+        store(grads, 1, q, diagonal(mm(pair, back[:, columns(q)]).T))
         hidden = mm(second_bd[q], pair).astype(BF)
         turned[columns(q), :] = hidden
-        carried[:, columns(q)] = mm(left, hidden, NT)
+        carried[:, columns(q)] = mm(left[...], hidden, NT)
     term = mm(gate[...], turned[...])
     left_grad[...] = mm(term * mask[...].astype(F32), onehot[...].astype(F32), precision=lax.Precision.HIGHEST)
 
 
-def last_kernel(p, received, right_t, upstream, carried, act, input_grad, right_grad):
+def last_kernel(received, right_t, upstream, carried, act, input_grad, right_grad):
     step = pl.program_id(0)
     chan_back = mm(right_t[...], received[...])
     input_grad[...] = (upstream[...].astype(F32) * carried[...] + chan_back).astype(BF)
@@ -283,35 +291,26 @@
         right_grad[...] += term
 
 
-def total_kernel(p, pieces, out):
+def total_kernel(pieces, out):
     total = pieces[0].astype(F32)
     for i in range(1, pieces.shape[0]):
         total += pieces[i].astype(F32)
     out[...] = total.astype(BF)
 
 
-def unpack_kernel(p, kept, came, first, second):
+def spread_kernel(*refs):
+    total = sum(ref[...].astype(F32) for ref in refs[:-1]).astype(BF)
+    for i in range(refs[-1].shape[0]):
+        refs[-1][i] = total
+
+
+def unpack_kernel(sums, first, second):
     side = first.shape[1]
-
-    def unpack(array, out):
-        for q in range(first.shape[0] // 2):
-            parts = []
-            for row in range(64 * q, 64 * (q + 1), min(64, array.shape[2])):
-                owner, at = divmod(row, array.shape[2])
-                parts.append(array[owner, 0, at : at + min(64, array.shape[2]), :].astype(F32))
-            value = jnp.concatenate(parts, axis=0) if len(parts) > 1 else parts[0]
-            out[2 * q] = value[:, :side]
-            out[2 * q + 1] = value[:, side:]
-
-    @pl.when(p[0] == 0)
-    def _():
-        unpack(kept, first)
-        unpack(came, second)
-
-    @pl.when(p[0] != 0)
-    def _():
-        unpack(kept, second)
-        unpack(came, first)
+    for part, out in enumerate((first, second)):
+        block = sums[:, part].astype(F32).reshape(-1, 2 * side)
+        for q in range(out.shape[0] // 2):
+            out[2 * q] = block[half(q), :side]
+            out[2 * q + 1] = block[half(q), side:]
 
 
 def swap(value):
@@ -325,6 +324,23 @@
 def exchange(rows, devices):
     chunks = rows.reshape(devices, rows.shape[0] // devices, *rows.shape[1:])
     return lax.all_to_all(chunks, "blk", split_axis=0, concat_axis=0, tiled=True).reshape(rows.shape)
+
+
+def summed(parts, devices):
+    far = 12 if devices == 16 else 0
+    members = devices // 2 if far else devices
+    groups = [[member ^ f for member in range(members)] for f in ((0, far) if far else (0,))]
+    shape = (members, devices // members * parts.shape[1]) + parts.shape[2:]
+
+    def exchanged(value):
+        return lax.all_to_all(value, "blk", split_axis=0, concat_axis=0, axis_index_groups=groups, tiled=True)
+
+    pieces = exchanged(parts.reshape(shape))
+    terms = [call(total_kernel, "total", sds(shape[1:], BF), (1,), [whole(shape)], whole(shape[1:]))(pieces)]
+    if far:
+        terms.append(lax.ppermute(terms[0], "blk", [(i, i ^ far) for i in range(devices)]))
+    share = [whole(shape[1:])] * len(terms)
+    return exchanged(call(spread_kernel, "spread", sds(shape, BF), (1,), share, whole(shape))(*terms)).reshape(parts.shape)
 
 
 def body(x_saved, cotangent, seq_right, seq_left, chan_first, chan_second):
@@ -359,8 +375,8 @@
     act_shape = (tokens, width)
     col_shape = (width, tokens)
     pair_shape = (pairs, 2 * side, 2 * side)
-    grad_shape = (pairs * side, 2 * side)
-    act_full, col_full, pair_full, grad_full = map(whole, (act_shape, col_shape, pair_shape, grad_shape))
+    owned = (devices, 2, pairs * side // devices, 2 * side)
+    act_full, col_full, pair_full = map(whole, (act_shape, col_shape, pair_shape))
     chosen_full = pl.BlockSpec((1,) + act_shape, lambda i, p: (p[0], 0, 0))
     box = whole((blocks, side, side))
     squared = sds((tokens, tokens), BF)
@@ -373,6 +389,7 @@
         [chosen, moving, chosen, narrow, narrow, narrow, square],
         moving,
         [pltpu.VMEM((tokens, tokens), BF)],
+        scalars=1,
     )(p, saved, received, cotangent, left_own, left_other, onehot, mask)
     returned_1 = exchange(back_1, devices)
     p = after(p, back_1)
@@ -385,38 +402,48 @@
             (1,),
             [box] * 4,
             [pair_full] * 4,
+            scalars=1,
         )(p, first_own, first_other, second_own, second_other)
 
     fbd_1, fbt_1, sbd_1, sbt_1 = expand(p, 1)
-    rows_1, mixed_1, right_act_1, act_0, act_1, right_t_1, right_t_0, right_0 = call(
+    rows_1, mixed_1, right_act_1, act_0, act_1, gate_1, right_t_1, right_t_0, right_0, full_1, full_0, turned_0 = call(
         forward_kernel,
         "forward",
-        [sds(act_shape, BF), sds(col_shape, BF)] + [sds(act_shape, BF)] * 3 + [squared] * 3,
+        [sds(act_shape, BF), sds(col_shape, BF)] + [sds(act_shape, BF)] * 4 + [squared] * 6,
         (1,),
-        [chosen_full, act_full, square, square, pair_full, pair_full, square],
-        [act_full, col_full] + [act_full] * 3 + [square] * 3,
+        [chosen_full, act_full, square, square, chosen_full, narrow, narrow, narrow, square, pair_full, pair_full, square],
+        [act_full, col_full] + [act_full] * 4 + [square] * 6,
         [pltpu.VMEM(col_shape, F32)],
-    )(p, saved, received, right_own, right_other, fbd_1, sbd_1, eye)
+        scalars=1,
+    )(
+        p,
+        saved,
+        received,
+        right_own,
+        right_other,
+        cotangent,
+        left_own,
+        left_other,
+        onehot,
+        mask,
+        fbd_1,
+        sbd_1,
+        eye,
+    )
     gathered_1 = exchange(rows_1, devices)
     p = after(p, rows_1)
     fbd_0, fbt_0, sbd_0, sbt_0 = expand(p, 0)
 
-    right_act_0, chan_back_1, right_grad_1, first_1, second_1 = call(
+    right_act_0, chan_back_1, right_grad_1, grads_1 = call(
         middle_kernel,
         "middle",
-        [sds(act_shape, BF), sds(act_shape, F32), sds((span, span), F32)] + [sds(grad_shape, BF)] * 2,
+        [sds(act_shape, BF), sds(act_shape, F32), sds((span, span), F32), sds(owned, BF)],
         (1,),
         [act_full, pair_full, pair_full, col_full, act_full, square, act_full, square, act_full],
-        [act_full, act_full, square, grad_full, grad_full],
+        [act_full, act_full, square, whole(owned)],
         [pltpu.VMEM(col_shape, F32), pltpu.VMEM(col_shape, BF)],
-    )(p, returned_1, sbt_1, fbt_1, mixed_1, right_act_1, right_t_1, act_1, right_0, act_0)
+    )(returned_1, sbt_1, fbt_1, mixed_1, right_act_1, right_t_1, act_1, right_0, act_0)
     gathered_0 = exchange(right_act_0, devices)
-
-    def over_cores(first, second):
-        came = swap(jnp.where(core == 0, second, first)).astype(F32)
-        return (jnp.where(core == 0, first, second).astype(F32) + came).astype(BF)
-
-    part_1 = over_cores(first_1, second_1)
 
     input_1, left_grad_1, gate_0, back_0, mixed_grad_0, sent_0 = call(
         turn_kernel,
@@ -432,29 +459,28 @@
         (width // step,),
         [
             moving,
-            chosen,
             moving,
             moving,
             moving,
-            narrow,
-            narrow,
-            pl.BlockSpec((step // (2 * side), 2 * side, 2 * side), lambda i, *_: (i, 0, 0)),
+            moving,
+            square,
+            square,
+            pl.BlockSpec((step // (2 * side), 2 * side, 2 * side), lambda i: (i, 0, 0)),
             pair_full,
             square,
             narrow,
             square,
         ],
         [moving, narrow, moving, moving, col_full, act_full],
-        [pltpu.VMEM(col_shape, F32), pltpu.VMEM((tokens, tokens), F32)] + [pltpu.VMEM((tokens, tokens), BF)] * 2,
+        [pltpu.VMEM(col_shape, F32), pltpu.VMEM((tokens, tokens), F32)],
     )(
-        p,
         gathered_1,
-        cotangent,
-        act_1,
+        lax.dynamic_index_in_dim(cotangent, core, 0, keepdims=False),
+        gate_1,
         chan_back_1,
         act_0,
-        left_own,
-        left_other,
+        full_1,
+        turned_0,
         sbt_0,
         fbt_0,
         eye,
@@ -463,24 +489,20 @@
     )
     returned_0 = exchange(sent_0, devices)
 
-    carried_0, left_grad_0, first_0, second_0 = call(
+
+    carried_0, left_grad_0, grads_0 = call(
         lower_kernel,
         "lower",
-        [sds(act_shape, F32), sds((tokens, count), F32)] + [sds(grad_shape, BF)] * 2,
+        [sds(act_shape, F32), sds((tokens, count), F32), sds(owned, BF)],
         (1,),
-        [act_full, pair_full, pair_full, narrow, narrow, act_full, act_full, col_full, narrow, square],
-        [act_full, narrow, grad_full, grad_full],
+        [act_full, pair_full, pair_full, square, act_full, act_full, col_full, narrow, square],
+        [act_full, narrow, whole(owned)],
         [pltpu.VMEM(col_shape, F32), pltpu.VMEM(col_shape, BF)],
-    )(p, gathered_0, fbd_0, sbd_0, left_own, left_other, gate_0, back_0, mixed_grad_0, onehot, mask)
-
-    parts = jnp.stack([over_cores(first_0, second_0), part_1]).reshape(2, devices, -1, 2 * side).swapaxes(0, 1)
-    pieces = lax.all_to_all(after(parts, returned_0), "blk", split_axis=0, concat_axis=0, tiled=True)
-    own = call(
-        total_kernel, "total", sds(pieces.shape[1:], BF), (1,), [whole(pieces.shape)], whole(pieces.shape[1:])
-    )(p, pieces)
-    everyone = jnp.broadcast_to(own[None], (devices,) + own.shape)
-    sums = lax.all_to_all(everyone, "blk", split_axis=0, concat_axis=0, tiled=True)
-    sums_came = swap(lax.dynamic_slice_in_dim(sums, 1 - core, 1, axis=1))
+    )(gathered_0, fbd_0, sbd_0, full_0, gate_0, back_0, mixed_grad_0, onehot, mask)
+
+    own = jnp.where(core == 0, grads_0, grads_1).astype(F32)
+    parts = (own + swap(jnp.where(core == 0, grads_1, grads_0)).astype(F32)).astype(BF)
+    sums = summed(after(parts, returned_0), devices)
 
     input_0, right_grad_0 = call(
         last_kernel,
@@ -489,25 +511,25 @@
         (width // step,),
         [moving, square, moving, moving, moving],
         [moving, square],
-    )(p, returned_0, right_t_0, input_1, carried_0, act_0)
+    )(returned_0, right_t_0, input_1, carried_0, act_0)
 
     def to_section(low, high):
         return jnp.where(core == 0, low, high) + swap(jnp.where(core == 0, high, low))
 
-    came = swap(jnp.where(core == 0, input_1, input_0))
-    input_grad = jnp.where(core == 0, jnp.stack([input_0, came]), jnp.stack([came, input_1]))
     left_grad = to_section(left_grad_0, left_grad_1).reshape(per, count, count)
     right_grad = to_section(right_grad_0, right_grad_1)
-    p = after(p, input_grad, left_grad, right_grad)
-    part = (sums.shape[0], 1) + sums.shape[2:]
+    input_grad = jnp.where(
+        core == 0, jnp.stack([input_0, swap(input_0)]), jnp.stack([swap(input_1), input_1])
+    )
+    parts = 4
     first_grad, second_grad = call(
         unpack_kernel,
         "unpack",
         [sds((blocks, side, side), F32)] * 2,
-        (1,),
-        [pl.BlockSpec(part, lambda i, p: (0, p[0], 0, 0)), whole(part)],
-        [box] * 2,
-    )(p, sums, sums_came)
+        (parts,),
+        [pl.BlockSpec((devices // parts,) + owned[1:], lambda i: (i, 0, 0, 0))],
+        [pl.BlockSpec((blocks // parts, side, side), lambda i: (i, 0, 0))] * 2,
+    )(after(sums, input_grad, left_grad, right_grad))
     return (
         input_grad[None],
         right_grad[None, None],

time: 202 us -> 185 us (0.916)
  blocking collectives: 30.8 us -> 18.9 us
  waiting for transfers between devices: 61.5 us -> 52 us
  Pallas kernels: 60 us -> 63.3 us
  starting transfers between devices: 32.8 us -> 35.1 us
    all_to_all x1, waiting for transfers between devices: 13.8 us -> 0.01 us  [exchanged(): lax.all_to_all(value, 'blk', split_axis=0, concat_axis=0, axis_index_grou...]
    all_to_all x1, blocking collectives: 30.8 us -> 18.9 us  [exchanged(): lax.all_to_all(value, 'blk', split_axis=0, concat_axis=0, axis_index_grou...]
    ppermute x0 -> x1, waiting for transfers between devices: none -> 5.17 us  [summed(): lax.ppermute(terms[0], 'blk', [(i, i ^ far) for i in range(devices)])]
    pallas_call x2 -> x3, Pallas kernels: 5.56 us -> 8.1 us  [the longest x1 4.07 us: body(): call(unpack_kernel, 'unpack', [sds((blocks, side, side), F32)] * 2, (part...]
    broadcast_in_dim x1 -> x0, local copies, waits for them, and re-layouts: 2.05 us -> none  [body(): everyone = jnp.broadcast_to(own[None], (devices,) + own.shape)]
    select_n x4 -> x2, other arithmetic: 5.57 us -> 3.65 us  [the longest x1 3.54 us: body(): jnp.where(core == 0, jnp.stack([input_0, swap(input_0)]), jnp.stack([swap...]
    unnamed x50 -> x36, local copies, waits for them, and re-layouts: 3.43 us -> 5.23 us
    ppermute x11 -> x10, waiting for transfers between devices: 8.81 us -> 8.54 us  [swap(): return lax.ppermute(value, 'pipe', [(0, 1), (1, 0)])]
  transfers between devices with their start and end apart: 16 -> 16, of which waited for: 10 -> 10; matrix products, arithmetic and copies ran while one was open for 4% -> 4% of each run, Pallas kernels for 25% -> 28%
where the time goes in v2:
time: 185 us; the launch traced here: 184 us
  Pallas kernels  63.3 us (34%)
  waiting for transfers between devices  52 us (28%)
  starting transfers between devices  35.1 us (19%)
  blocking collectives  18.9 us (10%)
  local copies, waits for them, and re-layouts  7.64 us (4%)
  other arithmetic  6.3 us (3%)
    all_to_all x4, waiting for transfers between devices, exchange(): lax.all_to_all(chunks, 'blk', split_axis=0, concat_axis=0, tiled=True)  38.3 us
    all_to_all x4, starting transfers between devices, exchange(): lax.all_to_all(chunks, 'blk', split_axis=0, concat_axis=0, tiled=True)  26.4 us
    all_to_all x1, blocking collectives, exchanged(): lax.all_to_all(value, 'blk', split_axis=0, concat_axis=0, axis_index_grou...  18.9 us
    pallas_call x1, Pallas kernels, body(): call(turn_kernel, 'turn', [sds(act_shape, BF), sds((tokens, count), F32),...  11.1 us
    pallas_call x2, Pallas kernels, expand(): call(functools.partial(expand_kernel, section), 'expand', [sds(pair_shape...  10.1 us
    pallas_call x1, Pallas kernels, body(): call(forward_kernel, 'forward', [sds(act_shape, BF), sds(col_shape, BF)]...  9 us
    ppermute x10, waiting for transfers between devices, swap(): return lax.ppermute(value, 'pipe', [(0, 1), (1, 0)])  8.54 us
    pallas_call x1, Pallas kernels, body(): call(middle_kernel, 'middle', [sds(act_shape, BF), sds(act_shape, F32), s...  7.99 us
  transfers between devices with their start and end apart: 16, of which 10 were waited for; matrix products, arithmetic and copies ran while one was open for 4% of the time, Pallas kernels for 28%

profile of v2, /device:TPU:0, one launch (start us, length us, event | category | flops | bytes accessed | tf_op | source)
XLA Modules:
  0.0 184.1 jit_solution(2566442578596571570)
XLA Ops:
  0.6 0.0 copy-start.13
  0.6 1.3 dynamic-slice_bitcast_fusion.1
  1.9 0.5 collective-permute-start
  2.5 0.0 copy-done.13
  2.5 0.1 collective-permute-start.1
  2.6 2.2 %collective-permute-done.1.left_other = bf16[128,16]{1,0:T(8,128)(2,1)S(1)} collective-permute-done((bf16[128,16]{1,0:T(8,128)(2,1)S(1)}, bf16[128,16]{1,0:T(8,128)(2,1)S(1)}, u32[]{:S(2)}, u32[]{:S(2)}) %collective-permute-start.1) | collective-permute-done | bytes 4128 | tf_op jit(solution)/shard_map/ppermute | solution.py:317
  4.8 0.0 collective-permute-done.recv
  4.8 0.6 copy-done.14
  5.4 0.4 copy-done.8
  5.8 4.5 %gate.1 = bf16[128,4096]{1,0:T(8,128)(2,1)} custom-call(s32[1]{0:T(128)} %bitcast.p, bf16[2,128,4096]{2,1,0:T(8,128)(2,1)} %bitcast.28, bf16[128,4096]{1,0:T(8,128)(2,1)} %copy-done.8, bf16[2,128,4096]{2,1,0:T(8,128)(2,1)} %upstream.3, bf16[128,16]{1,0:T(8,128)(2,1)} %bitcast.46, bf16[128,16]{1,0:T(8,128)(2,1)} %copy-done.14, ...), custom_call_target="tpu_custom_call" | custom-call | flops 268435456 | bytes 8388608 | tf_op jit(solution)/shard_map/gate/pallas_call | solution.py:384
  10.3 8.4 %all-to-all-start.1 = ((bf16[16,8,4096]{2,1,0:T(8,128)(2,1)}), bf16[16,8,4096]{2,1,0:T(8,128)(2,1)}, u32[]{:S(2)}, u32[]{:S(2)}) async-start(bf16[16,8,4096]{2,1,0:T(8,128)(2,1)} %bitcast.37), calls=%async_computation.1 | async-start | bytes 2097152 | tf_op jit(solution)/shard_map/all_to_all | solution.py:326
  18.7 0.1 collective-permute-start.3
  18.8 0.0 copy-done.2
  18.8 0.5 collective-permute-start.4
  19.3 0.0 copy-done.16
  19.3 0.1 collective-permute-start.2
  19.4 2.7 %collective-permute-done.3.first_other = bf16[64,64,64]{2,1,0:T(8,128)(2,1)S(1)} collective-permute-done((bf16[64,64,64]{2,1,0:T(8,128)(2,1)S(1)}, bf16[64,64,64]{2,1,0:T(8,128)(2,1)S(1)}, u32[]{:S(2)}, u32[]{:S(2)}) %collective-permute-start.3) | collective-permute-done | bytes 524320 | tf_op jit(solution)/shard_map/ppermute | solution.py:317
  22.1 1.0 copy-done.3
  23.0 0.1 collective-permute-done.4.second_other
  23.1 5.1 %expand.2 = (bf16[32,128,128]{2,1,0:T(8,128)(2,1)}, bf16[32,128,128]{2,1,0:T(8,128)(2,1)}, bf16[32,128,128]{2,1,0:T(8,128)(2,1)}, bf16[32,128,128]{2,1,0:T(8,128)(2,1)}) custom-call(s32[1]{0:T(128)} %bitcast.p, bf16[64,64,64]{2,1,0:T(8,128)(2,1)} %bitcast.30, bf16[64,64,64]{2,1,0:T(8,128)(2,1)} %copy-done.3, bf16[64,64,64]{2,1,0:T(8,128)(2,1)} %bitcast.33, ...), custom_call_target="tpu_custom_call" | custom-call | flops 268435456 | bytes 8388608 | tf_op jit(solution)/shard_map/expand/pallas_call | solution.py:398
  28.2 0.0 collective-permute-done.2.right_other
  28.2 0.6 copy-done.17
  28.8 9.0 %forward.1 = (bf16[128,4096]{1,0:T(8,128)(2,1)}, bf16[4096,128]{1,0:T(8,128)(2,1)}, bf16[128,4096]{1,0:T(8,128)(2,1)}, bf16[128,4096]{1,0:T(8,128)(2,1)}, bf16[1...) custom-call(s32[1]{0:T(128)} %bitcast.p, ...), custom_call_target="tpu_custom_call" | custom-call | flops 268435456 | bytes 8388608 | tf_op jit(solution)/shard_map/forward/pallas_call | solution.py:409
  37.8 5.6 %all-to-all-done.1 = bf16[16,8,4096]{2,1,0:T(8,128)(2,1)} async-done(((bf16[16,8,4096]{2,1,0:T(8,128)(2,1)}), bf16[16,8,4096]{2,1,0:T(8,128)(2,1)}, u32[]{:S(2)}, u32[]{:S(2)}) %all-to-all-start.1) | async-done | bytes 1048608 | tf_op jit(solution)/shard_map/all_to_all | solution.py:326
  43.4 6.1 %all-to-all-start = ((bf16[16,8,4096]{2,1,0:T(8,128)(2,1)}), bf16[16,8,4096]{2,1,0:T(8,128)(2,1)S(1)}, u32[]{:S(2)}, u32[]{:S(2)}) async-start(bf16[16,8,4096]{2,1,0:T(8,128)(2,1)} %bitcast.45), calls=%async_computation | async-start | bytes 2097152 | tf_op jit(solution)/shard_map/all_to_all | solution.py:326
  49.5 8.0 %middle.1 = (bf16[128,4096]{1,0:T(8,128)(2,1)}, f32[128,4096]{1,0:T(8,128)}, f32[128,128]{1,0:T(8,128)}, bf16[16,2,128,128]{3,2,1,0:T(8,128)(2,1)}) custom-call(bf16[128,4096]{1,0:T(8,128)(2,1)} %bitcast.11.back, bf16[32,128,128]{2,1,0:T(8,128)(2,1)} %get-tuple-element.51.second_bt, bf16[32,128,128]{2,1,0:T(8,128)(2,1)} %get-tuple-element.52.first_bt, ...), custom_call_target="tpu_custom_call" | custom-call | flops 268435456 | bytes 8388608 | tf_op jit(solution)/shard_map/middle/pallas_call | solution.py:437
  57.5 15.3 %all-to-all-done = bf16[16,8,4096]{2,1,0:T(8,128)(2,1)S(1)} async-done(((bf16[16,8,4096]{2,1,0:T(8,128)(2,1)}), bf16[16,8,4096]{2,1,0:T(8,128)(2,1)S(1)}, u32[]{:S(2)}, u32[]{:S(2)}) %all-to-all-start) | async-done | bytes 1048608 | tf_op jit(solution)/shard_map/all_to_all | solution.py:326
  72.8 1.0 copy-done.9
  73.8 5.9 %all-to-all-start.3 = ((bf16[16,8,4096]{2,1,0:T(8,128)(2,1)}), bf16[16,8,4096]{2,1,0:T(8,128)(2,1)S(1)}, u32[]{:S(2)}, u32[]{:S(2)}) async-start(bf16[16,8,4096]{2,1,0:T(8,128)(2,1)} %bitcast.43), calls=%async_computation.3 | async-start | bytes 2097152 | tf_op jit(solution)/shard_map/all_to_all | solution.py:326
  79.6 1.1 dynamic-slice_bitcast_fusion.upstream
  80.7 5.0 %expand.3 = (bf16[32,128,128]{2,1,0:T(8,128)(2,1)}, bf16[32,128,128]{2,1,0:T(8,128)(2,1)}, bf16[32,128,128]{2,1,0:T(8,128)(2,1)}, bf16[32,128,128]{2,1,0:T(8,128)(2,1)}) custom-call(s32[1]{0:T(128)} %bitcast.p, bf16[64,64,64]{2,1,0:T(8,128)(2,1)} %bitcast.31, bf16[64,64,64]{2,1,0:T(8,128)(2,1)} %copy-done.3, bf16[64,64,64]{2,1,0:T(8,128)(2,1)} %bitcast.34, ...), custom_call_target="tpu_custom_call" | custom-call | flops 268435456 | bytes 8388608 | tf_op jit(solution)/shard_map/expand/pallas_call | solution.py:398
  85.8 11.1 %turn.1 = (bf16[128,4096]{1,0:T(8,128)(2,1)}, f32[128,16]{1,0:T(8,128)}, bf16[128,4096]{1,0:T(8,128)(2,1)}, bf16[128,4096]{1,0:T(8,128)(2,1)}, bf16[4096,128]{1,0:T(8,128)(2,1)}, /*index=5*/bf16[128,4096]{1,0:T(8,128)(2,1)}) custom-call(bf16[128,4096]{1,0:T(8,128)(2,1)} %bitcast.40, bf16[128,4096]{1,0:T(8,128)(2,1)} %dynamic-slice_bitcast_fusion.upstream, ...), custom_call_target="tpu_custom_call" | custom-call | flops 268435456 | bytes 8388608 | tf_op jit(solution)/shard_map/turn/pallas_call | solution.py:448
  96.9 5.7 %all-to-all-done.3 = bf16[16,8,4096]{2,1,0:T(8,128)(2,1)S(1)} async-done(((bf16[16,8,4096]{2,1,0:T(8,128)(2,1)}), bf16[16,8,4096]{2,1,0:T(8,128)(2,1)S(1)}, u32[]{:S(2)}, u32[]{:S(2)}) %all-to-all-start.3) | async-done | bytes 1048608 | tf_op jit(solution)/shard_map/all_to_all | solution.py:326
  102.5 6.1 %all-to-all-start.2 = ((bf16[16,8,4096]{2,1,0:T(8,128)(2,1)}), bf16[16,8,4096]{2,1,0:T(8,128)(2,1)}, u32[]{:S(2)}, u32[]{:S(2)}) async-start(bf16[16,8,4096]{2,1,0:T(8,128)(2,1)} %bitcast.44), calls=%async_computation.2 | async-start | bytes 2097152 | tf_op jit(solution)/shard_map/all_to_all | solution.py:326
  108.6 7.7 %lower.1 = (f32[128,4096]{1,0:T(8,128)}, f32[128,16]{1,0:T(8,128)}, bf16[16,2,128,128]{3,2,1,0:T(8,128)(2,1)}) custom-call(bf16[128,4096]{1,0:T(8,128)(2,1)} %bitcast.36, bf16[32,128,128]{2,1,0:T(8,128)(2,1)} %get-tuple-element.69.first_bd, bf16[32,128,128]{2,1,0:T(8,128)(2,1)} %get-tuple-element.70.second_bd, bf16[128,128]{1,0:T(8,128)(2,1)} %get-tuple-element.71.left, ...), custom_call_target="tpu_custom_call" | custom-call | flops 268435456 | bytes 8388608 | tf_op jit(solution)/shard_map/lower/pallas_call | solution.py:493
  116.4 0.1 broadcast_select_fusion
  116.5 0.1 collective-permute-start.9
  116.6 2.6 %collective-permute-done.9 = bf16[16,2,128,128]{3,2,1,0:T(8,128)(2,1)S(1)} collective-permute-done((bf16[16,2,128,128]{3,2,1,0:T(8,128)(2,1)S(1)}, bf16[16,2,128,128]{3,2,1,0:T(8,128)(2,1)S(1)}, u32[]{:S(2)}, u32[]{:S(2)}) %collective-permute-start.9) | collective-permute-done | bytes 1048608 | tf_op jit(solution)/shard_map/ppermute | solution.py:317
  119.2 0.5 add_convert_fusion
  119.7 11.8 %all-to-all-done.2 = bf16[16,8,4096]{2,1,0:T(8,128)(2,1)} async-done(((bf16[16,8,4096]{2,1,0:T(8,128)(2,1)}), bf16[16,8,4096]{2,1,0:T(8,128)(2,1)}, u32[]{:S(2)}, u32[]{:S(2)}) %all-to-all-start.2) | async-done | bytes 1048608 | tf_op jit(solution)/shard_map/all_to_all | solution.py:326
  131.5 18.9 %all_to_all.30.pieces = bf16[8,4,128,128]{3,2,1,0:T(8,128)(2,1)} all-to-all(bf16[8,4,128,128]{3,2,1,0:T(8,128)(2,1)S(1)} %bitcast.38), channel_id=1, replica_groups={{0,2,4,6,8,10,12,14},{24,26,28,30,16,18,20,22},{1,3,5,7,9,11,13,15},{25..., dimensions={0} | all-to-all | bytes 2097152 | tf_op jit(solution)/shard_map/all_to_all | solution.py:336
  150.3 2.0 %total.1.refs_0_ = bf16[4,128,128]{2,1,0:T(8,128)(2,1)} custom-call(bf16[8,4,128,128]{3,2,1,0:T(8,128)(2,1)} %all_to_all.30.pieces), custom_call_target="tpu_custom_call" | custom-call | flops 268435456 | bytes 8388608 | tf_op jit(solution)/shard_map/total/pallas_call | solution.py:339
  152.4 1.8 collective-permute-start.10
  154.2 5.2 %collective-permute-done.10.refs_1_ = bf16[4,128,128]{2,1,0:T(8,128)(2,1)S(1)} collective-permute-done((bf16[4,128,128]{2,1,0:T(8,128)(2,1)}, bf16[4,128,128]{2,1,0:T(8,128)(2,1)S(1)}, u32[]{:S(2)}, u32[]{:S(2)}) %collective-permute-start.10) | collective-permute-done | bytes 131104 | tf_op jit(solution)/shard_map/ppermute | solution.py:341
  159.3 0.6 copy-done.15
  160.0 2.0 %spread.1 = bf16[8,4,128,128]{3,2,1,0:T(8,128)(2,1)} custom-call(bf16[4,128,128]{2,1,0:T(8,128)(2,1)} %total.1.refs_0_, bf16[4,128,128]{2,1,0:T(8,128)(2,1)} %copy-done.15), custom_call_target="tpu_custom_call" | custom-call | flops 268435456 | bytes 8388608 | tf_op jit(solution)/shard_map/spread/pallas_call | solution.py:343
  162.0 3.6 %all-to-all-start.5 = ((bf16[8,4,128,128]{3,2,1,0:T(8,128)(2,1)}), bf16[8,4,128,128]{3,2,1,0:T(8,128)(2,1)S(1)}, u32[]{:S(2)}, u32[]{:S(2)}) async-start(bf16[8,4,128,128]{3,2,1,0:T(8,128)(2,1)} %spread.1), calls=%async_computation.5 | async-start | bytes 2097152 | tf_op jit(solution)/shard_map/all_to_all | solution.py:336
  165.6 0.1 collective-permute-start.6
  165.6 0.0 copy-start.11
  165.7 0.0 copy-start.10
  165.7 4.8 %last.1 = (bf16[128,4096]{1,0:T(8,128)(2,1)}, f32[128,128]{1,0:T(8,128)}) custom-call(bf16[128,4096]{1,0:T(8,128)(2,1)} %bitcast.13.received, bf16[128,128]{1,0:T(8,128)(2,1)} %get-tuple-element.66.right_t, bf16[128,4096]{1,0:T(8,128)(2,1)} %get-tuple-element.67.upstream, f32[128,4096]{1,0:T(8,128)} %get-tuple-element.75.carried, ...), custom_call_target="tpu_custom_call" | custom-call | flops 268435456 | bytes 8388608 | tf_op jit(solution)/shard_map/last/pallas_call | solution.py:507
  170.5 0.5 collective-permute-start.5
  170.9 0.1 collective-permute-start.8
  171.1 1.3 collective-permute-start.7
  172.4 0.9 collective-permute-done.8
  173.3 0.6 select_add_fusion
  174.0 0.0 collective-permute-done.7
  174.0 1.5 select_add_fusion.1
  175.4 0.0 collective-permute-done.6
  175.4 0.0 collective-permute-done.5
  175.4 3.5 %maximum_select_fusion = bf16[1,2,128,4096]{3,2,1,0:T(8,128)(2,1)} fusion(bf16[1,1,128,4096]{3,2,1,0:T(8,128)(2,1)S(1)} %bitcast.42, bf16[1,1,128,4096]{3,2,1,0:T(8,128)(2,1)} %bitcast.41, bf16[1,1,128,4096]{3,2,1,0:T(8,128)(2,1)} %bitcast.19, bf16[1,1,128,4096]{3,2,1,0:T(8,128)(2,1)} %bitcast.18, pred[]{:T(512)S(6)} %eq.2), kind=kLoop, calls=%fused_computation | loop fusion | flops 3145728 | bytes 6291457 | tf_op jit(solution)/shard_map/jit(_where)/select_n | solution.py:521
  179.0 0.0 all-to-all-done.5
  179.0 1.0 copy-done.7
  180.0 4.1 %unpack.1 = (f32[64,64,64]{2,1,0:T(8,128)}, f32[64,64,64]{2,1,0:T(8,128)}) custom-call(bf16[16,2,128,128]{3,2,1,0:T(8,128)(2,1)} %bitcast.39), custom_call_target="tpu_custom_call" | custom-call | flops 268435456 | bytes 8388608 | tf_op jit(solution)/shard_map/unpack/pallas_call | solution.py:525
  (25 shorter events, 0.1 us)
Async XLA Ops:
  0.6 1.8 copy-start.13
  1.9 2.9 %collective-permute-start = (bf16[128,4096]{1,0:T(8,128)(2,1)S(1)}, bf16[128,4096]{1,0:T(8,128)(2,1)S(1)}, u32[]{:S(2)}, u32[]{:S(2)}) collective-permute-start(bf16[128,4096]{1,0:T(8,128)(2,1)S(1)} %dynamic-slice_bitcast_fusion.1), channel_id=1, source_target_pairs={{0,1},{1,0},{2,3},{3,2},{4,5},{5,4},{6,7},{7,6},{8,9},{9,8},{10,11... | collective-permute-start | bytes 3145736 | tf_op jit(solution)/shard_map/ppermute | solution.py:317
  2.5 2.3 %collective-permute-start.1 = (bf16[128,16]{1,0:T(8,128)(2,1)S(1)}, bf16[128,16]{1,0:T(8,128)(2,1)S(1)}, u32[]{:S(2)}, u32[]{:S(2)}) collective-permute-start(bf16[128,16]{1,0:T(8,128)(2,1)S(1)} %bitcast.48), channel_id=1, source_target_pairs={{0,1},{1,0},{2,3},{3,2},{4,5},{5,4},{6,7},{7,6},{8,9},{9,8},{10,11... | collective-permute-start | bytes 12296 | tf_op jit(solution)/shard_map/ppermute | solution.py:317
  4.8 0.6 copy-start.14
  4.8 1.0 copy-start.8
  5.8 13.5 %copy-start.16 = (bf16[1,1,128,128]{3,2,1,0:T(8,128)(2,1)S(1)}, bf16[1,1,128,128]{3,2,1,0:T(8,128)(2,1)}, u32[]{:S(2)}) copy-start(bf16[1,1,128,128]{3,2,1,0:T(8,128)(2,1)} %param.11) | copy-start | bytes 98308
  10.3 8.4 %copy-start.1 = (bf16[1,64,64,64]{3,2,1,0:T(8,128)(2,1)S(1)}, bf16[1,64,64,64]{3,2,1,0:T(8,128)(2,1)}, u32[]{:S(2)}) copy-start(bf16[1,64,64,64]{3,2,1,0:T(8,128)(2,1)} %param.13) | copy-start | bytes 1572868
  10.3 8.5 %copy-start.2 = (bf16[1,64,64,64]{3,2,1,0:T(8,128)(2,1)S(1)}, bf16[1,64,64,64]{3,2,1,0:T(8,128)(2,1)}, u32[]{:S(2)}) copy-start(bf16[1,64,64,64]{3,2,1,0:T(8,128)(2,1)} %param.14) | copy-start | bytes 1572868
  10.3 33.1 %all-to-all-start.1 = ((bf16[16,8,4096]{2,1,0:T(8,128)(2,1)}), bf16[16,8,4096]{2,1,0:T(8,128)(2,1)}, u32[]{:S(2)}, u32[]{:S(2)}) async-start(bf16[16,8,4096]{2,1,0:T(8,128)(2,1)} %bitcast.37), calls=%async_computation.1 | async-start | bytes 2097152 | tf_op jit(solution)/shard_map/all_to_all | solution.py:326
  18.7 3.3 %collective-permute-start.3 = (bf16[64,64,64]{2,1,0:T(8,128)(2,1)S(1)}, bf16[64,64,64]{2,1,0:T(8,128)(2,1)S(1)}, u32[]{:S(2)}, u32[]{:S(2)}) collective-permute-start(bf16[64,64,64]{2,1,0:T(8,128)(2,1)S(1)} %bitcast.32), channel_id=1, source_target_pairs={{0,1},{1,0},{2,3},{3,2},{4,5},{5,4},{6,7},{7,6},{8,9},{9,8},{10,11... | collective-permute-start | bytes 1572872 | tf_op jit(solution)/shard_map/ppermute | solution.py:317
  18.8 4.3 %collective-permute-start.4 = (bf16[64,64,64]{2,1,0:T(8,128)(2,1)S(1)}, bf16[64,64,64]{2,1,0:T(8,128)(2,1)}, u32[]{:S(2)}, u32[]{:S(2)}) collective-permute-start(bf16[64,64,64]{2,1,0:T(8,128)(2,1)S(1)} %bitcast.35), channel_id=1, source_target_pairs={{0,1},{1,0},{2,3},{3,2},{4,5},{5,4},{6,7},{7,6},{8,9},{9,8},{10,11... | collective-permute-start | bytes 1572872 | tf_op jit(solution)/shard_map/ppermute | solution.py:317
  19.3 8.9 %collective-permute-start.2 = (bf16[128,128]{1,0:T(8,128)(2,1)S(1)}, bf16[128,128]{1,0:T(8,128)(2,1)S(1)}, u32[]{:S(2)}, u32[]{:S(2)}) collective-permute-start(bf16[128,128]{1,0:T(8,128)(2,1)S(1)} %bitcast.52), channel_id=1, source_target_pairs={{0,1},{1,0},{2,3},{3,2},{4,5},{5,4},{6,7},{7,6},{8,9},{9,8},{10,11... | collective-permute-start | bytes 98312 | tf_op jit(solution)/shard_map/ppermute | solution.py:317
  22.1 1.0 copy-start.3
  28.2 0.6 copy-start.17
  43.4 29.4 %all-to-all-start = ((bf16[16,8,4096]{2,1,0:T(8,128)(2,1)}), bf16[16,8,4096]{2,1,0:T(8,128)(2,1)S(1)}, u32[]{:S(2)}, u32[]{:S(2)}) async-start(bf16[16,8,4096]{2,1,0:T(8,128)(2,1)} %bitcast.45), calls=%async_computation | async-start | bytes 2097152 | tf_op jit(solution)/shard_map/all_to_all | solution.py:326
  57.5 22.2 %copy-start = (bf16[2,128,4096]{2,1,0:T(8,128)(2,1)S(1)}, bf16[2,128,4096]{2,1,0:T(8,128)(2,1)}, u32[]{:S(2)}) copy-start(bf16[2,128,4096]{2,1,0:T(8,128)(2,1)} %upstream.3) | copy-start | bytes 6291460
  72.8 1.0 copy-start.9
  73.8 28.8 %all-to-all-start.3 = ((bf16[16,8,4096]{2,1,0:T(8,128)(2,1)}), bf16[16,8,4096]{2,1,0:T(8,128)(2,1)S(1)}, u32[]{:S(2)}, u32[]{:S(2)}) async-start(bf16[16,8,4096]{2,1,0:T(8,128)(2,1)} %bitcast.43), calls=%async_computation.3 | async-start | bytes 2097152 | tf_op jit(solution)/shard_map/all_to_all | solution.py:326
  102.5 6.1 %copy-start.5 = (bf16[16,8,4096]{2,1,0:T(8,128)(2,1)}, bf16[16,8,4096]{2,1,0:T(8,128)(2,1)S(1)}, u32[]{:S(2)}) copy-start(bf16[16,8,4096]{2,1,0:T(8,128)(2,1)S(1)} %all-to-all-done.3) | copy-start | bytes 3145732
  102.5 29.0 %all-to-all-start.2 = ((bf16[16,8,4096]{2,1,0:T(8,128)(2,1)}), bf16[16,8,4096]{2,1,0:T(8,128)(2,1)}, u32[]{:S(2)}, u32[]{:S(2)}) async-start(bf16[16,8,4096]{2,1,0:T(8,128)(2,1)} %bitcast.44), calls=%async_computation.2 | async-start | bytes 2097152 | tf_op jit(solution)/shard_map/all_to_all | solution.py:326
  108.6 7.7 %copy-start.4 = (bf16[16,2,128,128]{3,2,1,0:T(8,128)(2,1)S(1)}, bf16[16,2,128,128]{3,2,1,0:T(8,128)(2,1)}, u32[]{:S(2)}) copy-start(bf16[16,2,128,128]{3,2,1,0:T(8,128)(2,1)} %get-tuple-element.82) | copy-start | bytes 3145732
  116.3 2.9 %copy-start.6 = (bf16[16,2,128,128]{3,2,1,0:T(8,128)(2,1)S(1)}, bf16[16,2,128,128]{3,2,1,0:T(8,128)(2,1)}, u32[]{:S(2)}) copy-start(bf16[16,2,128,128]{3,2,1,0:T(8,128)(2,1)} %get-tuple-element.81) | copy-start | bytes 3145732
  116.5 2.7 %collective-permute-start.9 = (bf16[16,2,128,128]{3,2,1,0:T(8,128)(2,1)S(1)}, bf16[16,2,128,128]{3,2,1,0:T(8,128)(2,1)S(1)}, u32[]{:S(2)}, u32[]{:S(2)}) collective-permute-start(bf16[16,2,128,128]{3,2,1,0:T(8,128)(2,1)S(1)} %broadcast_select_fusion), channel_id=1, source_target_pairs={{0,1},{1,0},{2,3},{3,2},{4,5},{5,4},{6,7},{7,6},{8,9},{9,8},{10,11... | collective-permute-start | bytes 3145736 | tf_op jit(solution)/shard_map/ppermute | solution.py:317
  152.4 7.0 %collective-permute-start.10 = (bf16[4,128,128]{2,1,0:T(8,128)(2,1)}, bf16[4,128,128]{2,1,0:T(8,128)(2,1)S(1)}, u32[]{:S(2)}, u32[]{:S(2)}) collective-permute-start(bf16[4,128,128]{2,1,0:T(8,128)(2,1)} %total.1.refs_0_), channel_id=1, source_target_pairs={{0,24},{2,26},{4,28},{6,30},{8,16},{10,18},{12,20},{14,22},{16,8},... | collective-permute-start | bytes 393224 | tf_op jit(solution)/shard_map/ppermute | solution.py:341
  159.3 0.6 copy-start.15
  162.0 17.0 %all-to-all-start.5 = ((bf16[8,4,128,128]{3,2,1,0:T(8,128)(2,1)}), bf16[8,4,128,128]{3,2,1,0:T(8,128)(2,1)S(1)}, u32[]{:S(2)}, u32[]{:S(2)}) async-start(bf16[8,4,128,128]{3,2,1,0:T(8,128)(2,1)} %spread.1), calls=%async_computation.5 | async-start | bytes 2097152 | tf_op jit(solution)/shard_map/all_to_all | solution.py:336
  165.6 9.9 %collective-permute-start.6 = (bf16[128,4096]{1,0:T(8,128)(2,1)}, bf16[128,4096]{1,0:T(8,128)(2,1)}, u32[]{:S(2)}, u32[]{:S(2)}) collective-permute-start(bf16[128,4096]{1,0:T(8,128)(2,1)} %get-tuple-element.67.upstream), channel_id=1, source_target_pairs={{0,1},{1,0},{2,3},{3,2},{4,5},{5,4},{6,7},{7,6},{8,9},{9,8},{10,11... | collective-permute-start | bytes 3145736 | tf_op jit(solution)/shard_map/ppermute | solution.py:317
  165.6 5.3 %copy-start.11 = (f32[128,16]{1,0:T(8,128)S(1)}, f32[128,16]{1,0:T(8,128)}, u32[]{:S(2)}) copy-start(f32[128,16]{1,0:T(8,128)} %get-tuple-element.80) | copy-start | bytes 24580
  165.7 5.3 %copy-start.12 = (f32[128,16]{1,0:T(8,128)S(1)}, f32[128,16]{1,0:T(8,128)}, u32[]{:S(2)}) copy-start(f32[128,16]{1,0:T(8,128)} %get-tuple-element.79) | copy-start | bytes 24580
  165.7 5.4 %copy-start.10 = (f32[128,128]{1,0:T(8,128)S(1)}, f32[128,128]{1,0:T(8,128)}, u32[]{:S(2)}) copy-start(f32[128,128]{1,0:T(8,128)} %get-tuple-element.78) | copy-start | bytes 196612
  170.5 5.0 %collective-permute-start.5 = (bf16[128,4096]{1,0:T(8,128)(2,1)}, bf16[128,4096]{1,0:T(8,128)(2,1)S(1)}, u32[]{:S(2)}, u32[]{:S(2)}) collective-permute-start(bf16[128,4096]{1,0:T(8,128)(2,1)} %get-tuple-element.76), channel_id=1, source_target_pairs={{0,1},{1,0},{2,3},{3,2},{4,5},{5,4},{6,7},{7,6},{8,9},{9,8},{10,11... | collective-permute-start | bytes 3145736 | tf_op jit(solution)/shard_map/ppermute | solution.py:317
  170.9 2.4 %collective-permute-start.8 = (f32[128,16]{1,0:T(8,128)S(1)}, f32[128,16]{1,0:T(8,128)S(1)}, u32[]{:S(2)}, u32[]{:S(2)}) collective-permute-start(f32[128,16]{1,0:T(8,128)S(1)} %broadcast_select_fusion.1), channel_id=1, source_target_pairs={{0,1},{1,0},{2,3},{3,2},{4,5},{5,4},{6,7},{7,6},{8,9},{9,8},{10,11... | collective-permute-start | bytes 24584 | tf_op jit(solution)/shard_map/ppermute | solution.py:317
  171.1 2.9 %collective-permute-start.7 = (f32[128,128]{1,0:T(8,128)S(1)}, f32[128,128]{1,0:T(8,128)S(1)}, u32[]{:S(2)}, u32[]{:S(2)}) collective-permute-start(f32[128,128]{1,0:T(8,128)S(1)} %broadcast_select_fusion.2), channel_id=1, source_target_pairs={{0,1},{1,0},{2,3},{3,2},{4,5},{5,4},{6,7},{7,6},{8,9},{9,8},{10,11... | collective-permute-start | bytes 196616 | tf_op jit(solution)/shard_map/ppermute | solution.py:317
  179.0 1.0 copy-start.7

commit v3 on v2

--- a/solution.py
+++ b/solution.py
@@ -22,8 +22,8 @@
     return pl.BlockSpec(shape, lambda *_: (0,) * len(shape))
 
 
-def call(kernel, name, out_shape, grid, in_specs, out_specs, scratch=(), scalars=0):
-    params = pltpu.CompilerParams(vmem_limit_bytes=62 * 1024 * 1024)
+def call(kernel, name, out_shape, grid, in_specs, out_specs, scratch=(), scalars=0, room=62):
+    params = pltpu.CompilerParams(vmem_limit_bytes=room * 1024 * 1024)
     estimate = pl.CostEstimate(flops=1 << 28, bytes_accessed=8 << 20, transcendentals=0)
     spec = pltpu.PrefetchScalarGridSpec(
         num_scalar_prefetch=scalars, grid=grid, in_specs=in_specs, out_specs=out_specs, scratch_shapes=scratch
@@ -75,15 +75,9 @@
     return (mm(onehot, left, NT) * mask.astype(F32).T).astype(BF)
 
 
-def gate_kernel(p, keep, recv, upstream, left_own, left_other, onehot, mask, back, left_t):
-    @pl.when(pl.program_id(0) == 0)
-    def _():
-        left = pick(p, left_other[...], left_own[...]).astype(BF)
-        left_t[...] = spread_turned(left, onehot[...], mask[...])
-
-    act = pick(p, recv[...], keep[0])
-    gate = (upstream[0].astype(F32) * act).astype(BF)
-    back[...] = mm(left_t[...], gate).astype(BF)
+def left_kernel(left, onehot, mask, full, turned):
+    full[...] = spread(left[...], onehot[...], mask[...])
+    turned[...] = spread_turned(left[...], onehot[...], mask[...])
 
 
 def expand_kernel(section, p, first, first_other, second, second_other, first_bd, first_bt, second_bd, second_bt):
@@ -105,47 +99,26 @@
 
 def forward_kernel(
     p,
-    keep,
-    recv,
+    act,
     right_own,
     right_other,
-    upstream,
-    left_own,
-    left_other,
-    onehot,
-    mask,
     first_bd,
     second_bd,
     eye,
     rows,
     mixed,
     right_act,
-    act_0,
-    act_1,
-    gate,
     right_t_1,
     right_t_0,
     right_0,
-    full_1,
-    full_0,
-    turned_0,
     wide,
 ):
-    act_0[...] = pick(p, keep[0], recv[...]).astype(BF)
-    act = pick(p, recv[...], keep[0])
-    act_1[...] = act.astype(BF)
-    gate[...] = (upstream[0].astype(F32) * act).astype(BF)
-    left_0 = pick(p, left_own[...], left_other[...]).astype(BF)
-    left_1 = pick(p, left_other[...], left_own[...]).astype(BF)
-    full_1[...] = spread(left_1, onehot[...], mask[...])
-    full_0[...] = spread(left_0, onehot[...], mask[...])
-    turned_0[...] = spread_turned(left_0, onehot[...], mask[...])
     low = pick(p, right_own[...], right_other[...]).astype(BF)
     high = pick(p, right_other[...], right_own[...]).astype(BF)
     right_0[...] = low
     right_t_0[...] = low.astype(F32).T.astype(BF)
     right_t_1[...] = high.astype(F32).T.astype(BF)
-    right_act[...] = mm(high, act_1[...]).astype(BF)
+    right_act[...] = mm(high, act[...]).astype(BF)
     pairs = first_bd.shape[0]
     for q in range(pairs):
         wide[columns(q), :] = mm(first_bd[q], right_act[:, columns(q)], NT)
@@ -190,7 +163,7 @@
 def turn_kernel(
     rows,
     upstream,
-    gate_high,
+    act,
     chan_back,
     act_low,
     left,
@@ -213,10 +186,11 @@
     steps = pl.num_programs(0)
     pairs = second_bt.shape[0]
 
+    gy = upstream[...].astype(F32)
     carried = mm(left[...], rows[...])
-    incoming = (upstream[...].astype(F32) * carried + chan_back[...]).astype(BF)
+    incoming = (gy * carried + chan_back[...]).astype(BF)
     input_grad[...] = incoming
-    term = mm(gate_high[...], rows[...], NT)
+    term = mm((gy * act[...].astype(F32)).astype(BF), rows[...], NT)
 
     @pl.when(step == 0)
     def _():
@@ -291,19 +265,6 @@
         right_grad[...] += term
 
 
-def total_kernel(pieces, out):
-    total = pieces[0].astype(F32)
-    for i in range(1, pieces.shape[0]):
-        total += pieces[i].astype(F32)
-    out[...] = total.astype(BF)
-
-
-def spread_kernel(*refs):
-    total = sum(ref[...].astype(F32) for ref in refs[:-1]).astype(BF)
-    for i in range(refs[-1].shape[0]):
-        refs[-1][i] = total
-
-
 def unpack_kernel(sums, first, second):
     side = first.shape[1]
     for part, out in enumerate((first, second)):
@@ -326,7 +287,7 @@
     return lax.all_to_all(chunks, "blk", split_axis=0, concat_axis=0, tiled=True).reshape(rows.shape)
 
 
-def summed(parts, devices):
+def summed(parts, devices, others):
     far = 12 if devices == 16 else 0
     members = devices // 2 if far else devices
     groups = [[member ^ f for member in range(members)] for f in ((0, far) if far else (0,))]
@@ -335,12 +296,12 @@
     def exchanged(value):
         return lax.all_to_all(value, "blk", split_axis=0, concat_axis=0, axis_index_groups=groups, tiled=True)
 
-    pieces = exchanged(parts.reshape(shape))
-    terms = [call(total_kernel, "total", sds(shape[1:], BF), (1,), [whole(shape)], whole(shape[1:]))(pieces)]
+    pieces = after(exchanged(parts.reshape(shape)), *others)
+    total = jnp.sum(pieces.astype(F32), axis=0).astype(BF)
     if far:
-        terms.append(lax.ppermute(terms[0], "blk", [(i, i ^ far) for i in range(devices)]))
-    share = [whole(shape[1:])] * len(terms)
-    return exchanged(call(spread_kernel, "spread", sds(shape, BF), (1,), share, whole(shape))(*terms)).reshape(parts.shape)
+        came = lax.ppermute(total, "blk", [(i, i ^ far) for i in range(devices)])
+        total = (total.astype(F32) + came.astype(F32)).astype(BF)
+    return exchanged(jnp.broadcast_to(total[None], shape)).reshape(parts.shape)
 
 
 def body(x_saved, cotangent, seq_right, seq_left, chan_first, chan_second):
@@ -354,9 +315,8 @@
     blocks, side = chan_first.shape[1], chan_first.shape[2]
     pairs = blocks // 2
 
-    received = swap(lax.dynamic_index_in_dim(saved, 1 - core, 0, keepdims=False))
-    left_own = seq_left[0].reshape(per * count, count)
-    left_other = swap(left_own)
+    sent = lax.dynamic_index_in_dim(saved, 1 - core, 0, keepdims=False)
+    received = swap(sent)
     right_own = seq_right[0, 0]
     right_other = swap(right_own)
     first_own, first_other = chan_first[0], swap(chan_first[0])
@@ -371,28 +331,29 @@
     square = whole((tokens, tokens))
     narrow = whole((tokens, count))
     moving = pl.BlockSpec((tokens, step), lambda i, *_: (0, i))
-    chosen = pl.BlockSpec((1, tokens, step), lambda i, p: (p[0], 0, i))
     act_shape = (tokens, width)
     col_shape = (width, tokens)
     pair_shape = (pairs, 2 * side, 2 * side)
     owned = (devices, 2, pairs * side // devices, 2 * side)
     act_full, col_full, pair_full = map(whole, (act_shape, col_shape, pair_shape))
-    chosen_full = pl.BlockSpec((1,) + act_shape, lambda i, p: (p[0], 0, 0))
     box = whole((blocks, side, side))
     squared = sds((tokens, tokens), BF)
 
-    back_1 = call(
-        gate_kernel,
-        "gate",
-        sds(act_shape, BF),
-        (width // step,),
-        [chosen, moving, chosen, narrow, narrow, narrow, square],
-        moving,
-        [pltpu.VMEM((tokens, tokens), BF)],
-        scalars=1,
-    )(p, saved, received, cotangent, left_own, left_other, onehot, mask)
+    full, turned = call(left_kernel, "left", [squared] * 2, (1,), [narrow, narrow, square], [square] * 2, room=8)(
+        seq_left[0].reshape(per * count, count), onehot, mask
+    )
+    full_other, turned_other = swap(full), swap(turned)
+    turned_1 = jnp.where(core == 0, turned_other, turned)
+    mine = after(core, sent)
+    upstream, kept = lax.optimization_barrier(
+        tuple(lax.dynamic_index_in_dim(whole_array, mine, 0, keepdims=False) for whole_array in (cotangent, saved))
+    )
+    act_1 = jnp.where(core == 0, received, kept)
+    gate_1 = after((upstream.astype(F32) * act_1.astype(F32)).astype(BF))
+    back_1 = jnp.dot(turned_1, gate_1, preferred_element_type=F32).astype(BF)
     returned_1 = exchange(back_1, devices)
-    p = after(p, back_1)
+    p, received, kept = lax.optimization_barrier((p, received, kept, back_1))[:3]
+    act_0, act_1 = jnp.where(core == 0, kept, received), jnp.where(core == 0, received, kept)
 
     def expand(p, section):
         return call(
@@ -406,26 +367,20 @@
         )(p, first_own, first_other, second_own, second_other)
 
     fbd_1, fbt_1, sbd_1, sbt_1 = expand(p, 1)
-    rows_1, mixed_1, right_act_1, act_0, act_1, gate_1, right_t_1, right_t_0, right_0, full_1, full_0, turned_0 = call(
+    rows_1, mixed_1, right_act_1, right_t_1, right_t_0, right_0 = call(
         forward_kernel,
         "forward",
-        [sds(act_shape, BF), sds(col_shape, BF)] + [sds(act_shape, BF)] * 4 + [squared] * 6,
+        [sds(act_shape, BF), sds(col_shape, BF), sds(act_shape, BF)] + [squared] * 3,
         (1,),
-        [chosen_full, act_full, square, square, chosen_full, narrow, narrow, narrow, square, pair_full, pair_full, square],
-        [act_full, col_full] + [act_full] * 4 + [square] * 6,
+        [act_full, square, square, pair_full, pair_full, square],
+        [act_full, col_full, act_full] + [square] * 3,
         [pltpu.VMEM(col_shape, F32)],
         scalars=1,
     )(
         p,
-        saved,
-        received,
+        act_1,
         right_own,
         right_other,
-        cotangent,
-        left_own,
-        left_other,
-        onehot,
-        mask,
         fbd_1,
         sbd_1,
         eye,
@@ -473,14 +428,15 @@
         ],
         [moving, narrow, moving, moving, col_full, act_full],
         [pltpu.VMEM(col_shape, F32), pltpu.VMEM((tokens, tokens), F32)],
+        room=62,
     )(
         gathered_1,
-        lax.dynamic_index_in_dim(cotangent, core, 0, keepdims=False),
-        gate_1,
+        upstream,
+        act_1,
         chan_back_1,
         act_0,
-        full_1,
-        turned_0,
+        jnp.where(core == 0, full_other, full),
+        jnp.where(core == 0, turned, turned_other),
         sbt_0,
         fbt_0,
         eye,
@@ -498,11 +454,10 @@
         [act_full, pair_full, pair_full, square, act_full, act_full, col_full, narrow, square],
         [act_full, narrow, whole(owned)],
         [pltpu.VMEM(col_shape, F32), pltpu.VMEM(col_shape, BF)],
-    )(gathered_0, fbd_0, sbd_0, full_0, gate_0, back_0, mixed_grad_0, onehot, mask)
+    )(gathered_0, fbd_0, sbd_0, jnp.where(core == 0, full, full_other), gate_0, back_0, mixed_grad_0, onehot, mask)
 
     own = jnp.where(core == 0, grads_0, grads_1).astype(F32)
     parts = (own + swap(jnp.where(core == 0, grads_1, grads_0)).astype(F32)).astype(BF)
-    sums = summed(after(parts, returned_0), devices)
 
     input_0, right_grad_0 = call(
         last_kernel,
@@ -521,6 +476,7 @@
     input_grad = jnp.where(
         core == 0, jnp.stack([input_0, swap(input_0)]), jnp.stack([swap(input_1), input_1])
     )
+    sums = summed(after(parts, returned_0), devices, (input_grad, left_grad, right_grad))
     parts = 4
     first_grad, second_grad = call(
         unpack_kernel,
@@ -529,7 +485,8 @@
         (parts,),
         [pl.BlockSpec((devices // parts,) + owned[1:], lambda i: (i, 0, 0, 0))],
         [pl.BlockSpec((blocks // parts, side, side), lambda i: (i, 0, 0))] * 2,
-    )(after(sums, input_grad, left_grad, right_grad))
+        room=8,
+    )(sums)
     return (
         input_grad[None],
         right_grad[None, None],

time: 185 us -> 178 us (0.962)
  blocking collectives: 18.9 us -> 0 us
  waiting for transfers between devices: 52 us -> 64.7 us
  Pallas kernels: 63.3 us -> 51.6 us
  starting transfers between devices: 35.1 us -> 39.1 us
  other arithmetic: 6.3 us -> 10 us
  local copies, waits for them, and re-layouts: 7.64 us -> 9.52 us
    all_to_all x1 -> x0, blocking collectives: 18.9 us -> none  [exchanged(): lax.all_to_all(value, 'blk', split_axis=0, concat_axis=0, axis_index_grou...]
    all_to_all x1 -> x2, waiting for transfers between devices: 0.01 us -> 13.5 us  [exchanged(): lax.all_to_all(value, 'blk', split_axis=0, concat_axis=0, axis_index_grou...]
    pallas_call x4 -> x2, Pallas kernels: 17.5 us -> 7.32 us  [the longest x1 7.15 us: body(): call(forward_kernel, 'forward', [sds(act_shape, BF), sds(col_shape, BF),...]
    all_to_all x1 -> x2, starting transfers between devices: 3.56 us -> 8.83 us  [exchanged(): lax.all_to_all(value, 'blk', split_axis=0, concat_axis=0, axis_index_grou...]
    select_n x0 -> x3, other arithmetic: none -> 3.93 us  [the longest x1 2.68 us: body(): jnp.where(core == 0, kept, received)]
    squeeze x2 -> x3, local copies, waits for them, and re-layouts: 2.4 us -> 4.89 us  [the longest x2 2.59 us: body(): lax.dynamic_index_in_dim(whole_array, mine, 0, keepdims=False)]
    select_n x1, other arithmetic: 3.54 us -> 1.68 us  [body(): jnp.where(core == 0, jnp.stack([input_0, swap(input_0)]), jnp.stack([swap...]
    ppermute x10 -> x11, waiting for transfers between devices: 8.54 us -> 8.42 us  [swap(): return lax.ppermute(value, 'pipe', [(0, 1), (1, 0)])]
  transfers between devices with their start and end apart: 16 -> 18, of which waited for: 10 -> 13; matrix products, arithmetic and copies ran while one was open for 4% -> 7% of each run, Pallas kernels for 28% -> 28%
where the time goes in v3:
time: 178 us; the launch traced here: 177 us
  waiting for transfers between devices  64.7 us (36%)
  Pallas kernels  51.6 us (29%)
  starting transfers between devices  39.1 us (22%)
  other arithmetic  10 us (6%)
  local copies, waits for them, and re-layouts  9.52 us (5%)
    all_to_all x4, waiting for transfers between devices, exchange(): lax.all_to_all(chunks, 'blk', split_axis=0, concat_axis=0, tiled=True)  37.8 us
    all_to_all x4, starting transfers between devices, exchange(): lax.all_to_all(chunks, 'blk', split_axis=0, concat_axis=0, tiled=True)  26.3 us
    all_to_all x2, waiting for transfers between devices, exchanged(): lax.all_to_all(value, 'blk', split_axis=0, concat_axis=0, axis_index_grou...  13.5 us
    pallas_call x1, Pallas kernels, body(): call(turn_kernel, 'turn', [sds(act_shape, BF), sds((tokens, count), F32),...  11.2 us
    pallas_call x2, Pallas kernels, expand(): call(functools.partial(expand_kernel, section), 'expand', [sds(pair_shape...  10.1 us
    all_to_all x2, starting transfers between devices, exchanged(): lax.all_to_all(value, 'blk', split_axis=0, concat_axis=0, axis_index_grou...  8.83 us
    ppermute x11, waiting for transfers between devices, swap(): return lax.ppermute(value, 'pipe', [(0, 1), (1, 0)])  8.42 us
    pallas_call x1, Pallas kernels, body(): call(middle_kernel, 'middle', [sds(act_shape, BF), sds(act_shape, F32), s...  8.01 us
  transfers between devices with their start and end apart: 18, of which 13 were waited for; matrix products, arithmetic and copies ran while one was open for 7% of the time, Pallas kernels for 28%

profile of v3, /device:TPU:0, one launch (start us, length us, event | category | flops | bytes accessed | tf_op | source)
XLA Modules:
  0.0 177.4 jit_solution(3754887056374196027)
XLA Ops:
  0.6 0.0 copy-start
  0.6 0.0 copy-start.1
  0.7 2.3 %dynamic-slice_bitcast_fusion.2 = bf16[128,4096]{1,0:T(8,128)(2,1)} fusion(bf16[1,2,128,4096]{3,2,1,0:T(8,128)(2,1)} %param.9, s32[]{:T(128)S(6)} %select_n.94), kind=kLoop, calls=%fused_computation.6 | loop fusion | bytes 2097156 | tf_op jit(solution)/shard_map/jit(dynamic_index_in_dim)/squeeze | solution.py:318
  3.0 0.5 collective-permute-start
  3.4 0.2 left.1
  3.6 0.1 collective-permute-start.1
  3.7 1.3 dynamic-slice_bitcast_fusion
  5.0 1.3 dynamic-slice_bitcast_fusion.1.upstream
  6.3 0.0 copy-start.7
  6.4 0.5 multiply_convert_fusion
  6.8 0.5 copy-done.3
  7.3 0.3 copy-done.7
  7.6 1.4 convolution_convert_fusion
  9.1 8.4 %all-to-all-start.1 = ((bf16[16,8,4096]{2,1,0:T(8,128)(2,1)}), bf16[16,8,4096]{2,1,0:T(8,128)(2,1)}, u32[]{:S(2)}, u32[]{:S(2)}) async-start(bf16[16,8,4096]{2,1,0:T(8,128)(2,1)} %bitcast.40), calls=%async_computation.1 | async-start | bytes 2097152 | tf_op jit(solution)/shard_map/all_to_all | solution.py:287
  17.4 0.1 collective-permute-start.2
  17.5 0.5 collective-permute-start.3
  18.0 0.1 collective-permute-start.4
  18.1 2.7 %broadcast_select_fusion.1 = (bf16[128,4096]{1,0:T(8,128)(2,1)}, bf16[128,4096]{1,0:T(8,128)(2,1)}) fusion(bf16[128,4096]{1,0:T(8,128)(2,1)S(1)} %dynamic-slice_bitcast_fusion, bf16[128,4096]{1,0:T(8,128)(2,1)} %copy-done.7, pred[]{:T(512)S(6)} %eq.2), kind=kLoop, calls=%fused_computation.8 | loop fusion | flops 1048576 | bytes 4194305 | tf_op jit(solution)/shard_map/jit(_where)/select_n | solution.py:356
  20.8 0.2 collective-permute-done.3.first_other
  21.0 1.0 copy-done.6
  21.9 0.2 collective-permute-done.4.second_other
  22.2 5.1 %expand.2 = (bf16[32,128,128]{2,1,0:T(8,128)(2,1)}, bf16[32,128,128]{2,1,0:T(8,128)(2,1)}, bf16[32,128,128]{2,1,0:T(8,128)(2,1)}, bf16[32,128,128]{2,1,0:T(8,128)(2,1)}) custom-call(s32[1]{0:T(128)} %bitcast.p, bf16[64,64,64]{2,1,0:T(8,128)(2,1)} %bitcast.32, bf16[64,64,64]{2,1,0:T(8,128)(2,1)} %copy-done.6, bf16[64,64,64]{2,1,0:T(8,128)(2,1)} %bitcast.36, ...), custom_call_target="tpu_custom_call" | custom-call | flops 268435456 | bytes 8388608 | tf_op jit(solution)/shard_map/expand/pallas_call | solution.py:359
  27.2 0.6 copy-done.17
  27.8 7.1 %forward.1 = (bf16[128,4096]{1,0:T(8,128)(2,1)}, bf16[4096,128]{1,0:T(8,128)(2,1)}, bf16[128,4096]{1,0:T(8,128)(2,1)}, bf16[128,128]{1,0:T(8,128)(2,1)}, bf16[12...) custom-call(s32[1]{0:T(128)} %bitcast.p, bf16[128,4096]{1,0:T(8,128)(2,1)} %get-tuple-element.90.act, ...), custom_call_target="tpu_custom_call" | custom-call | flops 268435456 | bytes 8388608 | tf_op jit(solution)/shard_map/forward/pallas_call | solution.py:370
  35.0 7.1 %all-to-all-done.1 = bf16[16,8,4096]{2,1,0:T(8,128)(2,1)} async-done(((bf16[16,8,4096]{2,1,0:T(8,128)(2,1)}), bf16[16,8,4096]{2,1,0:T(8,128)(2,1)}, u32[]{:S(2)}, u32[]{:S(2)}) %all-to-all-start.1) | async-done | bytes 1048608 | tf_op jit(solution)/shard_map/all_to_all | solution.py:287
  42.1 5.9 %all-to-all-start = ((bf16[16,8,4096]{2,1,0:T(8,128)(2,1)}), bf16[16,8,4096]{2,1,0:T(8,128)(2,1)S(1)}, u32[]{:S(2)}, u32[]{:S(2)}) async-start(bf16[16,8,4096]{2,1,0:T(8,128)(2,1)} %bitcast.47), calls=%async_computation | async-start | bytes 2097152 | tf_op jit(solution)/shard_map/all_to_all | solution.py:287
  48.0 8.0 %middle.1 = (bf16[128,4096]{1,0:T(8,128)(2,1)}, f32[128,4096]{1,0:T(8,128)}, f32[128,128]{1,0:T(8,128)}, bf16[16,2,128,128]{3,2,1,0:T(8,128)(2,1)}) custom-call(bf16[128,4096]{1,0:T(8,128)(2,1)} %bitcast.11.back, bf16[32,128,128]{2,1,0:T(8,128)(2,1)} %get-tuple-element.57.second_bt, bf16[32,128,128]{2,1,0:T(8,128)(2,1)} %get-tuple-element.58.first_bt, ...), custom_call_target="tpu_custom_call" | custom-call | flops 268435456 | bytes 8388608 | tf_op jit(solution)/shard_map/middle/pallas_call | solution.py:392
  56.0 15.2 %all-to-all-done = bf16[16,8,4096]{2,1,0:T(8,128)(2,1)S(1)} async-done(((bf16[16,8,4096]{2,1,0:T(8,128)(2,1)}), bf16[16,8,4096]{2,1,0:T(8,128)(2,1)S(1)}, u32[]{:S(2)}, u32[]{:S(2)}) %all-to-all-start) | async-done | bytes 1048608 | tf_op jit(solution)/shard_map/all_to_all | solution.py:287
  71.2 1.0 copy-done.11
  72.2 5.9 %all-to-all-start.3 = ((bf16[16,8,4096]{2,1,0:T(8,128)(2,1)}), bf16[16,8,4096]{2,1,0:T(8,128)(2,1)S(1)}, u32[]{:S(2)}, u32[]{:S(2)}) async-start(bf16[16,8,4096]{2,1,0:T(8,128)(2,1)} %bitcast.45), calls=%async_computation.3 | async-start | bytes 2097152 | tf_op jit(solution)/shard_map/all_to_all | solution.py:287
  78.1 0.1 collective-permute-start.5
  78.2 0.6 broadcast_select_fusion.6.left_t_low
  78.8 0.6 collective-permute-done.5
  79.4 0.6 broadcast_select_fusion.5
  80.0 5.1 %expand.3 = (bf16[32,128,128]{2,1,0:T(8,128)(2,1)}, bf16[32,128,128]{2,1,0:T(8,128)(2,1)}, bf16[32,128,128]{2,1,0:T(8,128)(2,1)}, bf16[32,128,128]{2,1,0:T(8,128)(2,1)}) custom-call(s32[1]{0:T(128)} %bitcast.p, bf16[64,64,64]{2,1,0:T(8,128)(2,1)} %bitcast.33, bf16[64,64,64]{2,1,0:T(8,128)(2,1)} %copy-done.6, bf16[64,64,64]{2,1,0:T(8,128)(2,1)} %bitcast.37, ...), custom_call_target="tpu_custom_call" | custom-call | flops 268435456 | bytes 8388608 | tf_op jit(solution)/shard_map/expand/pallas_call | solution.py:359
  85.1 11.2 %turn.1 = (bf16[128,4096]{1,0:T(8,128)(2,1)}, f32[128,16]{1,0:T(8,128)}, bf16[128,4096]{1,0:T(8,128)(2,1)}, bf16[128,4096]{1,0:T(8,128)(2,1)}, bf16[4096,128]{1,0:T(8,128)(2,1)}, /*index=5*/bf16[128,4096]{1,0:T(8,128)(2,1)}) custom-call(bf16[128,4096]{1,0:T(8,128)(2,1)} %bitcast.41, bf16[128,4096]{1,0:T(8,128)(2,1)} %copy-done.3, ...), custom_call_target="tpu_custom_call" | custom-call | flops 268435456 | bytes 8388608 | tf_op jit(solution)/shard_map/turn/pallas_call | solution.py:403
  96.2 4.7 %all-to-all-done.3 = bf16[16,8,4096]{2,1,0:T(8,128)(2,1)S(1)} async-done(((bf16[16,8,4096]{2,1,0:T(8,128)(2,1)}), bf16[16,8,4096]{2,1,0:T(8,128)(2,1)S(1)}, u32[]{:S(2)}, u32[]{:S(2)}) %all-to-all-start.3) | async-done | bytes 1048608 | tf_op jit(solution)/shard_map/all_to_all | solution.py:287
  100.9 6.1 %all-to-all-start.2 = ((bf16[16,8,4096]{2,1,0:T(8,128)(2,1)}), bf16[16,8,4096]{2,1,0:T(8,128)(2,1)}, u32[]{:S(2)}, u32[]{:S(2)}) async-start(bf16[16,8,4096]{2,1,0:T(8,128)(2,1)} %bitcast.46), calls=%async_computation.2 | async-start | bytes 2097152 | tf_op jit(solution)/shard_map/all_to_all | solution.py:287
  107.0 7.7 %lower.1 = (f32[128,4096]{1,0:T(8,128)}, f32[128,16]{1,0:T(8,128)}, bf16[16,2,128,128]{3,2,1,0:T(8,128)(2,1)}) custom-call(bf16[128,4096]{1,0:T(8,128)(2,1)} %bitcast.39, bf16[32,128,128]{2,1,0:T(8,128)(2,1)} %get-tuple-element.72.first_bd, bf16[32,128,128]{2,1,0:T(8,128)(2,1)} %get-tuple-element.73.second_bd, bf16[128,128]{1,0:T(8,128)(2,1)} %get-tuple-element.91.left, ...), custom_call_target="tpu_custom_call" | custom-call | flops 268435456 | bytes 8388608 | tf_op jit(solution)/shard_map/lower/pallas_call | solution.py:449
  114.7 0.1 broadcast_select_fusion
  114.8 0.1 collective-permute-start.10
  114.9 2.6 %collective-permute-done.10 = bf16[16,2,128,128]{3,2,1,0:T(8,128)(2,1)S(1)} collective-permute-done((bf16[16,2,128,128]{3,2,1,0:T(8,128)(2,1)S(1)}, bf16[16,2,128,128]{3,2,1,0:T(8,128)(2,1)S(1)}, u32[]{:S(2)}, u32[]{:S(2)}) %collective-permute-start.10) | collective-permute-done | bytes 1048608 | tf_op jit(solution)/shard_map/ppermute | solution.py:278
  117.6 1.5 add_convert_fusion
  119.1 10.8 %all-to-all-done.2 = bf16[16,8,4096]{2,1,0:T(8,128)(2,1)} async-done(((bf16[16,8,4096]{2,1,0:T(8,128)(2,1)}), bf16[16,8,4096]{2,1,0:T(8,128)(2,1)}, u32[]{:S(2)}, u32[]{:S(2)}) %all-to-all-start.2) | async-done | bytes 1048608 | tf_op jit(solution)/shard_map/all_to_all | solution.py:287
  129.9 5.0 %all-to-all-start.4 = ((bf16[8,4,128,128]{3,2,1,0:T(8,128)(2,1)}), bf16[8,4,128,128]{3,2,1,0:T(8,128)(2,1)S(1)}, u32[]{:S(2)}, u32[]{:S(2)}) async-start(bf16[8,4,128,128]{3,2,1,0:T(8,128)(2,1)} %bitcast.22), calls=%async_computation.4 | async-start | bytes 2097152 | tf_op jit(solution)/shard_map/all_to_all | solution.py:297
  134.9 4.7 %last.1 = (bf16[128,4096]{1,0:T(8,128)(2,1)}, f32[128,128]{1,0:T(8,128)}) custom-call(bf16[128,4096]{1,0:T(8,128)(2,1)} %bitcast.13.received, bf16[128,128]{1,0:T(8,128)(2,1)} %get-tuple-element.69.right_t, bf16[128,4096]{1,0:T(8,128)(2,1)} %get-tuple-element.70.upstream, f32[128,4096]{1,0:T(8,128)} %get-tuple-element.77.carried, ...), custom_call_target="tpu_custom_call" | custom-call | flops 268435456 | bytes 8388608 | tf_op jit(solution)/shard_map/last/pallas_call | solution.py:462
  139.7 0.1 collective-permute-start.8
  139.8 1.2 collective-permute-done.8
  141.0 1.5 select_add_fusion.1
  142.5 6.1 %all-to-all-done.4 = bf16[8,4,128,128]{3,2,1,0:T(8,128)(2,1)S(1)} async-done(((bf16[8,4,128,128]{3,2,1,0:T(8,128)(2,1)}), bf16[8,4,128,128]{3,2,1,0:T(8,128)(2,1)S(1)}, u32[]{:S(2)}, u32[]{:S(2)}) %all-to-all-start.4) | async-done | bytes 1048608 | tf_op jit(solution)/shard_map/all_to_all | solution.py:297
  148.6 0.1 reduce_sum.12
  148.7 0.0 copy-start.12
  148.8 1.9 %collective-permute-start.11 = (bf16[4,128,128]{2,1,0:T(8,128)(2,1)S(1)}, bf16[4,128,128]{2,1,0:T(8,128)(2,1)S(1)}, u32[]{:S(2)}, u32[]{:S(2)}) collective-permute-start(bf16[4,128,128]{2,1,0:T(8,128)(2,1)S(1)} %reduce_sum.12), channel_id=1, source_target_pairs={{0,24},{2,26},{4,28},{6,30},{8,16},{10,18},{12,20},{14,22},{16,8},... | collective-permute-start | bytes 393224 | tf_op jit(solution)/shard_map/ppermute | solution.py:302
  150.7 5.0 %collective-permute-done.11 = bf16[4,128,128]{2,1,0:T(8,128)(2,1)S(1)} collective-permute-done((bf16[4,128,128]{2,1,0:T(8,128)(2,1)S(1)}, bf16[4,128,128]{2,1,0:T(8,128)(2,1)S(1)}, u32[]{:S(2)}, u32[]{:S(2)}) %collective-permute-start.11) | collective-permute-done | bytes 131104 | tf_op jit(solution)/shard_map/ppermute | solution.py:302
  155.7 1.2 broadcast_in_dim.17
  156.9 3.8 %all-to-all-start.5 = ((bf16[8,4,128,128]{3,2,1,0:T(8,128)(2,1)}), bf16[8,4,128,128]{3,2,1,0:T(8,128)(2,1)S(1)}, u32[]{:S(2)}, u32[]{:S(2)}) async-start(bf16[8,4,128,128]{3,2,1,0:T(8,128)(2,1)} %broadcast_in_dim.17), calls=%async_computation.5 | async-start | bytes 2097152 | tf_op jit(solution)/shard_map/all_to_all | solution.py:297
  160.8 0.1 collective-permute-start.7
  160.9 0.5 collective-permute-start.6
  161.4 0.2 collective-permute-start.9
  161.5 3.6 %collective-permute-done.9 = f32[128,16]{1,0:T(8,128)S(1)} collective-permute-done((f32[128,16]{1,0:T(8,128)S(1)}, f32[128,16]{1,0:T(8,128)S(1)}, u32[]{:S(2)}, u32[]{:S(2)}) %collective-permute-start.9) | collective-permute-done | bytes 8224 | tf_op jit(solution)/shard_map/ppermute | solution.py:278
  165.1 0.6 select_add_fusion
  165.8 1.7 maximum_select_fusion
  167.4 7.4 %all-to-all-done.5 = bf16[8,4,128,128]{3,2,1,0:T(8,128)(2,1)S(1)} async-done(((bf16[8,4,128,128]{3,2,1,0:T(8,128)(2,1)}), bf16[8,4,128,128]{3,2,1,0:T(8,128)(2,1)S(1)}, u32[]{:S(2)}, u32[]{:S(2)}) %all-to-all-start.5) | async-done | bytes 1048608 | tf_op jit(solution)/shard_map/all_to_all | solution.py:297
  174.9 2.5 %unpack.1 = (f32[64,64,64]{2,1,0:T(8,128)}, f32[64,64,64]{2,1,0:T(8,128)}) custom-call(bf16[16,2,128,128]{3,2,1,0:T(8,128)(2,1)S(1)} %bitcast.30), custom_call_target="tpu_custom_call" | custom-call | flops 268435456 | bytes 8388608 | tf_op jit(solution)/shard_map/unpack/pallas_call | solution.py:481
  (35 shorter events, 0.1 us)
Async XLA Ops:
  0.6 2.8 %copy-start = (bf16[128,16]{1,0:T(8,128)(2,1)S(1)}, bf16[128,16]{1,0:T(8,128)(2,1)}, u32[]{:S(2)}) copy-start(bf16[128,16]{1,0:T(8,128)(2,1)} %constant.31.clone.onehot) | copy-start | bytes 12292
  0.6 2.8 %copy-start.1 = (bf16[128,128]{1,0:T(8,128)(2,1)S(1)}, bf16[128,128]{1,0:T(8,128)(2,1)}, u32[]{:S(2)}) copy-start(bf16[128,128]{1,0:T(8,128)(2,1)} %constant.30.clone.mask) | copy-start | bytes 98308
  0.7 2.8 %copy-start.2 = (bf16[1,8,16,16]{3,2,1,0:T(8,128)(2,1)S(1)}, bf16[1,8,16,16]{3,2,1,0:T(8,128)(2,1)}, u32[]{:S(2)}) copy-start(bf16[1,8,16,16]{3,2,1,0:T(8,128)(2,1)} %param.12) | copy-start | bytes 12292
  3.0 3.4 %collective-permute-start = (bf16[128,4096]{1,0:T(8,128)(2,1)}, bf16[128,4096]{1,0:T(8,128)(2,1)S(1)}, u32[]{:S(2)}, u32[]{:S(2)}) collective-permute-start(bf16[128,4096]{1,0:T(8,128)(2,1)} %dynamic-slice_bitcast_fusion.2), channel_id=1, source_target_pairs={{0,1},{1,0},{2,3},{3,2},{4,5},{5,4},{6,7},{7,6},{8,9},{9,8},{10,11... | collective-permute-start | bytes 3145736 | tf_op jit(solution)/shard_map/ppermute | solution.py:278
  3.6 4.0 %collective-permute-start.1 = (bf16[128,128]{1,0:T(8,128)(2,1)S(1)}, bf16[128,128]{1,0:T(8,128)(2,1)S(1)}, u32[]{:S(2)}, u32[]{:S(2)}) collective-permute-start(bf16[128,128]{1,0:T(8,128)(2,1)S(1)} %get-tuple-element.49), channel_id=1, source_target_pairs={{0,1},{1,0},{2,3},{3,2},{4,5},{5,4},{6,7},{7,6},{8,9},{9,8},{10,11... | collective-permute-start | bytes 98312 | tf_op jit(solution)/shard_map/ppermute | solution.py:278
  6.3 1.0 copy-start.3
  6.3 1.3 copy-start.7
  7.6 9.8 %copy-start.16 = (bf16[1,1,128,128]{3,2,1,0:T(8,128)(2,1)S(1)}, bf16[1,1,128,128]{3,2,1,0:T(8,128)(2,1)}, u32[]{:S(2)}) copy-start(bf16[1,1,128,128]{3,2,1,0:T(8,128)(2,1)} %param.11) | copy-start | bytes 98308
  7.6 9.9 %copy-start.4 = (bf16[1,64,64,64]{3,2,1,0:T(8,128)(2,1)S(1)}, bf16[1,64,64,64]{3,2,1,0:T(8,128)(2,1)}, u32[]{:S(2)}) copy-start(bf16[1,64,64,64]{3,2,1,0:T(8,128)(2,1)} %param.13) | copy-start | bytes 1572868
  9.1 33.0 %all-to-all-start.1 = ((bf16[16,8,4096]{2,1,0:T(8,128)(2,1)}), bf16[16,8,4096]{2,1,0:T(8,128)(2,1)}, u32[]{:S(2)}, u32[]{:S(2)}) async-start(bf16[16,8,4096]{2,1,0:T(8,128)(2,1)} %bitcast.40), calls=%async_computation.1 | async-start | bytes 2097152 | tf_op jit(solution)/shard_map/all_to_all | solution.py:287
  17.4 9.8 %collective-permute-start.2 = (bf16[128,128]{1,0:T(8,128)(2,1)S(1)}, bf16[128,128]{1,0:T(8,128)(2,1)S(1)}, u32[]{:S(2)}, u32[]{:S(2)}) collective-permute-start(bf16[128,128]{1,0:T(8,128)(2,1)S(1)} %bitcast.51), channel_id=1, source_target_pairs={{0,1},{1,0},{2,3},{3,2},{4,5},{5,4},{6,7},{7,6},{8,9},{9,8},{10,11... | collective-permute-start | bytes 98312 | tf_op jit(solution)/shard_map/ppermute | solution.py:278
  17.5 3.4 %collective-permute-start.3 = (bf16[64,64,64]{2,1,0:T(8,128)(2,1)S(1)}, bf16[64,64,64]{2,1,0:T(8,128)(2,1)S(1)}, u32[]{:S(2)}, u32[]{:S(2)}) collective-permute-start(bf16[64,64,64]{2,1,0:T(8,128)(2,1)S(1)} %bitcast.34), channel_id=1, source_target_pairs={{0,1},{1,0},{2,3},{3,2},{4,5},{5,4},{6,7},{7,6},{8,9},{9,8},{10,11... | collective-permute-start | bytes 1572872 | tf_op jit(solution)/shard_map/ppermute | solution.py:278
  18.0 4.1 %collective-permute-start.4 = (bf16[64,64,64]{2,1,0:T(8,128)(2,1)}, bf16[64,64,64]{2,1,0:T(8,128)(2,1)}, u32[]{:S(2)}, u32[]{:S(2)}) collective-permute-start(bf16[64,64,64]{2,1,0:T(8,128)(2,1)} %bitcast.35), channel_id=1, source_target_pairs={{0,1},{1,0},{2,3},{3,2},{4,5},{5,4},{6,7},{7,6},{8,9},{9,8},{10,11... | collective-permute-start | bytes 1572872 | tf_op jit(solution)/shard_map/ppermute | solution.py:278
  20.9 1.0 copy-start.6
  27.2 0.6 copy-start.17
  42.1 29.1 %all-to-all-start = ((bf16[16,8,4096]{2,1,0:T(8,128)(2,1)}), bf16[16,8,4096]{2,1,0:T(8,128)(2,1)S(1)}, u32[]{:S(2)}, u32[]{:S(2)}) async-start(bf16[16,8,4096]{2,1,0:T(8,128)(2,1)} %bitcast.47), calls=%async_computation | async-start | bytes 2097152 | tf_op jit(solution)/shard_map/all_to_all | solution.py:287
  71.2 1.0 copy-start.11
  72.2 28.8 %all-to-all-start.3 = ((bf16[16,8,4096]{2,1,0:T(8,128)(2,1)}), bf16[16,8,4096]{2,1,0:T(8,128)(2,1)S(1)}, u32[]{:S(2)}, u32[]{:S(2)}) async-start(bf16[16,8,4096]{2,1,0:T(8,128)(2,1)} %bitcast.45), calls=%async_computation.3 | async-start | bytes 2097152 | tf_op jit(solution)/shard_map/all_to_all | solution.py:287
  78.1 1.3 collective-permute-start.5
  100.9 6.1 %copy-start.9 = (bf16[16,8,4096]{2,1,0:T(8,128)(2,1)}, bf16[16,8,4096]{2,1,0:T(8,128)(2,1)S(1)}, u32[]{:S(2)}) copy-start(bf16[16,8,4096]{2,1,0:T(8,128)(2,1)S(1)} %all-to-all-done.3) | copy-start | bytes 3145732
  100.9 29.0 %all-to-all-start.2 = ((bf16[16,8,4096]{2,1,0:T(8,128)(2,1)}), bf16[16,8,4096]{2,1,0:T(8,128)(2,1)}, u32[]{:S(2)}, u32[]{:S(2)}) async-start(bf16[16,8,4096]{2,1,0:T(8,128)(2,1)} %bitcast.46), calls=%async_computation.2 | async-start | bytes 2097152 | tf_op jit(solution)/shard_map/all_to_all | solution.py:287
  107.0 7.7 %copy-start.8 = (bf16[16,2,128,128]{3,2,1,0:T(8,128)(2,1)S(1)}, bf16[16,2,128,128]{3,2,1,0:T(8,128)(2,1)}, u32[]{:S(2)}) copy-start(bf16[16,2,128,128]{3,2,1,0:T(8,128)(2,1)} %get-tuple-element.84) | copy-start | bytes 3145732
  114.7 2.9 %copy-start.10 = (bf16[16,2,128,128]{3,2,1,0:T(8,128)(2,1)S(1)}, bf16[16,2,128,128]{3,2,1,0:T(8,128)(2,1)}, u32[]{:S(2)}) copy-start(bf16[16,2,128,128]{3,2,1,0:T(8,128)(2,1)} %get-tuple-element.83) | copy-start | bytes 3145732
  114.8 2.7 %collective-permute-start.10 = (bf16[16,2,128,128]{3,2,1,0:T(8,128)(2,1)S(1)}, bf16[16,2,128,128]{3,2,1,0:T(8,128)(2,1)S(1)}, u32[]{:S(2)}, u32[]{:S(2)}) collective-permute-start(bf16[16,2,128,128]{3,2,1,0:T(8,128)(2,1)S(1)} %broadcast_select_fusion), channel_id=1, source_target_pairs={{0,1},{1,0},{2,3},{3,2},{4,5},{5,4},{6,7},{7,6},{8,9},{9,8},{10,11... | collective-permute-start | bytes 3145736 | tf_op jit(solution)/shard_map/ppermute | solution.py:278
  129.9 18.6 %all-to-all-start.4 = ((bf16[8,4,128,128]{3,2,1,0:T(8,128)(2,1)}), bf16[8,4,128,128]{3,2,1,0:T(8,128)(2,1)S(1)}, u32[]{:S(2)}, u32[]{:S(2)}) async-start(bf16[8,4,128,128]{3,2,1,0:T(8,128)(2,1)} %bitcast.22), calls=%async_computation.4 | async-start | bytes 2097152 | tf_op jit(solution)/shard_map/all_to_all | solution.py:297
  134.9 4.8 %copy-start.14 = (f32[128,128]{1,0:T(8,128)S(1)}, f32[128,128]{1,0:T(8,128)}, u32[]{:S(2)}) copy-start(f32[128,128]{1,0:T(8,128)} %get-tuple-element.80) | copy-start | bytes 196612
  139.7 1.3 collective-permute-start.8
  148.7 12.1 %copy-start.5 = (bf16[128,4096]{1,0:T(8,128)(2,1)S(1)}, bf16[128,4096]{1,0:T(8,128)(2,1)}, u32[]{:S(2)}) copy-start(bf16[128,4096]{1,0:T(8,128)(2,1)} %get-tuple-element.70.upstream) | copy-start | bytes 3145732
  148.7 12.2 %copy-start.12 = (bf16[128,4096]{1,0:T(8,128)(2,1)S(1)}, bf16[128,4096]{1,0:T(8,128)(2,1)}, u32[]{:S(2)}) copy-start(bf16[128,4096]{1,0:T(8,128)(2,1)} %get-tuple-element.78) | copy-start | bytes 3145732
  148.7 12.6 %copy-start.13 = (f32[128,16]{1,0:T(8,128)S(1)}, f32[128,16]{1,0:T(8,128)}, u32[]{:S(2)}) copy-start(f32[128,16]{1,0:T(8,128)} %get-tuple-element.82) | copy-start | bytes 24580
  148.7 12.6 %copy-start.15 = (f32[128,16]{1,0:T(8,128)S(1)}, f32[128,16]{1,0:T(8,128)}, u32[]{:S(2)}) copy-start(f32[128,16]{1,0:T(8,128)} %get-tuple-element.81) | copy-start | bytes 24580
  148.8 6.9 %collective-permute-start.11 = (bf16[4,128,128]{2,1,0:T(8,128)(2,1)S(1)}, bf16[4,128,128]{2,1,0:T(8,128)(2,1)S(1)}, u32[]{:S(2)}, u32[]{:S(2)}) collective-permute-start(bf16[4,128,128]{2,1,0:T(8,128)(2,1)S(1)} %reduce_sum.12), channel_id=1, source_target_pairs={{0,24},{2,26},{4,28},{6,30},{8,16},{10,18},{12,20},{14,22},{16,8},... | collective-permute-start | bytes 393224 | tf_op jit(solution)/shard_map/ppermute | solution.py:302
  156.9 17.9 %all-to-all-start.5 = ((bf16[8,4,128,128]{3,2,1,0:T(8,128)(2,1)}), bf16[8,4,128,128]{3,2,1,0:T(8,128)(2,1)S(1)}, u32[]{:S(2)}, u32[]{:S(2)}) async-start(bf16[8,4,128,128]{3,2,1,0:T(8,128)(2,1)} %broadcast_in_dim.17), calls=%async_computation.5 | async-start | bytes 2097152 | tf_op jit(solution)/shard_map/all_to_all | solution.py:297
  160.8 5.0 %collective-permute-start.7 = (bf16[128,4096]{1,0:T(8,128)(2,1)S(1)}, bf16[128,4096]{1,0:T(8,128)(2,1)S(1)}, u32[]{:S(2)}, u32[]{:S(2)}) collective-permute-start(bf16[128,4096]{1,0:T(8,128)(2,1)S(1)} %copy-done.5), channel_id=1, source_target_pairs={{0,1},{1,0},{2,3},{3,2},{4,5},{5,4},{6,7},{7,6},{8,9},{9,8},{10,11... | collective-permute-start | bytes 3145736 | tf_op jit(solution)/shard_map/ppermute | solution.py:278
  160.9 4.9 %collective-permute-start.6 = (bf16[128,4096]{1,0:T(8,128)(2,1)S(1)}, bf16[128,4096]{1,0:T(8,128)(2,1)S(1)}, u32[]{:S(2)}, u32[]{:S(2)}) collective-permute-start(bf16[128,4096]{1,0:T(8,128)(2,1)S(1)} %copy-done.12), channel_id=1, source_target_pairs={{0,1},{1,0},{2,3},{3,2},{4,5},{5,4},{6,7},{7,6},{8,9},{9,8},{10,11... | collective-permute-start | bytes 3145736 | tf_op jit(solution)/shard_map/ppermute | solution.py:278
  161.4 3.7 %collective-permute-start.9 = (f32[128,16]{1,0:T(8,128)S(1)}, f32[128,16]{1,0:T(8,128)S(1)}, u32[]{:S(2)}, u32[]{:S(2)}) collective-permute-start(f32[128,16]{1,0:T(8,128)S(1)} %broadcast_select_fusion.3), channel_id=1, source_target_pairs={{0,1},{1,0},{2,3},{3,2},{4,5},{5,4},{6,7},{7,6},{8,9},{9,8},{10,11... | collective-permute-start | bytes 24584 | tf_op jit(solution)/shard_map/ppermute | solution.py:278

commit v4 on v3

--- a/solution.py
+++ b/solution.py
@@ -105,6 +105,7 @@
     first_bd,
     second_bd,
     eye,
+    order,
     rows,
     mixed,
     right_act,
@@ -113,8 +114,8 @@
     right_0,
     wide,
 ):
-    low = pick(p, right_own[...], right_other[...]).astype(BF)
-    high = pick(p, right_other[...], right_own[...]).astype(BF)
+    low = mm(order[...], pick(p, right_own[...], right_other[...]).astype(BF)).astype(BF)
+    high = mm(order[...], pick(p, right_other[...], right_own[...]).astype(BF)).astype(BF)
     right_0[...] = low
     right_t_0[...] = low.astype(F32).T.astype(BF)
     right_t_1[...] = high.astype(F32).T.astype(BF)
@@ -139,6 +140,7 @@
     act,
     right_low,
     act_low,
+    order,
     right_act_low,
     chan_back,
     right_grad,
@@ -157,7 +159,7 @@
         piece = mm(first_bt[q], pair).astype(BF)
         turned[columns(q), :] = piece
         chan_back[:, columns(q)] = mm(right_t[...], piece, NT)
-    right_grad[...] = mm(act[...], turned[...]).T
+    right_grad[...] = mm(order[...].astype(F32).T, mm(act[...], turned[...]), NT, lax.Precision.HIGHEST)
 
 
 def turn_kernel(
@@ -250,7 +252,7 @@
     left_grad[...] = mm(term * mask[...].astype(F32), onehot[...].astype(F32), precision=lax.Precision.HIGHEST)
 
 
-def last_kernel(received, right_t, upstream, carried, act, input_grad, right_grad):
+def last_kernel(received, right_t, order, upstream, carried, act, input_grad, right_grad, right_acc):
     step = pl.program_id(0)
     chan_back = mm(right_t[...], received[...])
     input_grad[...] = (upstream[...].astype(F32) * carried[...] + chan_back).astype(BF)
@@ -258,11 +260,15 @@
 
     @pl.when(step == 0)
     def _():
-        right_grad[...] = term
+        right_acc[...] = term
 
     @pl.when(step > 0)
     def _():
-        right_grad[...] += term
+        right_acc[...] += term
+
+    @pl.when(step == pl.num_programs(0) - 1)
+    def _():
+        right_grad[...] = mm(order[...].astype(F32).T, right_acc[...], precision=lax.Precision.HIGHEST)
 
 
 def unpack_kernel(sums, first, second):
@@ -282,15 +288,20 @@
     return lax.optimization_barrier((value, *others))[0]
 
 
+def ring(devices):
+    return [10, 7, 4, 1, 11, 12, 5, 3, 15, 0, 14, 6, 8, 2, 13, 9] if devices == 16 else list(range(devices))
+
+
 def exchange(rows, devices):
     chunks = rows.reshape(devices, rows.shape[0] // devices, *rows.shape[1:])
-    return lax.all_to_all(chunks, "blk", split_axis=0, concat_axis=0, tiled=True).reshape(rows.shape)
+    came = lax.all_to_all(chunks, "blk", split_axis=0, concat_axis=0, axis_index_groups=[ring(devices)], tiled=True)
+    return came.reshape(rows.shape)
 
 
 def summed(parts, devices, others):
     far = 12 if devices == 16 else 0
     members = devices // 2 if far else devices
-    groups = [[member ^ f for member in range(members)] for f in ((0, far) if far else (0,))]
+    groups = [[member ^ f for member in ((3, 5, 0, 4, 1, 6, 7, 2) if far else range(members))] for f in ((0, far) if far else (0,))]
     shape = (members, devices // members * parts.shape[1]) + parts.shape[2:]
 
     def exchanged(value):
@@ -324,7 +335,9 @@
 
     place = np.arange(tokens)
     mask = jnp.asarray(place[:, None] // count == place[None, :] % per, BF)
-    onehot = jnp.asarray(place[:, None] // per == np.arange(count)[None, :], BF)
+    whose = np.repeat(ring(devices), per)
+    onehot = jnp.asarray(whose[:, None] == np.arange(count)[None, :], BF)
+    order = jnp.asarray((whose * per + place % per)[:, None] == place[None, :], BF)
     eye = jnp.asarray(np.eye(tokens), BF)
 
     step = width // 4
@@ -372,7 +385,7 @@
         "forward",
         [sds(act_shape, BF), sds(col_shape, BF), sds(act_shape, BF)] + [squared] * 3,
         (1,),
-        [act_full, square, square, pair_full, pair_full, square],
+        [act_full, square, square, pair_full, pair_full, square, square],
         [act_full, col_full, act_full] + [square] * 3,
         [pltpu.VMEM(col_shape, F32)],
         scalars=1,
@@ -384,6 +397,7 @@
         fbd_1,
         sbd_1,
         eye,
+        order,
     )
     gathered_1 = exchange(rows_1, devices)
     p = after(p, rows_1)
@@ -394,10 +408,10 @@
         "middle",
         [sds(act_shape, BF), sds(act_shape, F32), sds((span, span), F32), sds(owned, BF)],
         (1,),
-        [act_full, pair_full, pair_full, col_full, act_full, square, act_full, square, act_full],
+        [act_full, pair_full, pair_full, col_full, act_full, square, act_full, square, act_full, square],
         [act_full, act_full, square, whole(owned)],
         [pltpu.VMEM(col_shape, F32), pltpu.VMEM(col_shape, BF)],
-    )(returned_1, sbt_1, fbt_1, mixed_1, right_act_1, right_t_1, act_1, right_0, act_0)
+    )(returned_1, sbt_1, fbt_1, mixed_1, right_act_1, right_t_1, act_1, right_0, act_0, order)
     gathered_0 = exchange(right_act_0, devices)
 
     input_1, left_grad_1, gate_0, back_0, mixed_grad_0, sent_0 = call(
@@ -464,9 +478,10 @@
         "last",
         [sds(act_shape, BF), sds((span, span), F32)],
         (width // step,),
-        [moving, square, moving, moving, moving],
+        [moving, square, square, moving, moving, moving],
         [moving, square],
-    )(returned_0, right_t_0, input_1, carried_0, act_0)
+        [pltpu.VMEM((span, span), F32)],
+    )(returned_0, right_t_0, order, input_1, carried_0, act_0)
 
     def to_section(low, high):
         return jnp.where(core == 0, low, high) + swap(jnp.where(core == 0, high, low))

time: 178 us -> 174 us (0.978)
  waiting for transfers between devices: 64.7 us -> 55.4 us
  starting transfers between devices: 39.1 us -> 43.9 us
    all_to_all x4, waiting for transfers between devices: 37.8 us -> 31.3 us  [exchange(): lax.all_to_all(chunks, 'blk', split_axis=0, concat_axis=0, axis_index_gro...]
    all_to_all x4, starting transfers between devices: 26.3 us -> 29.7 us  [exchange(): lax.all_to_all(chunks, 'blk', split_axis=0, concat_axis=0, axis_index_gro...]
  transfers between devices with their start and end apart: 18 -> 18, of which waited for: 13 -> 13; matrix products, arithmetic and copies ran while one was open for 7% -> 7% of each run, Pallas kernels for 28% -> 29%
where the time goes in v4:
time: 174 us; the launch traced here: 173 us
  waiting for transfers between devices  55.4 us (32%)
  Pallas kernels  51.9 us (30%)
  starting transfers between devices  43.9 us (25%)
  other arithmetic  10 us (6%)
  local copies, waits for them, and re-layouts  9.52 us (5%)
    all_to_all x4, waiting for transfers between devices, exchange(): lax.all_to_all(chunks, 'blk', split_axis=0, concat_axis=0, axis_index_gro...  31.3 us
    all_to_all x4, starting transfers between devices, exchange(): lax.all_to_all(chunks, 'blk', split_axis=0, concat_axis=0, axis_index_gro...  29.7 us
    all_to_all x2, waiting for transfers between devices, exchanged(): lax.all_to_all(value, 'blk', split_axis=0, concat_axis=0, axis_index_grou...  11.8 us
    pallas_call x1, Pallas kernels, body(): call(turn_kernel, 'turn', [sds(act_shape, BF), sds((tokens, count), F32),...  11.2 us
    pallas_call x2, Pallas kernels, expand(): call(functools.partial(expand_kernel, section), 'expand', [sds(pair_shape...  10.1 us
    all_to_all x2, starting transfers between devices, exchanged(): lax.all_to_all(value, 'blk', split_axis=0, concat_axis=0, axis_index_grou...  9.22 us
    ppermute x11, waiting for transfers between devices, swap(): return lax.ppermute(value, 'pipe', [(0, 1), (1, 0)])  8.43 us
    pallas_call x1, Pallas kernels, body(): call(middle_kernel, 'middle', [sds(act_shape, BF), sds(act_shape, F32), s...  8.04 us
  transfers between devices with their start and end apart: 18, of which 13 were waited for; matrix products, arithmetic and copies ran while one was open for 7% of the time, Pallas kernels for 29%

profile of v4, /device:TPU:0, one launch (start us, length us, event | category | flops | bytes accessed | tf_op | source)
XLA Modules:
  0.0 173.1 jit_solution(3778379800856184566)
XLA Ops:
  0.6 0.0 copy-start
  0.6 0.0 copy-start.1
  0.7 2.3 %dynamic-slice_bitcast_fusion.2 = bf16[128,4096]{1,0:T(8,128)(2,1)} fusion(bf16[1,2,128,4096]{3,2,1,0:T(8,128)(2,1)} %param.10, s32[]{:T(128)S(6)} %select_n.94), kind=kLoop, calls=%fused_computation.6 | loop fusion | bytes 2097156 | tf_op jit(solution)/shard_map/jit(dynamic_index_in_dim)/squeeze | solution.py:329
  3.0 0.5 collective-permute-start
  3.4 0.2 left.1
  3.6 0.1 collective-permute-start.1
  3.7 1.3 dynamic-slice_bitcast_fusion
  5.0 1.3 dynamic-slice_bitcast_fusion.1.upstream
  6.3 0.0 collective-permute-done
  6.3 0.0 copy-start.6
  6.4 0.5 multiply_convert_fusion
  6.8 0.5 copy-done.3
  7.3 0.3 copy-done.6
  7.6 1.4 convolution_convert_fusion
  9.1 9.1 %all-to-all-start.1 = ((bf16[16,8,4096]{2,1,0:T(8,128)(2,1)}), bf16[16,8,4096]{2,1,0:T(8,128)(2,1)}, u32[]{:S(2)}, u32[]{:S(2)}) async-start(bf16[16,8,4096]{2,1,0:T(8,128)(2,1)} %bitcast.39), calls=%async_computation.1 | async-start | bytes 2097152 | tf_op jit(solution)/shard_map/all_to_all | solution.py:297
  18.2 0.1 collective-permute-start.2
  18.3 0.5 collective-permute-start.3
  18.8 0.1 collective-permute-start.4
  18.9 2.7 %broadcast_select_fusion.1 = (bf16[128,4096]{1,0:T(8,128)(2,1)}, bf16[128,4096]{1,0:T(8,128)(2,1)}) fusion(bf16[128,4096]{1,0:T(8,128)(2,1)S(1)} %dynamic-slice_bitcast_fusion, bf16[128,4096]{1,0:T(8,128)(2,1)} %copy-done.6, pred[]{:T(512)S(6)} %eq.2), kind=kLoop, calls=%fused_computation.8 | loop fusion | flops 1048576 | bytes 4194305 | tf_op jit(solution)/shard_map/jit(_where)/select_n | solution.py:369
  21.5 0.2 collective-permute-done.3.first_other
  21.7 1.0 copy-done.5
  22.7 0.2 collective-permute-done.4.second_other
  22.9 5.1 %expand.2 = (bf16[32,128,128]{2,1,0:T(8,128)(2,1)}, bf16[32,128,128]{2,1,0:T(8,128)(2,1)}, bf16[32,128,128]{2,1,0:T(8,128)(2,1)}, bf16[32,128,128]{2,1,0:T(8,128)(2,1)}) custom-call(s32[1]{0:T(128)} %bitcast.p, bf16[64,64,64]{2,1,0:T(8,128)(2,1)} %bitcast.32, bf16[64,64,64]{2,1,0:T(8,128)(2,1)} %copy-done.5, bf16[64,64,64]{2,1,0:T(8,128)(2,1)} %bitcast.36, ...), custom_call_target="tpu_custom_call" | custom-call | flops 268435456 | bytes 8388608 | tf_op jit(solution)/shard_map/expand/pallas_call | solution.py:372
  28.0 0.6 copy-done.17
  28.6 7.2 %forward.1 = (bf16[128,4096]{1,0:T(8,128)(2,1)}, bf16[4096,128]{1,0:T(8,128)(2,1)}, bf16[128,4096]{1,0:T(8,128)(2,1)}, bf16[128,128]{1,0:T(8,128)(2,1)}, bf16[12...) custom-call(s32[1]{0:T(128)} %bitcast.p, bf16[128,4096]{1,0:T(8,128)(2,1)} %get-tuple-element.90.act, ...), custom_call_target="tpu_custom_call" | custom-call | flops 268435456 | bytes 8388608 | tf_op jit(solution)/shard_map/forward/pallas_call | solution.py:383
  35.8 5.6 %all-to-all-done.1 = bf16[16,8,4096]{2,1,0:T(8,128)(2,1)} async-done(((bf16[16,8,4096]{2,1,0:T(8,128)(2,1)}), bf16[16,8,4096]{2,1,0:T(8,128)(2,1)}, u32[]{:S(2)}, u32[]{:S(2)}) %all-to-all-start.1) | async-done | bytes 1048608 | tf_op jit(solution)/shard_map/all_to_all | solution.py:297
  41.5 6.7 %all-to-all-start = ((bf16[16,8,4096]{2,1,0:T(8,128)(2,1)}), bf16[16,8,4096]{2,1,0:T(8,128)(2,1)S(1)}, u32[]{:S(2)}, u32[]{:S(2)}) async-start(bf16[16,8,4096]{2,1,0:T(8,128)(2,1)} %bitcast.47), calls=%async_computation | async-start | bytes 2097152 | tf_op jit(solution)/shard_map/all_to_all | solution.py:297
  48.1 8.0 %middle.1 = (bf16[128,4096]{1,0:T(8,128)(2,1)}, f32[128,4096]{1,0:T(8,128)}, f32[128,128]{1,0:T(8,128)}, bf16[16,2,128,128]{3,2,1,0:T(8,128)(2,1)}) custom-call(bf16[128,4096]{1,0:T(8,128)(2,1)} %bitcast.11.back, bf16[32,128,128]{2,1,0:T(8,128)(2,1)} %get-tuple-element.57.second_bt, bf16[32,128,128]{2,1,0:T(8,128)(2,1)} %get-tuple-element.58.first_bt, ...), custom_call_target="tpu_custom_call" | custom-call | flops 268435456 | bytes 8388608 | tf_op jit(solution)/shard_map/middle/pallas_call | solution.py:406
  56.2 13.8 %all-to-all-done = bf16[16,8,4096]{2,1,0:T(8,128)(2,1)S(1)} async-done(((bf16[16,8,4096]{2,1,0:T(8,128)(2,1)}), bf16[16,8,4096]{2,1,0:T(8,128)(2,1)S(1)}, u32[]{:S(2)}, u32[]{:S(2)}) %all-to-all-start) | async-done | bytes 1048608 | tf_op jit(solution)/shard_map/all_to_all | solution.py:297
  69.9 1.0 copy-done.11
  70.9 6.7 %all-to-all-start.3 = ((bf16[16,8,4096]{2,1,0:T(8,128)(2,1)}), bf16[16,8,4096]{2,1,0:T(8,128)(2,1)S(1)}, u32[]{:S(2)}, u32[]{:S(2)}) async-start(bf16[16,8,4096]{2,1,0:T(8,128)(2,1)} %bitcast.45), calls=%async_computation.3 | async-start | bytes 2097152 | tf_op jit(solution)/shard_map/all_to_all | solution.py:297
  77.6 0.1 collective-permute-start.5
  77.7 0.6 broadcast_select_fusion.6.left_t_low
  78.3 0.6 collective-permute-done.5
  78.9 0.6 broadcast_select_fusion.5
  79.5 5.1 %expand.3 = (bf16[32,128,128]{2,1,0:T(8,128)(2,1)}, bf16[32,128,128]{2,1,0:T(8,128)(2,1)}, bf16[32,128,128]{2,1,0:T(8,128)(2,1)}, bf16[32,128,128]{2,1,0:T(8,128)(2,1)}) custom-call(s32[1]{0:T(128)} %bitcast.p, bf16[64,64,64]{2,1,0:T(8,128)(2,1)} %bitcast.33, bf16[64,64,64]{2,1,0:T(8,128)(2,1)} %copy-done.5, bf16[64,64,64]{2,1,0:T(8,128)(2,1)} %bitcast.37, ...), custom_call_target="tpu_custom_call" | custom-call | flops 268435456 | bytes 8388608 | tf_op jit(solution)/shard_map/expand/pallas_call | solution.py:372
  84.6 11.2 %turn.1 = (bf16[128,4096]{1,0:T(8,128)(2,1)}, f32[128,16]{1,0:T(8,128)}, bf16[128,4096]{1,0:T(8,128)(2,1)}, bf16[128,4096]{1,0:T(8,128)(2,1)}, bf16[4096,128]{1,0:T(8,128)(2,1)}, /*index=5*/bf16[128,4096]{1,0:T(8,128)(2,1)}) custom-call(bf16[128,4096]{1,0:T(8,128)(2,1)} %bitcast.41, bf16[128,4096]{1,0:T(8,128)(2,1)} %copy-done.3, ...), custom_call_target="tpu_custom_call" | custom-call | flops 268435456 | bytes 8388608 | tf_op jit(solution)/shard_map/turn/pallas_call | solution.py:417
  95.7 3.0 %all-to-all-done.3 = bf16[16,8,4096]{2,1,0:T(8,128)(2,1)S(1)} async-done(((bf16[16,8,4096]{2,1,0:T(8,128)(2,1)}), bf16[16,8,4096]{2,1,0:T(8,128)(2,1)S(1)}, u32[]{:S(2)}, u32[]{:S(2)}) %all-to-all-start.3) | async-done | bytes 1048608 | tf_op jit(solution)/shard_map/all_to_all | solution.py:297
  98.8 7.2 %all-to-all-start.2 = ((bf16[16,8,4096]{2,1,0:T(8,128)(2,1)}), bf16[16,8,4096]{2,1,0:T(8,128)(2,1)}, u32[]{:S(2)}, u32[]{:S(2)}) async-start(bf16[16,8,4096]{2,1,0:T(8,128)(2,1)} %bitcast.46), calls=%async_computation.2 | async-start | bytes 2097152 | tf_op jit(solution)/shard_map/all_to_all | solution.py:297
  106.0 7.7 %lower.1 = (f32[128,4096]{1,0:T(8,128)}, f32[128,16]{1,0:T(8,128)}, bf16[16,2,128,128]{3,2,1,0:T(8,128)(2,1)}) custom-call(bf16[128,4096]{1,0:T(8,128)(2,1)} %bitcast.38, bf16[32,128,128]{2,1,0:T(8,128)(2,1)} %get-tuple-element.72.first_bd, bf16[32,128,128]{2,1,0:T(8,128)(2,1)} %get-tuple-element.73.second_bd, bf16[128,128]{1,0:T(8,128)(2,1)} %get-tuple-element.91.left, ...), custom_call_target="tpu_custom_call" | custom-call | flops 268435456 | bytes 8388608 | tf_op jit(solution)/shard_map/lower/pallas_call | solution.py:463
  113.7 0.1 broadcast_select_fusion
  113.9 0.1 collective-permute-start.10
  114.0 2.6 %collective-permute-done.10 = bf16[16,2,128,128]{3,2,1,0:T(8,128)(2,1)S(1)} collective-permute-done((bf16[16,2,128,128]{3,2,1,0:T(8,128)(2,1)S(1)}, bf16[16,2,128,128]{3,2,1,0:T(8,128)(2,1)S(1)}, u32[]{:S(2)}, u32[]{:S(2)}) %collective-permute-start.10) | collective-permute-done | bytes 1048608 | tf_op jit(solution)/shard_map/ppermute | solution.py:284
  116.6 1.5 add_convert_fusion
  118.1 8.8 %all-to-all-done.2 = bf16[16,8,4096]{2,1,0:T(8,128)(2,1)} async-done(((bf16[16,8,4096]{2,1,0:T(8,128)(2,1)}), bf16[16,8,4096]{2,1,0:T(8,128)(2,1)}, u32[]{:S(2)}, u32[]{:S(2)}) %all-to-all-start.2) | async-done | bytes 1048608 | tf_op jit(solution)/shard_map/all_to_all | solution.py:297
  126.9 5.0 %all-to-all-start.4 = ((bf16[8,4,128,128]{3,2,1,0:T(8,128)(2,1)}), bf16[8,4,128,128]{3,2,1,0:T(8,128)(2,1)S(1)}, u32[]{:S(2)}, u32[]{:S(2)}) async-start(bf16[8,4,128,128]{3,2,1,0:T(8,128)(2,1)} %bitcast.22), calls=%async_computation.4 | async-start | bytes 2097152 | tf_op jit(solution)/shard_map/all_to_all | solution.py:308
  131.9 5.0 %last.1 = (bf16[128,4096]{1,0:T(8,128)(2,1)}, f32[128,128]{1,0:T(8,128)}) custom-call(bf16[128,4096]{1,0:T(8,128)(2,1)} %bitcast.13.received, bf16[128,128]{1,0:T(8,128)(2,1)} %get-tuple-element.69.right_t, bf16[128,128]{1,0:T(8,128)(2,1)} %constant.34.clone.order, bf16[128,4096]{1,0:T(8,128)(2,1)} %get-tuple-element.70.upstream, ...), custom_call_target="tpu_custom_call" | custom-call | flops 268435456 | bytes 8388608 | tf_op jit(solution)/shard_map/last/pallas_call | solution.py:476
  136.9 0.1 collective-permute-start.8
  137.0 1.2 collective-permute-done.8
  138.2 1.5 select_add_fusion.1
  139.7 5.9 %all-to-all-done.4 = bf16[8,4,128,128]{3,2,1,0:T(8,128)(2,1)S(1)} async-done(((bf16[8,4,128,128]{3,2,1,0:T(8,128)(2,1)}), bf16[8,4,128,128]{3,2,1,0:T(8,128)(2,1)S(1)}, u32[]{:S(2)}, u32[]{:S(2)}) %all-to-all-start.4) | async-done | bytes 1048608 | tf_op jit(solution)/shard_map/all_to_all | solution.py:308
  145.6 0.1 reduce_sum.12
  145.8 0.0 copy-start.12
  145.8 2.9 %collective-permute-start.11 = (bf16[4,128,128]{2,1,0:T(8,128)(2,1)S(1)}, bf16[4,128,128]{2,1,0:T(8,128)(2,1)S(1)}, u32[]{:S(2)}, u32[]{:S(2)}) collective-permute-start(bf16[4,128,128]{2,1,0:T(8,128)(2,1)S(1)} %reduce_sum.12), channel_id=1, source_target_pairs={{0,24},{2,26},{4,28},{6,30},{8,16},{10,18},{12,20},{14,22},{16,8},... | collective-permute-start | bytes 393224 | tf_op jit(solution)/shard_map/ppermute | solution.py:313
  148.7 3.9 %collective-permute-done.11 = bf16[4,128,128]{2,1,0:T(8,128)(2,1)S(1)} collective-permute-done((bf16[4,128,128]{2,1,0:T(8,128)(2,1)S(1)}, bf16[4,128,128]{2,1,0:T(8,128)(2,1)S(1)}, u32[]{:S(2)}, u32[]{:S(2)}) %collective-permute-start.11) | collective-permute-done | bytes 131104 | tf_op jit(solution)/shard_map/ppermute | solution.py:313
  152.7 1.2 broadcast_in_dim.17
  153.9 4.2 %all-to-all-start.5 = ((bf16[8,4,128,128]{3,2,1,0:T(8,128)(2,1)}), bf16[8,4,128,128]{3,2,1,0:T(8,128)(2,1)S(1)}, u32[]{:S(2)}, u32[]{:S(2)}) async-start(bf16[8,4,128,128]{3,2,1,0:T(8,128)(2,1)} %broadcast_in_dim.17), calls=%async_computation.5 | async-start | bytes 2097152 | tf_op jit(solution)/shard_map/all_to_all | solution.py:308
  158.1 0.5 collective-permute-start.6
  158.6 0.1 collective-permute-start.9
  158.8 3.6 %collective-permute-done.9 = f32[128,16]{1,0:T(8,128)S(1)} collective-permute-done((f32[128,16]{1,0:T(8,128)S(1)}, f32[128,16]{1,0:T(8,128)S(1)}, u32[]{:S(2)}, u32[]{:S(2)}) %collective-permute-start.9) | collective-permute-done | bytes 8224 | tf_op jit(solution)/shard_map/ppermute | solution.py:284
  162.3 0.6 select_add_fusion
  163.0 1.7 maximum_select_fusion
  164.7 6.0 %all-to-all-done.5 = bf16[8,4,128,128]{3,2,1,0:T(8,128)(2,1)S(1)} async-done(((bf16[8,4,128,128]{3,2,1,0:T(8,128)(2,1)}), bf16[8,4,128,128]{3,2,1,0:T(8,128)(2,1)S(1)}, u32[]{:S(2)}, u32[]{:S(2)}) %all-to-all-start.5) | async-done | bytes 1048608 | tf_op jit(solution)/shard_map/all_to_all | solution.py:308
  170.6 2.5 %unpack.1 = (f32[64,64,64]{2,1,0:T(8,128)}, f32[64,64,64]{2,1,0:T(8,128)}) custom-call(bf16[16,2,128,128]{3,2,1,0:T(8,128)(2,1)S(1)} %bitcast.30), custom_call_target="tpu_custom_call" | custom-call | flops 268435456 | bytes 8388608 | tf_op jit(solution)/shard_map/unpack/pallas_call | solution.py:496
  (35 shorter events, 0.1 us)
Async XLA Ops:
  0.6 2.8 %copy-start = (bf16[128,16]{1,0:T(8,128)(2,1)S(1)}, bf16[128,16]{1,0:T(8,128)(2,1)}, u32[]{:S(2)}) copy-start(bf16[128,16]{1,0:T(8,128)(2,1)} %constant.33.clone.onehot) | copy-start | bytes 12292
  0.6 2.8 %copy-start.1 = (bf16[128,128]{1,0:T(8,128)(2,1)S(1)}, bf16[128,128]{1,0:T(8,128)(2,1)}, u32[]{:S(2)}) copy-start(bf16[128,128]{1,0:T(8,128)(2,1)} %constant.32.clone.mask) | copy-start | bytes 98308
  0.7 2.8 %copy-start.2 = (bf16[1,8,16,16]{3,2,1,0:T(8,128)(2,1)S(1)}, bf16[1,8,16,16]{3,2,1,0:T(8,128)(2,1)}, u32[]{:S(2)}) copy-start(bf16[1,8,16,16]{3,2,1,0:T(8,128)(2,1)} %param.13) | copy-start | bytes 12292
  3.0 3.4 %collective-permute-start = (bf16[128,4096]{1,0:T(8,128)(2,1)}, bf16[128,4096]{1,0:T(8,128)(2,1)S(1)}, u32[]{:S(2)}, u32[]{:S(2)}) collective-permute-start(bf16[128,4096]{1,0:T(8,128)(2,1)} %dynamic-slice_bitcast_fusion.2), channel_id=1, source_target_pairs={{0,1},{1,0},{2,3},{3,2},{4,5},{5,4},{6,7},{7,6},{8,9},{9,8},{10,11... | collective-permute-start | bytes 3145736 | tf_op jit(solution)/shard_map/ppermute | solution.py:284
  3.6 4.0 %collective-permute-start.1 = (bf16[128,128]{1,0:T(8,128)(2,1)S(1)}, bf16[128,128]{1,0:T(8,128)(2,1)S(1)}, u32[]{:S(2)}, u32[]{:S(2)}) collective-permute-start(bf16[128,128]{1,0:T(8,128)(2,1)S(1)} %get-tuple-element.49), channel_id=1, source_target_pairs={{0,1},{1,0},{2,3},{3,2},{4,5},{5,4},{6,7},{7,6},{8,9},{9,8},{10,11... | collective-permute-start | bytes 98312 | tf_op jit(solution)/shard_map/ppermute | solution.py:284
  6.3 1.0 copy-start.3
  6.3 1.3 copy-start.6
  7.6 10.6 %copy-start.16 = (bf16[1,1,128,128]{3,2,1,0:T(8,128)(2,1)S(1)}, bf16[1,1,128,128]{3,2,1,0:T(8,128)(2,1)}, u32[]{:S(2)}) copy-start(bf16[1,1,128,128]{3,2,1,0:T(8,128)(2,1)} %param.12) | copy-start | bytes 98308
  7.6 10.6 %copy-start.4 = (bf16[1,64,64,64]{3,2,1,0:T(8,128)(2,1)S(1)}, bf16[1,64,64,64]{3,2,1,0:T(8,128)(2,1)}, u32[]{:S(2)}) copy-start(bf16[1,64,64,64]{3,2,1,0:T(8,128)(2,1)} %param.14) | copy-start | bytes 1572868
  9.1 32.4 %all-to-all-start.1 = ((bf16[16,8,4096]{2,1,0:T(8,128)(2,1)}), bf16[16,8,4096]{2,1,0:T(8,128)(2,1)}, u32[]{:S(2)}, u32[]{:S(2)}) async-start(bf16[16,8,4096]{2,1,0:T(8,128)(2,1)} %bitcast.39), calls=%async_computation.1 | async-start | bytes 2097152 | tf_op jit(solution)/shard_map/all_to_all | solution.py:297
  18.2 9.8 %collective-permute-start.2 = (bf16[128,128]{1,0:T(8,128)(2,1)S(1)}, bf16[128,128]{1,0:T(8,128)(2,1)S(1)}, u32[]{:S(2)}, u32[]{:S(2)}) collective-permute-start(bf16[128,128]{1,0:T(8,128)(2,1)S(1)} %bitcast.51), channel_id=1, source_target_pairs={{0,1},{1,0},{2,3},{3,2},{4,5},{5,4},{6,7},{7,6},{8,9},{9,8},{10,11... | collective-permute-start | bytes 98312 | tf_op jit(solution)/shard_map/ppermute | solution.py:284
  18.3 3.4 %collective-permute-start.3 = (bf16[64,64,64]{2,1,0:T(8,128)(2,1)S(1)}, bf16[64,64,64]{2,1,0:T(8,128)(2,1)S(1)}, u32[]{:S(2)}, u32[]{:S(2)}) collective-permute-start(bf16[64,64,64]{2,1,0:T(8,128)(2,1)S(1)} %bitcast.34), channel_id=1, source_target_pairs={{0,1},{1,0},{2,3},{3,2},{4,5},{5,4},{6,7},{7,6},{8,9},{9,8},{10,11... | collective-permute-start | bytes 1572872 | tf_op jit(solution)/shard_map/ppermute | solution.py:284
  18.8 4.1 %collective-permute-start.4 = (bf16[64,64,64]{2,1,0:T(8,128)(2,1)}, bf16[64,64,64]{2,1,0:T(8,128)(2,1)}, u32[]{:S(2)}, u32[]{:S(2)}) collective-permute-start(bf16[64,64,64]{2,1,0:T(8,128)(2,1)} %bitcast.35), channel_id=1, source_target_pairs={{0,1},{1,0},{2,3},{3,2},{4,5},{5,4},{6,7},{7,6},{8,9},{9,8},{10,11... | collective-permute-start | bytes 1572872 | tf_op jit(solution)/shard_map/ppermute | solution.py:284
  21.7 1.0 copy-start.5
  28.0 0.6 copy-start.17
  41.5 28.5 %all-to-all-start = ((bf16[16,8,4096]{2,1,0:T(8,128)(2,1)}), bf16[16,8,4096]{2,1,0:T(8,128)(2,1)S(1)}, u32[]{:S(2)}, u32[]{:S(2)}) async-start(bf16[16,8,4096]{2,1,0:T(8,128)(2,1)} %bitcast.47), calls=%async_computation | async-start | bytes 2097152 | tf_op jit(solution)/shard_map/all_to_all | solution.py:297
  69.9 1.0 copy-start.11
  70.9 27.9 %all-to-all-start.3 = ((bf16[16,8,4096]{2,1,0:T(8,128)(2,1)}), bf16[16,8,4096]{2,1,0:T(8,128)(2,1)S(1)}, u32[]{:S(2)}, u32[]{:S(2)}) async-start(bf16[16,8,4096]{2,1,0:T(8,128)(2,1)} %bitcast.45), calls=%async_computation.3 | async-start | bytes 2097152 | tf_op jit(solution)/shard_map/all_to_all | solution.py:297
  77.6 1.3 collective-permute-start.5
  98.8 7.2 %copy-start.8 = (bf16[16,8,4096]{2,1,0:T(8,128)(2,1)}, bf16[16,8,4096]{2,1,0:T(8,128)(2,1)S(1)}, u32[]{:S(2)}) copy-start(bf16[16,8,4096]{2,1,0:T(8,128)(2,1)S(1)} %all-to-all-done.3) | copy-start | bytes 3145732
  98.8 28.1 %all-to-all-start.2 = ((bf16[16,8,4096]{2,1,0:T(8,128)(2,1)}), bf16[16,8,4096]{2,1,0:T(8,128)(2,1)}, u32[]{:S(2)}, u32[]{:S(2)}) async-start(bf16[16,8,4096]{2,1,0:T(8,128)(2,1)} %bitcast.46), calls=%async_computation.2 | async-start | bytes 2097152 | tf_op jit(solution)/shard_map/all_to_all | solution.py:297
  106.0 7.7 %copy-start.7 = (bf16[16,2,128,128]{3,2,1,0:T(8,128)(2,1)S(1)}, bf16[16,2,128,128]{3,2,1,0:T(8,128)(2,1)}, u32[]{:S(2)}) copy-start(bf16[16,2,128,128]{3,2,1,0:T(8,128)(2,1)} %get-tuple-element.84) | copy-start | bytes 3145732
  113.7 2.9 %copy-start.9 = (bf16[16,2,128,128]{3,2,1,0:T(8,128)(2,1)S(1)}, bf16[16,2,128,128]{3,2,1,0:T(8,128)(2,1)}, u32[]{:S(2)}) copy-start(bf16[16,2,128,128]{3,2,1,0:T(8,128)(2,1)} %get-tuple-element.83) | copy-start | bytes 3145732
  113.9 2.7 %collective-permute-start.10 = (bf16[16,2,128,128]{3,2,1,0:T(8,128)(2,1)S(1)}, bf16[16,2,128,128]{3,2,1,0:T(8,128)(2,1)S(1)}, u32[]{:S(2)}, u32[]{:S(2)}) collective-permute-start(bf16[16,2,128,128]{3,2,1,0:T(8,128)(2,1)S(1)} %broadcast_select_fusion), channel_id=1, source_target_pairs={{0,1},{1,0},{2,3},{3,2},{4,5},{5,4},{6,7},{7,6},{8,9},{9,8},{10,11... | collective-permute-start | bytes 3145736 | tf_op jit(solution)/shard_map/ppermute | solution.py:284
  126.9 18.7 %all-to-all-start.4 = ((bf16[8,4,128,128]{3,2,1,0:T(8,128)(2,1)}), bf16[8,4,128,128]{3,2,1,0:T(8,128)(2,1)S(1)}, u32[]{:S(2)}, u32[]{:S(2)}) async-start(bf16[8,4,128,128]{3,2,1,0:T(8,128)(2,1)} %bitcast.22), calls=%async_computation.4 | async-start | bytes 2097152 | tf_op jit(solution)/shard_map/all_to_all | solution.py:308
  131.9 5.0 %copy-start.14 = (f32[128,128]{1,0:T(8,128)S(1)}, f32[128,128]{1,0:T(8,128)}, u32[]{:S(2)}) copy-start(f32[128,128]{1,0:T(8,128)} %get-tuple-element.80) | copy-start | bytes 196612
  136.9 1.3 collective-permute-start.8
  145.8 12.3 %copy-start.10 = (bf16[128,4096]{1,0:T(8,128)(2,1)S(1)}, bf16[128,4096]{1,0:T(8,128)(2,1)}, u32[]{:S(2)}) copy-start(bf16[128,4096]{1,0:T(8,128)(2,1)} %get-tuple-element.70.upstream) | copy-start | bytes 3145732
  145.8 12.3 %copy-start.12 = (bf16[128,4096]{1,0:T(8,128)(2,1)S(1)}, bf16[128,4096]{1,0:T(8,128)(2,1)}, u32[]{:S(2)}) copy-start(bf16[128,4096]{1,0:T(8,128)(2,1)} %get-tuple-element.78) | copy-start | bytes 3145732
  145.8 12.8 %copy-start.13 = (f32[128,16]{1,0:T(8,128)S(1)}, f32[128,16]{1,0:T(8,128)}, u32[]{:S(2)}) copy-start(f32[128,16]{1,0:T(8,128)} %get-tuple-element.82) | copy-start | bytes 24580
  145.8 12.8 %copy-start.15 = (f32[128,16]{1,0:T(8,128)S(1)}, f32[128,16]{1,0:T(8,128)}, u32[]{:S(2)}) copy-start(f32[128,16]{1,0:T(8,128)} %get-tuple-element.81) | copy-start | bytes 24580
  145.8 6.8 %collective-permute-start.11 = (bf16[4,128,128]{2,1,0:T(8,128)(2,1)S(1)}, bf16[4,128,128]{2,1,0:T(8,128)(2,1)S(1)}, u32[]{:S(2)}, u32[]{:S(2)}) collective-permute-start(bf16[4,128,128]{2,1,0:T(8,128)(2,1)S(1)} %reduce_sum.12), channel_id=1, source_target_pairs={{0,24},{2,26},{4,28},{6,30},{8,16},{10,18},{12,20},{14,22},{16,8},... | collective-permute-start | bytes 393224 | tf_op jit(solution)/shard_map/ppermute | solution.py:313
  153.9 16.7 %all-to-all-start.5 = ((bf16[8,4,128,128]{3,2,1,0:T(8,128)(2,1)}), bf16[8,4,128,128]{3,2,1,0:T(8,128)(2,1)S(1)}, u32[]{:S(2)}, u32[]{:S(2)}) async-start(bf16[8,4,128,128]{3,2,1,0:T(8,128)(2,1)} %broadcast_in_dim.17), calls=%async_computation.5 | async-start | bytes 2097152 | tf_op jit(solution)/shard_map/all_to_all | solution.py:308
  158.1 4.9 %collective-permute-start.7 = (bf16[128,4096]{1,0:T(8,128)(2,1)S(1)}, bf16[128,4096]{1,0:T(8,128)(2,1)S(1)}, u32[]{:S(2)}, u32[]{:S(2)}) collective-permute-start(bf16[128,4096]{1,0:T(8,128)(2,1)S(1)} %copy-done.10), channel_id=1, source_target_pairs={{0,1},{1,0},{2,3},{3,2},{4,5},{5,4},{6,7},{7,6},{8,9},{9,8},{10,11... | collective-permute-start | bytes 3145736 | tf_op jit(solution)/shard_map/ppermute | solution.py:284
  158.1 4.9 %collective-permute-start.6 = (bf16[128,4096]{1,0:T(8,128)(2,1)S(1)}, bf16[128,4096]{1,0:T(8,128)(2,1)S(1)}, u32[]{:S(2)}, u32[]{:S(2)}) collective-permute-start(bf16[128,4096]{1,0:T(8,128)(2,1)S(1)} %copy-done.12), channel_id=1, source_target_pairs={{0,1},{1,0},{2,3},{3,2},{4,5},{5,4},{6,7},{7,6},{8,9},{9,8},{10,11... | collective-permute-start | bytes 3145736 | tf_op jit(solution)/shard_map/ppermute | solution.py:284
  158.6 3.7 %collective-permute-start.9 = (f32[128,16]{1,0:T(8,128)S(1)}, f32[128,16]{1,0:T(8,128)S(1)}, u32[]{:S(2)}, u32[]{:S(2)}) collective-permute-start(f32[128,16]{1,0:T(8,128)S(1)} %broadcast_select_fusion.3), channel_id=1, source_target_pairs={{0,1},{1,0},{2,3},{3,2},{4,5},{5,4},{6,7},{7,6},{8,9},{9,8},{10,11... | collective-permute-start | bytes 24584 | tf_op jit(solution)/shard_map/ppermute | solution.py:284

commit v5 on v4

--- a/solution.py
+++ b/solution.py
@@ -163,46 +163,25 @@
 
 
 def turn_kernel(
-    rows,
-    upstream,
-    act,
-    chan_back,
+    incoming,
     act_low,
-    left,
     left_t_low,
     second_bt,
     first_bt,
     eye,
+    left_term,
     onehot,
     mask,
-    input_grad,
     left_grad,
     gate_low,
     back_low,
     mixed_grad,
     sent,
     wide,
-    left_acc,
 ):
     step = pl.program_id(0)
-    steps = pl.num_programs(0)
     pairs = second_bt.shape[0]
-
-    gy = upstream[...].astype(F32)
-    carried = mm(left[...], rows[...])
-    incoming = (gy * carried + chan_back[...]).astype(BF)
-    input_grad[...] = incoming
-    term = mm((gy * act[...].astype(F32)).astype(BF), rows[...], NT)
-
-    @pl.when(step == 0)
-    def _():
-        left_acc[...] = term
-
-    @pl.when(step > 0)
-    def _():
-        left_acc[...] += term
-
-    gate = (incoming.astype(F32) * act_low[...].astype(F32)).astype(BF)
+    gate = (incoming[...].astype(F32) * act_low[...].astype(F32)).astype(BF)
     gate_low[...] = gate
     back = mm(left_t_low[...], gate).astype(BF)
     back_low[...] = back
@@ -210,7 +189,7 @@
         at = pl.multiple_of((step * pairs + q) * 128, 128)
         wide[pl.ds(at, 128), :] = mm(second_bt[q], back[:, columns(q)], NT)
 
-    @pl.when(step == steps - 1)
+    @pl.when(step == pl.num_programs(0) - 1)
     def _():
         for q in range(first_bt.shape[0]):
             pair = regroup(wide, q, 2 * first_bt.shape[0])
@@ -218,7 +197,7 @@
             piece = mm(first_bt[q], pair).astype(BF)
             sent[:, columns(q)] = mm(eye[...], piece, NT).astype(BF)
         left_grad[...] = mm(
-            left_acc[...] * mask[...].astype(F32), onehot[...].astype(F32), precision=lax.Precision.HIGHEST
+            left_term[...] * mask[...].astype(F32), onehot[...].astype(F32), precision=lax.Precision.HIGHEST
         )
 
 
@@ -412,13 +391,18 @@
         [act_full, act_full, square, whole(owned)],
         [pltpu.VMEM(col_shape, F32), pltpu.VMEM(col_shape, BF)],
     )(returned_1, sbt_1, fbt_1, mixed_1, right_act_1, right_t_1, act_1, right_0, act_0, order)
-    gathered_0 = exchange(right_act_0, devices)
-
-    input_1, left_grad_1, gate_0, back_0, mixed_grad_0, sent_0 = call(
+    gathered_0 = exchange(after(right_act_0, sbt_0), devices)
+
+    upstream_1 = lax.dynamic_index_in_dim(cotangent, after(core, rows_1), 0, keepdims=False)
+    carried_1 = after(jnp.dot(jnp.where(core == 0, full_other, full), gathered_1, preferred_element_type=F32))
+    input_1 = (upstream_1.astype(F32) * carried_1 + chan_back_1).astype(BF)
+    gate_1 = (upstream_1.astype(F32) * act_1.astype(F32)).astype(BF)
+    left_term = lax.dot_general(after(gate_1), gathered_1, NT, preferred_element_type=F32)
+
+    left_grad_1, gate_0, back_0, mixed_grad_0, sent_0 = call(
         turn_kernel,
         "turn",
         [
-            sds(act_shape, BF),
             sds((tokens, count), F32),
             sds(act_shape, BF),
             sds(act_shape, BF),
@@ -429,31 +413,24 @@
         [
             moving,
             moving,
-            moving,
-            moving,
-            moving,
-            square,
             square,
             pl.BlockSpec((step // (2 * side), 2 * side, 2 * side), lambda i: (i, 0, 0)),
             pair_full,
             square,
+            square,
             narrow,
             square,
         ],
-        [moving, narrow, moving, moving, col_full, act_full],
-        [pltpu.VMEM(col_shape, F32), pltpu.VMEM((tokens, tokens), F32)],
-        room=62,
+        [narrow, moving, moving, col_full, act_full],
+        [pltpu.VMEM(col_shape, F32)],
     )(
-        gathered_1,
-        upstream,
-        act_1,
-        chan_back_1,
+        input_1,
         act_0,
-        jnp.where(core == 0, full_other, full),
         jnp.where(core == 0, turned, turned_other),
         sbt_0,
         fbt_0,
         eye,
+        left_term,
         onehot,
         mask,
     )

time: 174 us -> 174 us (level)
  other arithmetic: 10 us -> 13.2 us
  waiting for transfers between devices: 55.4 us -> 52.7 us
  Pallas kernels: 51.9 us -> 49.7 us
    convert_element_type x0 -> x1, other arithmetic: none -> 3.15 us  [body(): gate_1 = (upstream_1.astype(F32) * act_1.astype(F32)).astype(BF)]
    all_to_all x4, waiting for transfers between devices: 31.3 us -> 28.4 us  [exchange(): lax.all_to_all(chunks, 'blk', split_axis=0, concat_axis=0, axis_index_gro...]
    pallas_call x1, Pallas kernels: 11.2 us -> 8.96 us  [body(): call(turn_kernel, 'turn', [sds((tokens, count), F32), sds(act_shape, BF),...]
  transfers between devices with their start and end apart: 18 -> 18, of which waited for: 13 -> 13; matrix products, arithmetic and copies ran while one was open for 7% -> 10% of each run, Pallas kernels for 29% -> 27%
where the time goes in v5:
time: 174 us; the launch traced here: 173 us
  waiting for transfers between devices  52.7 us (30%)
  Pallas kernels  49.7 us (29%)
  starting transfers between devices  44.3 us (25%)
  other arithmetic  13.2 us (8%)
  local copies, waits for them, and re-layouts  9.36 us (5%)
  matrix products  2.89 us (2%)
    all_to_all x4, starting transfers between devices, exchange(): lax.all_to_all(chunks, 'blk', split_axis=0, concat_axis=0, axis_index_gro...  30.2 us
    all_to_all x4, waiting for transfers between devices, exchange(): lax.all_to_all(chunks, 'blk', split_axis=0, concat_axis=0, axis_index_gro...  28.4 us
    all_to_all x2, waiting for transfers between devices, exchanged(): lax.all_to_all(value, 'blk', split_axis=0, concat_axis=0, axis_index_grou...  11.9 us
    pallas_call x2, Pallas kernels, expand(): call(functools.partial(expand_kernel, section), 'expand', [sds(pair_shape...  10.1 us
    all_to_all x2, starting transfers between devices, exchanged(): lax.all_to_all(value, 'blk', split_axis=0, concat_axis=0, axis_index_grou...  9.14 us
    pallas_call x1, Pallas kernels, body(): call(turn_kernel, 'turn', [sds((tokens, count), F32), sds(act_shape, BF),...  8.96 us
    ppermute x11, waiting for transfers between devices, swap(): return lax.ppermute(value, 'pipe', [(0, 1), (1, 0)])  8.46 us
    pallas_call x1, Pallas kernels, body(): call(middle_kernel, 'middle', [sds(act_shape, BF), sds(act_shape, F32), s...  8.04 us
  transfers between devices with their start and end apart: 18, of which 13 were waited for; matrix products, arithmetic and copies ran while one was open for 10% of the time, Pallas kernels for 27%

profile of v5, /device:TPU:0, one launch (start us, length us, event | category | flops | bytes accessed | tf_op | source)
XLA Modules:
  0.0 173.0 jit_solution(3052558379905894748)
XLA Ops:
  0.6 0.0 copy-start
  0.6 0.0 copy-start.1
  0.7 2.3 %dynamic-slice_bitcast_fusion.2 = bf16[128,4096]{1,0:T(8,128)(2,1)} fusion(bf16[1,2,128,4096]{3,2,1,0:T(8,128)(2,1)} %param.10, s32[]{:T(128)S(6)} %select_n.97), kind=kLoop, calls=%fused_computation.15 | loop fusion | bytes 2097156 | tf_op jit(solution)/shard_map/jit(dynamic_index_in_dim)/squeeze | solution.py:308
  3.0 0.5 collective-permute-start
  3.4 0.2 left.1
  3.6 0.1 collective-permute-start.1
  3.7 1.3 dynamic-slice_bitcast_fusion
  5.0 1.3 dynamic-slice_bitcast_fusion.1
  6.3 0.0 copy-start.7
  6.3 1.0 copy-done.7
  7.3 0.5 multiply_convert_fusion
  7.8 1.4 convolution_convert_fusion
  9.2 9.1 %all-to-all-start.1 = ((bf16[16,8,4096]{2,1,0:T(8,128)(2,1)}), bf16[16,8,4096]{2,1,0:T(8,128)(2,1)}, u32[]{:S(2)}, u32[]{:S(2)}) async-start(bf16[16,8,4096]{2,1,0:T(8,128)(2,1)} %bitcast.48), calls=%async_computation.1 | async-start | bytes 2097152 | tf_op jit(solution)/shard_map/all_to_all | solution.py:276
  18.3 0.1 collective-permute-start.2
  18.4 0.5 collective-permute-start.3
  18.9 0.1 collective-permute-start.4
  19.0 2.7 %broadcast_select_fusion.1 = (bf16[128,4096]{1,0:T(8,128)(2,1)}, bf16[128,4096]{1,0:T(8,128)(2,1)}) fusion(bf16[128,4096]{1,0:T(8,128)(2,1)S(1)} %dynamic-slice_bitcast_fusion, bf16[128,4096]{1,0:T(8,128)(2,1)} %copy-done.7, pred[]{:T(512)S(6)} %eq.2), kind=kLoop, calls=%fused_computation.17 | loop fusion | flops 1048576 | bytes 4194305 | tf_op jit(solution)/shard_map/jit(_where)/select_n | solution.py:348
  21.7 0.2 collective-permute-done.3.first_other
  21.8 1.0 copy-done.6
  22.8 0.2 collective-permute-done.4.second_other
  23.1 5.1 %expand.2 = (bf16[32,128,128]{2,1,0:T(8,128)(2,1)}, bf16[32,128,128]{2,1,0:T(8,128)(2,1)}, bf16[32,128,128]{2,1,0:T(8,128)(2,1)}, bf16[32,128,128]{2,1,0:T(8,128)(2,1)}) custom-call(s32[1]{0:T(128)} %bitcast.p, bf16[64,64,64]{2,1,0:T(8,128)(2,1)} %bitcast.42, bf16[64,64,64]{2,1,0:T(8,128)(2,1)} %copy-done.6, bf16[64,64,64]{2,1,0:T(8,128)(2,1)} %bitcast.46, ...), custom_call_target="tpu_custom_call" | custom-call | flops 268435456 | bytes 8388608 | tf_op jit(solution)/shard_map/expand/pallas_call | solution.py:351
  28.1 0.6 copy-done.16
  28.7 7.2 %forward.1 = (bf16[128,4096]{1,0:T(8,128)(2,1)}, bf16[4096,128]{1,0:T(8,128)(2,1)}, bf16[128,4096]{1,0:T(8,128)(2,1)}, bf16[128,128]{1,0:T(8,128)(2,1)}, bf16[12...) custom-call(s32[1]{0:T(128)} %bitcast.p, bf16[128,4096]{1,0:T(8,128)(2,1)} %get-tuple-element.94.act, ...), custom_call_target="tpu_custom_call" | custom-call | flops 268435456 | bytes 8388608 | tf_op jit(solution)/shard_map/forward/pallas_call | solution.py:362
  36.0 5.6 %all-to-all-done.1 = bf16[16,8,4096]{2,1,0:T(8,128)(2,1)} async-done(((bf16[16,8,4096]{2,1,0:T(8,128)(2,1)}), bf16[16,8,4096]{2,1,0:T(8,128)(2,1)}, u32[]{:S(2)}, u32[]{:S(2)}) %all-to-all-start.1) | async-done | bytes 1048608 | tf_op jit(solution)/shard_map/all_to_all | solution.py:276
  41.6 6.7 %all-to-all-start = ((bf16[16,8,4096]{2,1,0:T(8,128)(2,1)}), bf16[16,8,4096]{2,1,0:T(8,128)(2,1)S(1)}, u32[]{:S(2)}, u32[]{:S(2)}) async-start(bf16[16,8,4096]{2,1,0:T(8,128)(2,1)} %bitcast.54), calls=%async_computation | async-start | bytes 2097152 | tf_op jit(solution)/shard_map/all_to_all | solution.py:276
  48.3 5.0 %expand.3 = (bf16[32,128,128]{2,1,0:T(8,128)(2,1)}, bf16[32,128,128]{2,1,0:T(8,128)(2,1)}, bf16[32,128,128]{2,1,0:T(8,128)(2,1)}, bf16[32,128,128]{2,1,0:T(8,128)(2,1)}) custom-call(s32[1]{0:T(128)} %bitcast.p, bf16[64,64,64]{2,1,0:T(8,128)(2,1)} %bitcast.43, bf16[64,64,64]{2,1,0:T(8,128)(2,1)} %copy-done.6, bf16[64,64,64]{2,1,0:T(8,128)(2,1)} %bitcast.47, ...), custom_call_target="tpu_custom_call" | custom-call | flops 268435456 | bytes 8388608 | tf_op jit(solution)/shard_map/expand/pallas_call | solution.py:351
  53.3 8.0 %middle.1 = (bf16[128,4096]{1,0:T(8,128)(2,1)}, f32[128,4096]{1,0:T(8,128)}, f32[128,128]{1,0:T(8,128)}, bf16[16,2,128,128]{3,2,1,0:T(8,128)(2,1)}) custom-call(bf16[128,4096]{1,0:T(8,128)(2,1)} %bitcast.12.back, bf16[32,128,128]{2,1,0:T(8,128)(2,1)} %get-tuple-element.60.second_bt, bf16[32,128,128]{2,1,0:T(8,128)(2,1)} %get-tuple-element.61.first_bt, ...), custom_call_target="tpu_custom_call" | custom-call | flops 268435456 | bytes 8388608 | tf_op jit(solution)/shard_map/middle/pallas_call | solution.py:385
  61.3 8.8 %all-to-all-done = bf16[16,8,4096]{2,1,0:T(8,128)(2,1)S(1)} async-done(((bf16[16,8,4096]{2,1,0:T(8,128)(2,1)}), bf16[16,8,4096]{2,1,0:T(8,128)(2,1)S(1)}, u32[]{:S(2)}, u32[]{:S(2)}) %all-to-all-start) | async-done | bytes 1048608 | tf_op jit(solution)/shard_map/all_to_all | solution.py:276
  70.1 7.3 %all-to-all-start.3 = ((bf16[16,8,4096]{2,1,0:T(8,128)(2,1)}), bf16[16,8,4096]{2,1,0:T(8,128)(2,1)}, u32[]{:S(2)}, u32[]{:S(2)}) async-start(bf16[16,8,4096]{2,1,0:T(8,128)(2,1)} %bitcast.52), calls=%async_computation.3 | async-start | bytes 2097152 | tf_op jit(solution)/shard_map/all_to_all | solution.py:276
  77.4 0.1 collective-permute-start.5
  77.5 0.6 broadcast_select_fusion.6.left_t_low
  78.1 0.6 collective-permute-done.5
  78.7 0.4 fusion.5
  79.1 0.6 copy-done.10
  79.7 3.2 %fusion.2 = (bf16[128,4096]{1,0:T(8,128)(2,1)S(1)}, bf16[128,4096]{1,0:T(8,128)(2,1)}) fusion(bf16[128,4096]{1,0:T(8,128)(2,1)S(1)} %copy-done.3, bf16[2,128,4096]{2,1,0:T(8,128)(2,1)S(1)} %copy-done.10, s32[]{:T(128)S(6)} %select_n.104, f32[128,4096]{1,0:T(8,128)} %get-tuple-element.66, f32[128,4096]{1,0:T(8,128)S(1)} %fusion.5), kind=kLoop, calls=%fused_computation.5 | loop fusion | flops 3670016 | bytes 8388612 | tf_op jit(solution)/shard_map/convert_element_type | solution.py:399
  82.9 1.1 fusion.3.left_term
  84.0 9.0 %turn.1 = (f32[128,16]{1,0:T(8,128)}, bf16[128,4096]{1,0:T(8,128)(2,1)}, bf16[128,4096]{1,0:T(8,128)(2,1)}, bf16[4096,128]{1,0:T(8,128)(2,1)}, bf16[128,4096]{1,0:T(8,128)(2,1)}) custom-call(bf16[128,4096]{1,0:T(8,128)(2,1)} %get-tuple-element.92.incoming.upstream, bf16[128,4096]{1,0:T(8,128)(2,1)} %get-tuple-element.93.act_low.act, ...), custom_call_target="tpu_custom_call" | custom-call | flops 268435456 | bytes 8388608 | tf_op jit(solution)/shard_map/turn/pallas_call | solution.py:402
  92.9 5.7 %all-to-all-done.3 = bf16[16,8,4096]{2,1,0:T(8,128)(2,1)} async-done(((bf16[16,8,4096]{2,1,0:T(8,128)(2,1)}), bf16[16,8,4096]{2,1,0:T(8,128)(2,1)}, u32[]{:S(2)}, u32[]{:S(2)}) %all-to-all-start.3) | async-done | bytes 1048608 | tf_op jit(solution)/shard_map/all_to_all | solution.py:276
  98.6 7.1 %all-to-all-start.2 = ((bf16[16,8,4096]{2,1,0:T(8,128)(2,1)}), bf16[16,8,4096]{2,1,0:T(8,128)(2,1)}, u32[]{:S(2)}, u32[]{:S(2)}) async-start(bf16[16,8,4096]{2,1,0:T(8,128)(2,1)} %bitcast.53), calls=%async_computation.2 | async-start | bytes 2097152 | tf_op jit(solution)/shard_map/all_to_all | solution.py:276
  105.8 0.6 broadcast_select_fusion.5.left
  106.4 7.7 %lower.1 = (f32[128,4096]{1,0:T(8,128)}, f32[128,16]{1,0:T(8,128)}, bf16[16,2,128,128]{3,2,1,0:T(8,128)(2,1)}) custom-call(bf16[128,4096]{1,0:T(8,128)(2,1)} %bitcast.17.rows, bf16[32,128,128]{2,1,0:T(8,128)(2,1)} %get-tuple-element.74.first_bd, bf16[32,128,128]{2,1,0:T(8,128)(2,1)} %get-tuple-element.75.second_bd, ...), custom_call_target="tpu_custom_call" | custom-call | flops 268435456 | bytes 8388608 | tf_op jit(solution)/shard_map/lower/pallas_call | solution.py:440
  114.1 0.1 broadcast_select_fusion
  114.2 0.1 collective-permute-start.10
  114.3 2.6 %collective-permute-done.10 = bf16[16,2,128,128]{3,2,1,0:T(8,128)(2,1)S(1)} collective-permute-done((bf16[16,2,128,128]{3,2,1,0:T(8,128)(2,1)S(1)}, bf16[16,2,128,128]{3,2,1,0:T(8,128)(2,1)S(1)}, u32[]{:S(2)}, u32[]{:S(2)}) %collective-permute-start.10) | collective-permute-done | bytes 1048608 | tf_op jit(solution)/shard_map/ppermute | solution.py:263
  117.0 1.5 add_convert_fusion
  118.5 8.3 %all-to-all-done.2 = bf16[16,8,4096]{2,1,0:T(8,128)(2,1)} async-done(((bf16[16,8,4096]{2,1,0:T(8,128)(2,1)}), bf16[16,8,4096]{2,1,0:T(8,128)(2,1)}, u32[]{:S(2)}, u32[]{:S(2)}) %all-to-all-start.2) | async-done | bytes 1048608 | tf_op jit(solution)/shard_map/all_to_all | solution.py:276
  126.7 4.9 %all-to-all-start.4 = ((bf16[8,4,128,128]{3,2,1,0:T(8,128)(2,1)}), bf16[8,4,128,128]{3,2,1,0:T(8,128)(2,1)S(1)}, u32[]{:S(2)}, u32[]{:S(2)}) async-start(bf16[8,4,128,128]{3,2,1,0:T(8,128)(2,1)} %bitcast.24), calls=%async_computation.4 | async-start | bytes 2097152 | tf_op jit(solution)/shard_map/all_to_all | solution.py:287
  131.7 5.0 %last.1 = (bf16[128,4096]{1,0:T(8,128)(2,1)}, f32[128,128]{1,0:T(8,128)}) custom-call(bf16[128,4096]{1,0:T(8,128)(2,1)} %bitcast.15.received, bf16[128,128]{1,0:T(8,128)(2,1)} %get-tuple-element.71.right_t, bf16[128,128]{1,0:T(8,128)(2,1)} %constant.36.clone.order, bf16[128,4096]{1,0:T(8,128)(2,1)} %get-tuple-element.92.incoming.upstream, ...), custom_call_target="tpu_custom_call" | custom-call | flops 268435456 | bytes 8388608 | tf_op jit(solution)/shard_map/last/pallas_call | solution.py:453
  136.7 0.1 collective-permute-start.8
  136.8 1.2 collective-permute-done.8
  138.0 1.5 select_add_fusion.1
  139.5 6.0 %all-to-all-done.4 = bf16[8,4,128,128]{3,2,1,0:T(8,128)(2,1)S(1)} async-done(((bf16[8,4,128,128]{3,2,1,0:T(8,128)(2,1)}), bf16[8,4,128,128]{3,2,1,0:T(8,128)(2,1)S(1)}, u32[]{:S(2)}, u32[]{:S(2)}) %all-to-all-start.4) | async-done | bytes 1048608 | tf_op jit(solution)/shard_map/all_to_all | solution.py:287
  145.6 0.1 reduce_sum.12
  145.7 2.8 %collective-permute-start.11 = (bf16[4,128,128]{2,1,0:T(8,128)(2,1)S(1)}, bf16[4,128,128]{2,1,0:T(8,128)(2,1)S(1)}, u32[]{:S(2)}, u32[]{:S(2)}) collective-permute-start(bf16[4,128,128]{2,1,0:T(8,128)(2,1)S(1)} %reduce_sum.12), channel_id=1, source_target_pairs={{0,24},{2,26},{4,28},{6,30},{8,16},{10,18},{12,20},{14,22},{16,8},... | collective-permute-start | bytes 393224 | tf_op jit(solution)/shard_map/ppermute | solution.py:292
  148.6 4.0 %collective-permute-done.11 = bf16[4,128,128]{2,1,0:T(8,128)(2,1)S(1)} collective-permute-done((bf16[4,128,128]{2,1,0:T(8,128)(2,1)S(1)}, bf16[4,128,128]{2,1,0:T(8,128)(2,1)S(1)}, u32[]{:S(2)}, u32[]{:S(2)}) %collective-permute-start.11) | collective-permute-done | bytes 131104 | tf_op jit(solution)/shard_map/ppermute | solution.py:292
  152.6 1.2 broadcast_in_dim.17
  153.8 4.2 %all-to-all-start.5 = ((bf16[8,4,128,128]{3,2,1,0:T(8,128)(2,1)}), bf16[8,4,128,128]{3,2,1,0:T(8,128)(2,1)S(1)}, u32[]{:S(2)}, u32[]{:S(2)}) async-start(bf16[8,4,128,128]{3,2,1,0:T(8,128)(2,1)} %broadcast_in_dim.17), calls=%async_computation.5 | async-start | bytes 2097152 | tf_op jit(solution)/shard_map/all_to_all | solution.py:287
  158.0 0.5 collective-permute-start.6
  158.6 0.1 collective-permute-start.9
  158.7 3.6 %collective-permute-done.9 = f32[128,16]{1,0:T(8,128)S(1)} collective-permute-done((f32[128,16]{1,0:T(8,128)S(1)}, f32[128,16]{1,0:T(8,128)S(1)}, u32[]{:S(2)}, u32[]{:S(2)}) %collective-permute-start.9) | collective-permute-done | bytes 8224 | tf_op jit(solution)/shard_map/ppermute | solution.py:263
  162.3 0.6 select_add_fusion
  162.9 1.7 maximum_select_fusion
  164.6 5.9 %all-to-all-done.5 = bf16[8,4,128,128]{3,2,1,0:T(8,128)(2,1)S(1)} async-done(((bf16[8,4,128,128]{3,2,1,0:T(8,128)(2,1)}), bf16[8,4,128,128]{3,2,1,0:T(8,128)(2,1)S(1)}, u32[]{:S(2)}, u32[]{:S(2)}) %all-to-all-start.5) | async-done | bytes 1048608 | tf_op jit(solution)/shard_map/all_to_all | solution.py:287
  170.5 2.5 %unpack.1 = (f32[64,64,64]{2,1,0:T(8,128)}, f32[64,64,64]{2,1,0:T(8,128)}) custom-call(bf16[16,2,128,128]{3,2,1,0:T(8,128)(2,1)S(1)} %bitcast.39), custom_call_target="tpu_custom_call" | custom-call | flops 268435456 | bytes 8388608 | tf_op jit(solution)/shard_map/unpack/pallas_call | solution.py:473
  (36 shorter events, 0.1 us)
Async XLA Ops:
  0.6 2.8 %copy-start = (bf16[128,16]{1,0:T(8,128)(2,1)S(1)}, bf16[128,16]{1,0:T(8,128)(2,1)}, u32[]{:S(2)}) copy-start(bf16[128,16]{1,0:T(8,128)(2,1)} %constant.35.clone.onehot) | copy-start | bytes 12292
  0.6 2.8 %copy-start.1 = (bf16[128,128]{1,0:T(8,128)(2,1)S(1)}, bf16[128,128]{1,0:T(8,128)(2,1)}, u32[]{:S(2)}) copy-start(bf16[128,128]{1,0:T(8,128)(2,1)} %constant.34.clone.mask) | copy-start | bytes 98308
  0.7 2.8 %copy-start.2 = (bf16[1,8,16,16]{3,2,1,0:T(8,128)(2,1)S(1)}, bf16[1,8,16,16]{3,2,1,0:T(8,128)(2,1)}, u32[]{:S(2)}) copy-start(bf16[1,8,16,16]{3,2,1,0:T(8,128)(2,1)} %param.13) | copy-start | bytes 12292
  3.0 3.4 %collective-permute-start = (bf16[128,4096]{1,0:T(8,128)(2,1)}, bf16[128,4096]{1,0:T(8,128)(2,1)S(1)}, u32[]{:S(2)}, u32[]{:S(2)}) collective-permute-start(bf16[128,4096]{1,0:T(8,128)(2,1)} %dynamic-slice_bitcast_fusion.2), channel_id=1, source_target_pairs={{0,1},{1,0},{2,3},{3,2},{4,5},{5,4},{6,7},{7,6},{8,9},{9,8},{10,11... | collective-permute-start | bytes 3145736 | tf_op jit(solution)/shard_map/ppermute | solution.py:263
  3.6 4.2 %collective-permute-start.1 = (bf16[128,128]{1,0:T(8,128)(2,1)S(1)}, bf16[128,128]{1,0:T(8,128)(2,1)S(1)}, u32[]{:S(2)}, u32[]{:S(2)}) collective-permute-start(bf16[128,128]{1,0:T(8,128)(2,1)S(1)} %get-tuple-element.50), channel_id=1, source_target_pairs={{0,1},{1,0},{2,3},{3,2},{4,5},{5,4},{6,7},{7,6},{8,9},{9,8},{10,11... | collective-permute-start | bytes 98312 | tf_op jit(solution)/shard_map/ppermute | solution.py:263
  6.3 1.0 copy-start.7
  7.8 10.6 %copy-start.15 = (bf16[1,1,128,128]{3,2,1,0:T(8,128)(2,1)S(1)}, bf16[1,1,128,128]{3,2,1,0:T(8,128)(2,1)}, u32[]{:S(2)}) copy-start(bf16[1,1,128,128]{3,2,1,0:T(8,128)(2,1)} %param.12) | copy-start | bytes 98308
  7.8 10.6 %copy-start.5 = (bf16[1,64,64,64]{3,2,1,0:T(8,128)(2,1)S(1)}, bf16[1,64,64,64]{3,2,1,0:T(8,128)(2,1)}, u32[]{:S(2)}) copy-start(bf16[1,64,64,64]{3,2,1,0:T(8,128)(2,1)} %param.14) | copy-start | bytes 1572868
  9.2 32.4 %all-to-all-start.1 = ((bf16[16,8,4096]{2,1,0:T(8,128)(2,1)}), bf16[16,8,4096]{2,1,0:T(8,128)(2,1)}, u32[]{:S(2)}, u32[]{:S(2)}) async-start(bf16[16,8,4096]{2,1,0:T(8,128)(2,1)} %bitcast.48), calls=%async_computation.1 | async-start | bytes 2097152 | tf_op jit(solution)/shard_map/all_to_all | solution.py:276
  18.3 9.8 %collective-permute-start.2 = (bf16[128,128]{1,0:T(8,128)(2,1)S(1)}, bf16[128,128]{1,0:T(8,128)(2,1)S(1)}, u32[]{:S(2)}, u32[]{:S(2)}) collective-permute-start(bf16[128,128]{1,0:T(8,128)(2,1)S(1)} %bitcast.58), channel_id=1, source_target_pairs={{0,1},{1,0},{2,3},{3,2},{4,5},{5,4},{6,7},{7,6},{8,9},{9,8},{10,11... | collective-permute-start | bytes 98312 | tf_op jit(solution)/shard_map/ppermute | solution.py:263
  18.4 3.4 %collective-permute-start.3 = (bf16[64,64,64]{2,1,0:T(8,128)(2,1)S(1)}, bf16[64,64,64]{2,1,0:T(8,128)(2,1)S(1)}, u32[]{:S(2)}, u32[]{:S(2)}) collective-permute-start(bf16[64,64,64]{2,1,0:T(8,128)(2,1)S(1)} %bitcast.44), channel_id=1, source_target_pairs={{0,1},{1,0},{2,3},{3,2},{4,5},{5,4},{6,7},{7,6},{8,9},{9,8},{10,11... | collective-permute-start | bytes 1572872 | tf_op jit(solution)/shard_map/ppermute | solution.py:263
  18.9 4.1 %collective-permute-start.4 = (bf16[64,64,64]{2,1,0:T(8,128)(2,1)}, bf16[64,64,64]{2,1,0:T(8,128)(2,1)}, u32[]{:S(2)}, u32[]{:S(2)}) collective-permute-start(bf16[64,64,64]{2,1,0:T(8,128)(2,1)} %bitcast.45), channel_id=1, source_target_pairs={{0,1},{1,0},{2,3},{3,2},{4,5},{5,4},{6,7},{7,6},{8,9},{9,8},{10,11... | collective-permute-start | bytes 1572872 | tf_op jit(solution)/shard_map/ppermute | solution.py:263
  21.8 1.0 copy-start.6
  28.1 0.6 copy-start.16
  41.6 28.5 %all-to-all-start = ((bf16[16,8,4096]{2,1,0:T(8,128)(2,1)}), bf16[16,8,4096]{2,1,0:T(8,128)(2,1)S(1)}, u32[]{:S(2)}, u32[]{:S(2)}) async-start(bf16[16,8,4096]{2,1,0:T(8,128)(2,1)} %bitcast.54), calls=%async_computation | async-start | bytes 2097152 | tf_op jit(solution)/shard_map/all_to_all | solution.py:276
  70.1 28.5 %all-to-all-start.3 = ((bf16[16,8,4096]{2,1,0:T(8,128)(2,1)}), bf16[16,8,4096]{2,1,0:T(8,128)(2,1)}, u32[]{:S(2)}, u32[]{:S(2)}) async-start(bf16[16,8,4096]{2,1,0:T(8,128)(2,1)} %bitcast.52), calls=%async_computation.3 | async-start | bytes 2097152 | tf_op jit(solution)/shard_map/all_to_all | solution.py:276
  77.4 1.7 copy-start.3
  77.4 1.3 collective-permute-start.5
  78.1 1.7 copy-start.10
  98.6 28.1 %all-to-all-start.2 = ((bf16[16,8,4096]{2,1,0:T(8,128)(2,1)}), bf16[16,8,4096]{2,1,0:T(8,128)(2,1)}, u32[]{:S(2)}, u32[]{:S(2)}) async-start(bf16[16,8,4096]{2,1,0:T(8,128)(2,1)} %bitcast.53), calls=%async_computation.2 | async-start | bytes 2097152 | tf_op jit(solution)/shard_map/all_to_all | solution.py:276
  106.4 7.7 %copy-start.8 = (bf16[16,2,128,128]{3,2,1,0:T(8,128)(2,1)S(1)}, bf16[16,2,128,128]{3,2,1,0:T(8,128)(2,1)}, u32[]{:S(2)}) copy-start(bf16[16,2,128,128]{3,2,1,0:T(8,128)(2,1)} %get-tuple-element.86) | copy-start | bytes 3145732
  114.1 2.9 %copy-start.9 = (bf16[16,2,128,128]{3,2,1,0:T(8,128)(2,1)S(1)}, bf16[16,2,128,128]{3,2,1,0:T(8,128)(2,1)}, u32[]{:S(2)}) copy-start(bf16[16,2,128,128]{3,2,1,0:T(8,128)(2,1)} %get-tuple-element.85) | copy-start | bytes 3145732
  114.2 2.7 %collective-permute-start.10 = (bf16[16,2,128,128]{3,2,1,0:T(8,128)(2,1)S(1)}, bf16[16,2,128,128]{3,2,1,0:T(8,128)(2,1)S(1)}, u32[]{:S(2)}, u32[]{:S(2)}) collective-permute-start(bf16[16,2,128,128]{3,2,1,0:T(8,128)(2,1)S(1)} %broadcast_select_fusion), channel_id=1, source_target_pairs={{0,1},{1,0},{2,3},{3,2},{4,5},{5,4},{6,7},{7,6},{8,9},{9,8},{10,11... | collective-permute-start | bytes 3145736 | tf_op jit(solution)/shard_map/ppermute | solution.py:263
  126.7 18.8 %all-to-all-start.4 = ((bf16[8,4,128,128]{3,2,1,0:T(8,128)(2,1)}), bf16[8,4,128,128]{3,2,1,0:T(8,128)(2,1)S(1)}, u32[]{:S(2)}, u32[]{:S(2)}) async-start(bf16[8,4,128,128]{3,2,1,0:T(8,128)(2,1)} %bitcast.24), calls=%async_computation.4 | async-start | bytes 2097152 | tf_op jit(solution)/shard_map/all_to_all | solution.py:287
  131.7 5.0 %copy-start.12 = (f32[128,128]{1,0:T(8,128)S(1)}, f32[128,128]{1,0:T(8,128)}, u32[]{:S(2)}) copy-start(f32[128,128]{1,0:T(8,128)} %get-tuple-element.82) | copy-start | bytes 196612
  136.7 1.3 collective-permute-start.8
  145.7 12.3 %copy-start.4 = (bf16[128,4096]{1,0:T(8,128)(2,1)S(1)}, bf16[128,4096]{1,0:T(8,128)(2,1)}, u32[]{:S(2)}) copy-start(bf16[128,4096]{1,0:T(8,128)(2,1)} %get-tuple-element.92.incoming.upstream) | copy-start | bytes 3145732
  145.7 12.3 %copy-start.11 = (bf16[128,4096]{1,0:T(8,128)(2,1)S(1)}, bf16[128,4096]{1,0:T(8,128)(2,1)}, u32[]{:S(2)}) copy-start(bf16[128,4096]{1,0:T(8,128)(2,1)} %get-tuple-element.80) | copy-start | bytes 3145732
  145.7 12.8 %copy-start.13 = (f32[128,16]{1,0:T(8,128)S(1)}, f32[128,16]{1,0:T(8,128)}, u32[]{:S(2)}) copy-start(f32[128,16]{1,0:T(8,128)} %get-tuple-element.84) | copy-start | bytes 24580
  145.7 12.8 %copy-start.14 = (f32[128,16]{1,0:T(8,128)S(1)}, f32[128,16]{1,0:T(8,128)}, u32[]{:S(2)}) copy-start(f32[128,16]{1,0:T(8,128)} %get-tuple-element.83) | copy-start | bytes 24580
  145.7 6.8 %collective-permute-start.11 = (bf16[4,128,128]{2,1,0:T(8,128)(2,1)S(1)}, bf16[4,128,128]{2,1,0:T(8,128)(2,1)S(1)}, u32[]{:S(2)}, u32[]{:S(2)}) collective-permute-start(bf16[4,128,128]{2,1,0:T(8,128)(2,1)S(1)} %reduce_sum.12), channel_id=1, source_target_pairs={{0,24},{2,26},{4,28},{6,30},{8,16},{10,18},{12,20},{14,22},{16,8},... | collective-permute-start | bytes 393224 | tf_op jit(solution)/shard_map/ppermute | solution.py:292
  153.8 16.7 %all-to-all-start.5 = ((bf16[8,4,128,128]{3,2,1,0:T(8,128)(2,1)}), bf16[8,4,128,128]{3,2,1,0:T(8,128)(2,1)S(1)}, u32[]{:S(2)}, u32[]{:S(2)}) async-start(bf16[8,4,128,128]{3,2,1,0:T(8,128)(2,1)} %broadcast_in_dim.17), calls=%async_computation.5 | async-start | bytes 2097152 | tf_op jit(solution)/shard_map/all_to_all | solution.py:287
  158.0 4.9 %collective-permute-start.7 = (bf16[128,4096]{1,0:T(8,128)(2,1)S(1)}, bf16[128,4096]{1,0:T(8,128)(2,1)S(1)}, u32[]{:S(2)}, u32[]{:S(2)}) collective-permute-start(bf16[128,4096]{1,0:T(8,128)(2,1)S(1)} %copy-done.4), channel_id=1, source_target_pairs={{0,1},{1,0},{2,3},{3,2},{4,5},{5,4},{6,7},{7,6},{8,9},{9,8},{10,11... | collective-permute-start | bytes 3145736 | tf_op jit(solution)/shard_map/ppermute | solution.py:263
  158.0 4.9 %collective-permute-start.6 = (bf16[128,4096]{1,0:T(8,128)(2,1)S(1)}, bf16[128,4096]{1,0:T(8,128)(2,1)S(1)}, u32[]{:S(2)}, u32[]{:S(2)}) collective-permute-start(bf16[128,4096]{1,0:T(8,128)(2,1)S(1)} %copy-done.11), channel_id=1, source_target_pairs={{0,1},{1,0},{2,3},{3,2},{4,5},{5,4},{6,7},{7,6},{8,9},{9,8},{10,11... | collective-permute-start | bytes 3145736 | tf_op jit(solution)/shard_map/ppermute | solution.py:263
  158.6 3.7 %collective-permute-start.9 = (f32[128,16]{1,0:T(8,128)S(1)}, f32[128,16]{1,0:T(8,128)S(1)}, u32[]{:S(2)}, u32[]{:S(2)}) collective-permute-start(f32[128,16]{1,0:T(8,128)S(1)} %broadcast_select_fusion.3), channel_id=1, source_target_pairs={{0,1},{1,0},{2,3},{3,2},{4,5},{5,4},{6,7},{7,6},{8,9},{9,8},{10,11... | collective-permute-start | bytes 24584 | tf_op jit(solution)/shard_map/ppermute | solution.py:263

commit v6 on v5

--- a/solution.py
+++ b/solution.py
@@ -280,7 +280,7 @@
 def summed(parts, devices, others):
     far = 12 if devices == 16 else 0
     members = devices // 2 if far else devices
-    groups = [[member ^ f for member in ((3, 5, 0, 4, 1, 6, 7, 2) if far else range(members))] for f in ((0, far) if far else (0,))]
+    groups = [[member ^ f for member in ((0, 4, 6, 2, 3, 7, 5, 1) if far else range(members))] for f in ((0, far) if far else (0,))]
     shape = (members, devices // members * parts.shape[1]) + parts.shape[2:]
 
     def exchanged(value):

time: 174 us -> 169 us (0.971)
  waiting for transfers between devices: 52.7 us -> 49.6 us
    all_to_all x2, waiting for transfers between devices: 11.9 us -> 8.31 us  [exchanged(): lax.all_to_all(value, 'blk', split_axis=0, concat_axis=0, axis_index_grou...]
  transfers between devices with their start and end apart: 18 -> 18, of which waited for: 13 -> 13; matrix products, arithmetic and copies ran while one was open for 10% -> 10% of each run, Pallas kernels for 27% -> 28%
where the time goes in v6:
time: 169 us; the launch traced here: 168 us
  Pallas kernels  49.7 us (29%)
  waiting for transfers between devices  49.6 us (29%)
  starting transfers between devices  42.8 us (25%)
  other arithmetic  13.2 us (8%)
  local copies, waits for them, and re-layouts  9.36 us (6%)
  matrix products  2.89 us (2%)
    all_to_all x4, starting transfers between devices, exchange(): lax.all_to_all(chunks, 'blk', split_axis=0, concat_axis=0, axis_index_gro...  30.2 us
    all_to_all x4, waiting for transfers between devices, exchange(): lax.all_to_all(chunks, 'blk', split_axis=0, concat_axis=0, axis_index_gro...  28.4 us
    pallas_call x2, Pallas kernels, expand(): call(functools.partial(expand_kernel, section), 'expand', [sds(pair_shape...  10.1 us
    pallas_call x1, Pallas kernels, body(): call(turn_kernel, 'turn', [sds((tokens, count), F32), sds(act_shape, BF),...  8.96 us
    ppermute x11, waiting for transfers between devices, swap(): return lax.ppermute(value, 'pipe', [(0, 1), (1, 0)])  8.45 us
    all_to_all x2, waiting for transfers between devices, exchanged(): lax.all_to_all(value, 'blk', split_axis=0, concat_axis=0, axis_index_grou...  8.31 us
    pallas_call x1, Pallas kernels, body(): call(middle_kernel, 'middle', [sds(act_shape, BF), sds(act_shape, F32), s...  8.04 us
    all_to_all x2, starting transfers between devices, exchanged(): lax.all_to_all(value, 'blk', split_axis=0, concat_axis=0, axis_index_grou...  7.9 us
  transfers between devices with their start and end apart: 18, of which 13 were waited for; matrix products, arithmetic and copies ran while one was open for 10% of the time, Pallas kernels for 28%

profile of v6, /device:TPU:0, one launch (start us, length us, event | category | flops | bytes accessed | tf_op | source)
XLA Modules:
  0.0 168.4 jit_solution(2278961150257190463)
XLA Ops:
  0.6 0.0 copy-start
  0.6 0.0 copy-start.1
  0.7 2.3 %dynamic-slice_bitcast_fusion.2 = bf16[128,4096]{1,0:T(8,128)(2,1)} fusion(bf16[1,2,128,4096]{3,2,1,0:T(8,128)(2,1)} %param.10, s32[]{:T(128)S(6)} %select_n.97), kind=kLoop, calls=%fused_computation.15 | loop fusion | bytes 2097156 | tf_op jit(solution)/shard_map/jit(dynamic_index_in_dim)/squeeze | solution.py:308
  3.0 0.5 collective-permute-start
  3.4 0.2 left.1
  3.6 0.1 collective-permute-start.1
  3.7 1.3 dynamic-slice_bitcast_fusion
  5.0 1.3 dynamic-slice_bitcast_fusion.1
  6.3 1.0 copy-done.7
  7.3 0.5 multiply_convert_fusion
  7.8 1.4 convolution_convert_fusion
  9.2 9.1 %all-to-all-start.1 = ((bf16[16,8,4096]{2,1,0:T(8,128)(2,1)}), bf16[16,8,4096]{2,1,0:T(8,128)(2,1)}, u32[]{:S(2)}, u32[]{:S(2)}) async-start(bf16[16,8,4096]{2,1,0:T(8,128)(2,1)} %bitcast.48), calls=%async_computation.1 | async-start | bytes 2097152 | tf_op jit(solution)/shard_map/all_to_all | solution.py:276
  18.3 0.1 collective-permute-start.2
  18.4 0.5 collective-permute-start.3
  18.9 0.1 collective-permute-start.4
  19.0 2.7 %broadcast_select_fusion.1 = (bf16[128,4096]{1,0:T(8,128)(2,1)}, bf16[128,4096]{1,0:T(8,128)(2,1)}) fusion(bf16[128,4096]{1,0:T(8,128)(2,1)S(1)} %dynamic-slice_bitcast_fusion, bf16[128,4096]{1,0:T(8,128)(2,1)} %copy-done.7, pred[]{:T(512)S(6)} %eq.2), kind=kLoop, calls=%fused_computation.17 | loop fusion | flops 1048576 | bytes 4194305 | tf_op jit(solution)/shard_map/jit(_where)/select_n | solution.py:348
  21.7 0.2 collective-permute-done.3.first_other
  21.8 1.0 copy-done.6
  22.8 0.2 collective-permute-done.4.second_other
  23.1 5.1 %expand.2 = (bf16[32,128,128]{2,1,0:T(8,128)(2,1)}, bf16[32,128,128]{2,1,0:T(8,128)(2,1)}, bf16[32,128,128]{2,1,0:T(8,128)(2,1)}, bf16[32,128,128]{2,1,0:T(8,128)(2,1)}) custom-call(s32[1]{0:T(128)} %bitcast.p, bf16[64,64,64]{2,1,0:T(8,128)(2,1)} %bitcast.42, bf16[64,64,64]{2,1,0:T(8,128)(2,1)} %copy-done.6, bf16[64,64,64]{2,1,0:T(8,128)(2,1)} %bitcast.46, ...), custom_call_target="tpu_custom_call" | custom-call | flops 268435456 | bytes 8388608 | tf_op jit(solution)/shard_map/expand/pallas_call | solution.py:351
  28.1 0.6 copy-done.16
  28.7 7.2 %forward.1 = (bf16[128,4096]{1,0:T(8,128)(2,1)}, bf16[4096,128]{1,0:T(8,128)(2,1)}, bf16[128,4096]{1,0:T(8,128)(2,1)}, bf16[128,128]{1,0:T(8,128)(2,1)}, bf16[12...) custom-call(s32[1]{0:T(128)} %bitcast.p, bf16[128,4096]{1,0:T(8,128)(2,1)} %get-tuple-element.94.act, ...), custom_call_target="tpu_custom_call" | custom-call | flops 268435456 | bytes 8388608 | tf_op jit(solution)/shard_map/forward/pallas_call | solution.py:362
  36.0 5.6 %all-to-all-done.1 = bf16[16,8,4096]{2,1,0:T(8,128)(2,1)} async-done(((bf16[16,8,4096]{2,1,0:T(8,128)(2,1)}), bf16[16,8,4096]{2,1,0:T(8,128)(2,1)}, u32[]{:S(2)}, u32[]{:S(2)}) %all-to-all-start.1) | async-done | bytes 1048608 | tf_op jit(solution)/shard_map/all_to_all | solution.py:276
  41.6 6.7 %all-to-all-start = ((bf16[16,8,4096]{2,1,0:T(8,128)(2,1)}), bf16[16,8,4096]{2,1,0:T(8,128)(2,1)S(1)}, u32[]{:S(2)}, u32[]{:S(2)}) async-start(bf16[16,8,4096]{2,1,0:T(8,128)(2,1)} %bitcast.54), calls=%async_computation | async-start | bytes 2097152 | tf_op jit(solution)/shard_map/all_to_all | solution.py:276
  48.3 5.0 %expand.3 = (bf16[32,128,128]{2,1,0:T(8,128)(2,1)}, bf16[32,128,128]{2,1,0:T(8,128)(2,1)}, bf16[32,128,128]{2,1,0:T(8,128)(2,1)}, bf16[32,128,128]{2,1,0:T(8,128)(2,1)}) custom-call(s32[1]{0:T(128)} %bitcast.p, bf16[64,64,64]{2,1,0:T(8,128)(2,1)} %bitcast.43, bf16[64,64,64]{2,1,0:T(8,128)(2,1)} %copy-done.6, bf16[64,64,64]{2,1,0:T(8,128)(2,1)} %bitcast.47, ...), custom_call_target="tpu_custom_call" | custom-call | flops 268435456 | bytes 8388608 | tf_op jit(solution)/shard_map/expand/pallas_call | solution.py:351
  53.3 8.0 %middle.1 = (bf16[128,4096]{1,0:T(8,128)(2,1)}, f32[128,4096]{1,0:T(8,128)}, f32[128,128]{1,0:T(8,128)}, bf16[16,2,128,128]{3,2,1,0:T(8,128)(2,1)}) custom-call(bf16[128,4096]{1,0:T(8,128)(2,1)} %bitcast.12.back, bf16[32,128,128]{2,1,0:T(8,128)(2,1)} %get-tuple-element.60.second_bt, bf16[32,128,128]{2,1,0:T(8,128)(2,1)} %get-tuple-element.61.first_bt, ...), custom_call_target="tpu_custom_call" | custom-call | flops 268435456 | bytes 8388608 | tf_op jit(solution)/shard_map/middle/pallas_call | solution.py:385
  61.3 8.8 %all-to-all-done = bf16[16,8,4096]{2,1,0:T(8,128)(2,1)S(1)} async-done(((bf16[16,8,4096]{2,1,0:T(8,128)(2,1)}), bf16[16,8,4096]{2,1,0:T(8,128)(2,1)S(1)}, u32[]{:S(2)}, u32[]{:S(2)}) %all-to-all-start) | async-done | bytes 1048608 | tf_op jit(solution)/shard_map/all_to_all | solution.py:276
  70.1 7.3 %all-to-all-start.3 = ((bf16[16,8,4096]{2,1,0:T(8,128)(2,1)}), bf16[16,8,4096]{2,1,0:T(8,128)(2,1)}, u32[]{:S(2)}, u32[]{:S(2)}) async-start(bf16[16,8,4096]{2,1,0:T(8,128)(2,1)} %bitcast.52), calls=%async_computation.3 | async-start | bytes 2097152 | tf_op jit(solution)/shard_map/all_to_all | solution.py:276
  77.4 0.1 collective-permute-start.5
  77.5 0.6 broadcast_select_fusion.6.left_t_low
  78.1 0.6 collective-permute-done.5
  78.7 0.4 fusion.5
  79.1 0.6 copy-done.10
  79.7 3.2 %fusion.2 = (bf16[128,4096]{1,0:T(8,128)(2,1)S(1)}, bf16[128,4096]{1,0:T(8,128)(2,1)}) fusion(bf16[128,4096]{1,0:T(8,128)(2,1)S(1)} %copy-done.3, bf16[2,128,4096]{2,1,0:T(8,128)(2,1)S(1)} %copy-done.10, s32[]{:T(128)S(6)} %select_n.104, f32[128,4096]{1,0:T(8,128)} %get-tuple-element.66, f32[128,4096]{1,0:T(8,128)S(1)} %fusion.5), kind=kLoop, calls=%fused_computation.5 | loop fusion | flops 3670016 | bytes 8388612 | tf_op jit(solution)/shard_map/convert_element_type | solution.py:399
  82.9 1.1 fusion.3.left_term
  84.0 9.0 %turn.1 = (f32[128,16]{1,0:T(8,128)}, bf16[128,4096]{1,0:T(8,128)(2,1)}, bf16[128,4096]{1,0:T(8,128)(2,1)}, bf16[4096,128]{1,0:T(8,128)(2,1)}, bf16[128,4096]{1,0:T(8,128)(2,1)}) custom-call(bf16[128,4096]{1,0:T(8,128)(2,1)} %get-tuple-element.92.incoming.upstream, bf16[128,4096]{1,0:T(8,128)(2,1)} %get-tuple-element.93.act_low.act, ...), custom_call_target="tpu_custom_call" | custom-call | flops 268435456 | bytes 8388608 | tf_op jit(solution)/shard_map/turn/pallas_call | solution.py:402
  92.9 5.7 %all-to-all-done.3 = bf16[16,8,4096]{2,1,0:T(8,128)(2,1)} async-done(((bf16[16,8,4096]{2,1,0:T(8,128)(2,1)}), bf16[16,8,4096]{2,1,0:T(8,128)(2,1)}, u32[]{:S(2)}, u32[]{:S(2)}) %all-to-all-start.3) | async-done | bytes 1048608 | tf_op jit(solution)/shard_map/all_to_all | solution.py:276
  98.6 7.1 %all-to-all-start.2 = ((bf16[16,8,4096]{2,1,0:T(8,128)(2,1)}), bf16[16,8,4096]{2,1,0:T(8,128)(2,1)}, u32[]{:S(2)}, u32[]{:S(2)}) async-start(bf16[16,8,4096]{2,1,0:T(8,128)(2,1)} %bitcast.53), calls=%async_computation.2 | async-start | bytes 2097152 | tf_op jit(solution)/shard_map/all_to_all | solution.py:276
  105.8 0.6 broadcast_select_fusion.5.left
  106.4 7.7 %lower.1 = (f32[128,4096]{1,0:T(8,128)}, f32[128,16]{1,0:T(8,128)}, bf16[16,2,128,128]{3,2,1,0:T(8,128)(2,1)}) custom-call(bf16[128,4096]{1,0:T(8,128)(2,1)} %bitcast.17.rows, bf16[32,128,128]{2,1,0:T(8,128)(2,1)} %get-tuple-element.74.first_bd, bf16[32,128,128]{2,1,0:T(8,128)(2,1)} %get-tuple-element.75.second_bd, ...), custom_call_target="tpu_custom_call" | custom-call | flops 268435456 | bytes 8388608 | tf_op jit(solution)/shard_map/lower/pallas_call | solution.py:440
  114.1 0.1 broadcast_select_fusion
  114.2 0.1 collective-permute-start.10
  114.3 2.6 %collective-permute-done.10 = bf16[16,2,128,128]{3,2,1,0:T(8,128)(2,1)S(1)} collective-permute-done((bf16[16,2,128,128]{3,2,1,0:T(8,128)(2,1)S(1)}, bf16[16,2,128,128]{3,2,1,0:T(8,128)(2,1)S(1)}, u32[]{:S(2)}, u32[]{:S(2)}) %collective-permute-start.10) | collective-permute-done | bytes 1048608 | tf_op jit(solution)/shard_map/ppermute | solution.py:263
  117.0 1.5 add_convert_fusion
  118.5 8.3 %all-to-all-done.2 = bf16[16,8,4096]{2,1,0:T(8,128)(2,1)} async-done(((bf16[16,8,4096]{2,1,0:T(8,128)(2,1)}), bf16[16,8,4096]{2,1,0:T(8,128)(2,1)}, u32[]{:S(2)}, u32[]{:S(2)}) %all-to-all-start.2) | async-done | bytes 1048608 | tf_op jit(solution)/shard_map/all_to_all | solution.py:276
  126.7 4.3 %all-to-all-start.4 = ((bf16[8,4,128,128]{3,2,1,0:T(8,128)(2,1)}), bf16[8,4,128,128]{3,2,1,0:T(8,128)(2,1)S(1)}, u32[]{:S(2)}, u32[]{:S(2)}) async-start(bf16[8,4,128,128]{3,2,1,0:T(8,128)(2,1)} %bitcast.24), calls=%async_computation.4 | async-start | bytes 2097152 | tf_op jit(solution)/shard_map/all_to_all | solution.py:287
  131.1 5.0 %last.1 = (bf16[128,4096]{1,0:T(8,128)(2,1)}, f32[128,128]{1,0:T(8,128)}) custom-call(bf16[128,4096]{1,0:T(8,128)(2,1)} %bitcast.15.received, bf16[128,128]{1,0:T(8,128)(2,1)} %get-tuple-element.71.right_t, bf16[128,128]{1,0:T(8,128)(2,1)} %constant.36.clone.order, bf16[128,4096]{1,0:T(8,128)(2,1)} %get-tuple-element.92.incoming.upstream, ...), custom_call_target="tpu_custom_call" | custom-call | flops 268435456 | bytes 8388608 | tf_op jit(solution)/shard_map/last/pallas_call | solution.py:453
  136.1 0.1 collective-permute-start.8
  136.2 1.2 collective-permute-done.8
  137.4 1.5 select_add_fusion.1
  138.9 4.8 %all-to-all-done.4 = bf16[8,4,128,128]{3,2,1,0:T(8,128)(2,1)S(1)} async-done(((bf16[8,4,128,128]{3,2,1,0:T(8,128)(2,1)}), bf16[8,4,128,128]{3,2,1,0:T(8,128)(2,1)S(1)}, u32[]{:S(2)}, u32[]{:S(2)}) %all-to-all-start.4) | async-done | bytes 1048608 | tf_op jit(solution)/shard_map/all_to_all | solution.py:287
  143.7 0.1 reduce_sum.12
  143.9 2.5 %collective-permute-start.11 = (bf16[4,128,128]{2,1,0:T(8,128)(2,1)S(1)}, bf16[4,128,128]{2,1,0:T(8,128)(2,1)S(1)}, u32[]{:S(2)}, u32[]{:S(2)}) collective-permute-start(bf16[4,128,128]{2,1,0:T(8,128)(2,1)S(1)} %reduce_sum.12), channel_id=1, source_target_pairs={{0,24},{2,26},{4,28},{6,30},{8,16},{10,18},{12,20},{14,22},{16,8},... | collective-permute-start | bytes 393224 | tf_op jit(solution)/shard_map/ppermute | solution.py:292
  146.4 4.4 %collective-permute-done.11 = bf16[4,128,128]{2,1,0:T(8,128)(2,1)S(1)} collective-permute-done((bf16[4,128,128]{2,1,0:T(8,128)(2,1)S(1)}, bf16[4,128,128]{2,1,0:T(8,128)(2,1)S(1)}, u32[]{:S(2)}, u32[]{:S(2)}) %collective-permute-start.11) | collective-permute-done | bytes 131104 | tf_op jit(solution)/shard_map/ppermute | solution.py:292
  150.9 1.2 broadcast_in_dim.17
  152.1 3.6 %all-to-all-start.5 = ((bf16[8,4,128,128]{3,2,1,0:T(8,128)(2,1)}), bf16[8,4,128,128]{3,2,1,0:T(8,128)(2,1)S(1)}, u32[]{:S(2)}, u32[]{:S(2)}) async-start(bf16[8,4,128,128]{3,2,1,0:T(8,128)(2,1)} %broadcast_in_dim.17), calls=%async_computation.5 | async-start | bytes 2097152 | tf_op jit(solution)/shard_map/all_to_all | solution.py:287
  155.7 0.1 collective-permute-start.7
  155.8 0.5 collective-permute-start.6
  156.3 0.2 collective-permute-start.9
  156.4 3.6 %collective-permute-done.9 = f32[128,16]{1,0:T(8,128)S(1)} collective-permute-done((f32[128,16]{1,0:T(8,128)S(1)}, f32[128,16]{1,0:T(8,128)S(1)}, u32[]{:S(2)}, u32[]{:S(2)}) %collective-permute-start.9) | collective-permute-done | bytes 8224 | tf_op jit(solution)/shard_map/ppermute | solution.py:263
  160.0 0.6 select_add_fusion
  160.6 1.7 maximum_select_fusion
  162.3 3.5 %all-to-all-done.5 = bf16[8,4,128,128]{3,2,1,0:T(8,128)(2,1)S(1)} async-done(((bf16[8,4,128,128]{3,2,1,0:T(8,128)(2,1)}), bf16[8,4,128,128]{3,2,1,0:T(8,128)(2,1)S(1)}, u32[]{:S(2)}, u32[]{:S(2)}) %all-to-all-start.5) | async-done | bytes 1048608 | tf_op jit(solution)/shard_map/all_to_all | solution.py:287
  165.9 2.5 %unpack.1 = (f32[64,64,64]{2,1,0:T(8,128)}, f32[64,64,64]{2,1,0:T(8,128)}) custom-call(bf16[16,2,128,128]{3,2,1,0:T(8,128)(2,1)S(1)} %bitcast.39), custom_call_target="tpu_custom_call" | custom-call | flops 268435456 | bytes 8388608 | tf_op jit(solution)/shard_map/unpack/pallas_call | solution.py:473
  (36 shorter events, 0.1 us)
Async XLA Ops:
  0.6 2.8 %copy-start = (bf16[128,16]{1,0:T(8,128)(2,1)S(1)}, bf16[128,16]{1,0:T(8,128)(2,1)}, u32[]{:S(2)}) copy-start(bf16[128,16]{1,0:T(8,128)(2,1)} %constant.35.clone.onehot) | copy-start | bytes 12292
  0.6 2.8 %copy-start.1 = (bf16[128,128]{1,0:T(8,128)(2,1)S(1)}, bf16[128,128]{1,0:T(8,128)(2,1)}, u32[]{:S(2)}) copy-start(bf16[128,128]{1,0:T(8,128)(2,1)} %constant.34.clone.mask) | copy-start | bytes 98308
  0.7 2.8 %copy-start.2 = (bf16[1,8,16,16]{3,2,1,0:T(8,128)(2,1)S(1)}, bf16[1,8,16,16]{3,2,1,0:T(8,128)(2,1)}, u32[]{:S(2)}) copy-start(bf16[1,8,16,16]{3,2,1,0:T(8,128)(2,1)} %param.13) | copy-start | bytes 12292
  3.0 3.4 %collective-permute-start = (bf16[128,4096]{1,0:T(8,128)(2,1)}, bf16[128,4096]{1,0:T(8,128)(2,1)S(1)}, u32[]{:S(2)}, u32[]{:S(2)}) collective-permute-start(bf16[128,4096]{1,0:T(8,128)(2,1)} %dynamic-slice_bitcast_fusion.2), channel_id=1, source_target_pairs={{0,1},{1,0},{2,3},{3,2},{4,5},{5,4},{6,7},{7,6},{8,9},{9,8},{10,11... | collective-permute-start | bytes 3145736 | tf_op jit(solution)/shard_map/ppermute | solution.py:263
  3.6 4.2 %collective-permute-start.1 = (bf16[128,128]{1,0:T(8,128)(2,1)S(1)}, bf16[128,128]{1,0:T(8,128)(2,1)S(1)}, u32[]{:S(2)}, u32[]{:S(2)}) collective-permute-start(bf16[128,128]{1,0:T(8,128)(2,1)S(1)} %get-tuple-element.50), channel_id=1, source_target_pairs={{0,1},{1,0},{2,3},{3,2},{4,5},{5,4},{6,7},{7,6},{8,9},{9,8},{10,11... | collective-permute-start | bytes 98312 | tf_op jit(solution)/shard_map/ppermute | solution.py:263
  6.3 1.0 copy-start.7
  7.8 10.6 %copy-start.15 = (bf16[1,1,128,128]{3,2,1,0:T(8,128)(2,1)S(1)}, bf16[1,1,128,128]{3,2,1,0:T(8,128)(2,1)}, u32[]{:S(2)}) copy-start(bf16[1,1,128,128]{3,2,1,0:T(8,128)(2,1)} %param.12) | copy-start | bytes 98308
  7.8 10.6 %copy-start.5 = (bf16[1,64,64,64]{3,2,1,0:T(8,128)(2,1)S(1)}, bf16[1,64,64,64]{3,2,1,0:T(8,128)(2,1)}, u32[]{:S(2)}) copy-start(bf16[1,64,64,64]{3,2,1,0:T(8,128)(2,1)} %param.14) | copy-start | bytes 1572868
  9.2 32.4 %all-to-all-start.1 = ((bf16[16,8,4096]{2,1,0:T(8,128)(2,1)}), bf16[16,8,4096]{2,1,0:T(8,128)(2,1)}, u32[]{:S(2)}, u32[]{:S(2)}) async-start(bf16[16,8,4096]{2,1,0:T(8,128)(2,1)} %bitcast.48), calls=%async_computation.1 | async-start | bytes 2097152 | tf_op jit(solution)/shard_map/all_to_all | solution.py:276
  18.3 9.8 %collective-permute-start.2 = (bf16[128,128]{1,0:T(8,128)(2,1)S(1)}, bf16[128,128]{1,0:T(8,128)(2,1)S(1)}, u32[]{:S(2)}, u32[]{:S(2)}) collective-permute-start(bf16[128,128]{1,0:T(8,128)(2,1)S(1)} %bitcast.58), channel_id=1, source_target_pairs={{0,1},{1,0},{2,3},{3,2},{4,5},{5,4},{6,7},{7,6},{8,9},{9,8},{10,11... | collective-permute-start | bytes 98312 | tf_op jit(solution)/shard_map/ppermute | solution.py:263
  18.4 3.4 %collective-permute-start.3 = (bf16[64,64,64]{2,1,0:T(8,128)(2,1)S(1)}, bf16[64,64,64]{2,1,0:T(8,128)(2,1)S(1)}, u32[]{:S(2)}, u32[]{:S(2)}) collective-permute-start(bf16[64,64,64]{2,1,0:T(8,128)(2,1)S(1)} %bitcast.44), channel_id=1, source_target_pairs={{0,1},{1,0},{2,3},{3,2},{4,5},{5,4},{6,7},{7,6},{8,9},{9,8},{10,11... | collective-permute-start | bytes 1572872 | tf_op jit(solution)/shard_map/ppermute | solution.py:263
  18.9 4.1 %collective-permute-start.4 = (bf16[64,64,64]{2,1,0:T(8,128)(2,1)}, bf16[64,64,64]{2,1,0:T(8,128)(2,1)}, u32[]{:S(2)}, u32[]{:S(2)}) collective-permute-start(bf16[64,64,64]{2,1,0:T(8,128)(2,1)} %bitcast.45), channel_id=1, source_target_pairs={{0,1},{1,0},{2,3},{3,2},{4,5},{5,4},{6,7},{7,6},{8,9},{9,8},{10,11... | collective-permute-start | bytes 1572872 | tf_op jit(solution)/shard_map/ppermute | solution.py:263
  21.8 1.0 copy-start.6
  28.1 0.6 copy-start.16
  41.6 28.5 %all-to-all-start = ((bf16[16,8,4096]{2,1,0:T(8,128)(2,1)}), bf16[16,8,4096]{2,1,0:T(8,128)(2,1)S(1)}, u32[]{:S(2)}, u32[]{:S(2)}) async-start(bf16[16,8,4096]{2,1,0:T(8,128)(2,1)} %bitcast.54), calls=%async_computation | async-start | bytes 2097152 | tf_op jit(solution)/shard_map/all_to_all | solution.py:276
  70.1 28.5 %all-to-all-start.3 = ((bf16[16,8,4096]{2,1,0:T(8,128)(2,1)}), bf16[16,8,4096]{2,1,0:T(8,128)(2,1)}, u32[]{:S(2)}, u32[]{:S(2)}) async-start(bf16[16,8,4096]{2,1,0:T(8,128)(2,1)} %bitcast.52), calls=%async_computation.3 | async-start | bytes 2097152 | tf_op jit(solution)/shard_map/all_to_all | solution.py:276
  77.4 1.7 %copy-start.3 = (bf16[128,4096]{1,0:T(8,128)(2,1)S(1)}, bf16[128,4096]{1,0:T(8,128)(2,1)}, u32[]{:S(2)}) copy-start(bf16[128,4096]{1,0:T(8,128)(2,1)} %get-tuple-element.94.act) | copy-start | bytes 3145732
  77.4 1.3 collective-permute-start.5
  78.1 1.7 copy-start.10
  98.6 28.1 %all-to-all-start.2 = ((bf16[16,8,4096]{2,1,0:T(8,128)(2,1)}), bf16[16,8,4096]{2,1,0:T(8,128)(2,1)}, u32[]{:S(2)}, u32[]{:S(2)}) async-start(bf16[16,8,4096]{2,1,0:T(8,128)(2,1)} %bitcast.53), calls=%async_computation.2 | async-start | bytes 2097152 | tf_op jit(solution)/shard_map/all_to_all | solution.py:276
  106.4 7.7 %copy-start.8 = (bf16[16,2,128,128]{3,2,1,0:T(8,128)(2,1)S(1)}, bf16[16,2,128,128]{3,2,1,0:T(8,128)(2,1)}, u32[]{:S(2)}) copy-start(bf16[16,2,128,128]{3,2,1,0:T(8,128)(2,1)} %get-tuple-element.86) | copy-start | bytes 3145732
  114.1 2.9 %copy-start.9 = (bf16[16,2,128,128]{3,2,1,0:T(8,128)(2,1)S(1)}, bf16[16,2,128,128]{3,2,1,0:T(8,128)(2,1)}, u32[]{:S(2)}) copy-start(bf16[16,2,128,128]{3,2,1,0:T(8,128)(2,1)} %get-tuple-element.85) | copy-start | bytes 3145732
  114.2 2.7 %collective-permute-start.10 = (bf16[16,2,128,128]{3,2,1,0:T(8,128)(2,1)S(1)}, bf16[16,2,128,128]{3,2,1,0:T(8,128)(2,1)S(1)}, u32[]{:S(2)}, u32[]{:S(2)}) collective-permute-start(bf16[16,2,128,128]{3,2,1,0:T(8,128)(2,1)S(1)} %broadcast_select_fusion), channel_id=1, source_target_pairs={{0,1},{1,0},{2,3},{3,2},{4,5},{5,4},{6,7},{7,6},{8,9},{9,8},{10,11... | collective-permute-start | bytes 3145736 | tf_op jit(solution)/shard_map/ppermute | solution.py:263
  126.7 17.0 %all-to-all-start.4 = ((bf16[8,4,128,128]{3,2,1,0:T(8,128)(2,1)}), bf16[8,4,128,128]{3,2,1,0:T(8,128)(2,1)S(1)}, u32[]{:S(2)}, u32[]{:S(2)}) async-start(bf16[8,4,128,128]{3,2,1,0:T(8,128)(2,1)} %bitcast.24), calls=%async_computation.4 | async-start | bytes 2097152 | tf_op jit(solution)/shard_map/all_to_all | solution.py:287
  131.1 5.0 %copy-start.12 = (f32[128,128]{1,0:T(8,128)S(1)}, f32[128,128]{1,0:T(8,128)}, u32[]{:S(2)}) copy-start(f32[128,128]{1,0:T(8,128)} %get-tuple-element.82) | copy-start | bytes 196612
  136.1 1.3 collective-permute-start.8
  143.9 11.8 %copy-start.4 = (bf16[128,4096]{1,0:T(8,128)(2,1)S(1)}, bf16[128,4096]{1,0:T(8,128)(2,1)}, u32[]{:S(2)}) copy-start(bf16[128,4096]{1,0:T(8,128)(2,1)} %get-tuple-element.92.incoming.upstream) | copy-start | bytes 3145732
  143.9 11.9 %copy-start.11 = (bf16[128,4096]{1,0:T(8,128)(2,1)S(1)}, bf16[128,4096]{1,0:T(8,128)(2,1)}, u32[]{:S(2)}) copy-start(bf16[128,4096]{1,0:T(8,128)(2,1)} %get-tuple-element.80) | copy-start | bytes 3145732
  143.9 12.4 %copy-start.13 = (f32[128,16]{1,0:T(8,128)S(1)}, f32[128,16]{1,0:T(8,128)}, u32[]{:S(2)}) copy-start(f32[128,16]{1,0:T(8,128)} %get-tuple-element.84) | copy-start | bytes 24580
  143.9 12.4 %copy-start.14 = (f32[128,16]{1,0:T(8,128)S(1)}, f32[128,16]{1,0:T(8,128)}, u32[]{:S(2)}) copy-start(f32[128,16]{1,0:T(8,128)} %get-tuple-element.83) | copy-start | bytes 24580
  143.9 6.9 %collective-permute-start.11 = (bf16[4,128,128]{2,1,0:T(8,128)(2,1)S(1)}, bf16[4,128,128]{2,1,0:T(8,128)(2,1)S(1)}, u32[]{:S(2)}, u32[]{:S(2)}) collective-permute-start(bf16[4,128,128]{2,1,0:T(8,128)(2,1)S(1)} %reduce_sum.12), channel_id=1, source_target_pairs={{0,24},{2,26},{4,28},{6,30},{8,16},{10,18},{12,20},{14,22},{16,8},... | collective-permute-start | bytes 393224 | tf_op jit(solution)/shard_map/ppermute | solution.py:292
  152.1 13.8 %all-to-all-start.5 = ((bf16[8,4,128,128]{3,2,1,0:T(8,128)(2,1)}), bf16[8,4,128,128]{3,2,1,0:T(8,128)(2,1)S(1)}, u32[]{:S(2)}, u32[]{:S(2)}) async-start(bf16[8,4,128,128]{3,2,1,0:T(8,128)(2,1)} %broadcast_in_dim.17), calls=%async_computation.5 | async-start | bytes 2097152 | tf_op jit(solution)/shard_map/all_to_all | solution.py:287
  155.7 5.0 %collective-permute-start.7 = (bf16[128,4096]{1,0:T(8,128)(2,1)S(1)}, bf16[128,4096]{1,0:T(8,128)(2,1)S(1)}, u32[]{:S(2)}, u32[]{:S(2)}) collective-permute-start(bf16[128,4096]{1,0:T(8,128)(2,1)S(1)} %copy-done.4), channel_id=1, source_target_pairs={{0,1},{1,0},{2,3},{3,2},{4,5},{5,4},{6,7},{7,6},{8,9},{9,8},{10,11... | collective-permute-start | bytes 3145736 | tf_op jit(solution)/shard_map/ppermute | solution.py:263
  155.8 4.9 %collective-permute-start.6 = (bf16[128,4096]{1,0:T(8,128)(2,1)S(1)}, bf16[128,4096]{1,0:T(8,128)(2,1)S(1)}, u32[]{:S(2)}, u32[]{:S(2)}) collective-permute-start(bf16[128,4096]{1,0:T(8,128)(2,1)S(1)} %copy-done.11), channel_id=1, source_target_pairs={{0,1},{1,0},{2,3},{3,2},{4,5},{5,4},{6,7},{7,6},{8,9},{9,8},{10,11... | collective-permute-start | bytes 3145736 | tf_op jit(solution)/shard_map/ppermute | solution.py:263
  156.3 3.7 %collective-permute-start.9 = (f32[128,16]{1,0:T(8,128)S(1)}, f32[128,16]{1,0:T(8,128)S(1)}, u32[]{:S(2)}, u32[]{:S(2)}) collective-permute-start(f32[128,16]{1,0:T(8,128)S(1)} %broadcast_select_fusion.3), channel_id=1, source_target_pairs={{0,1},{1,0},{2,3},{3,2},{4,5},{5,4},{6,7},{7,6},{8,9},{9,8},{10,11... | collective-permute-start | bytes 24584 | tf_op jit(solution)/shard_map/ppermute | solution.py:263
